TPU v7x, 512 devices: a whole 4x4x16 slice. The times are simulated.
512 devices in a mesh: depth: 4 (over y), seq: 32 (over z, x_lo), rep: 4 (over x_hi, core).
Axes of the slice: x: 4 (x_hi: 2, x_lo: 2; x = x_hi * 2 + x_lo), y: 4, z: 16, core: 2. Of those that a mesh axis runs over, the one named last changes fastest.
Arguments:
- read_feats: bfloat16 [4, 2048, 128, 512], P('rep', 'seq', 'depth'), may hold values from -96 to 96
- base_codes: int32 [4, 2048, 128], P('rep', 'seq', 'depth'), may hold values from 0 to 7
- qual_codes: int32 [4, 2048, 128], P('rep', 'seq', 'depth'), may hold values from 0 to 93
- depth_counts: int32 [4, 2048], P('rep', 'seq'), may hold values from 4 to 128, as said below
- base_table: bfloat16 [8, 512], replicated, may hold values from -3 to 3
- qual_table: bfloat16 [94, 512], replicated, may hold values from -3 to 3
- value_weight: bfloat16 [1024, 512], replicated, may hold values from -0.25 to 0.25
- score_weight: bfloat16 [512, 8], replicated, may hold values from -1 to 1
- conv_weight: bfloat16 [1024, 5, 512], P('depth'), may hold values from -0.078125 to 0.078125
- cotangent: bfloat16 [4, 2048, 512], P('rep', 'seq'), may hold values from -0.15625 to 0.15625
Outputs:
- value_weight_grad: float32 [1024, 512], P(('depth', 'seq', 'rep'))
- score_weight_grad: float32 [512, 8], replicated
- conv_weight_grad: float32 [1024, 5, 512], P(('depth', 'seq'), None, 'rep')
Inputs may be any that keep to these rules, and one draw needn't show every extreme that they name: `depth_counts`: reads at or beyond the count are padding; some positions of every window hold 128 live reads.
All inputs are finite; a program needn't handle non-finite values.
Results may differ from a plain program's by a relative error of at most 0.035.
Values may be sent and summed in bfloat16 or wider, within the bound.
No kernel may reach another device: no remote copies, remote signals or barrier semaphores. Data moves between devices by JAX's collectives and lax.ppermute only.
A program may use at most 128 MiB of HBM per device.

v0:
```python
import jax
import jax.numpy as jnp
from jax import lax
from jax.sharding import PartitionSpec as P


def padded(block, sides, width):
    for axis, dim in sides:
        count = lax.axis_size(axis)
        forward = [(i, i + 1) for i in range(count - 1)]
        backward = [(target, source) for source, target in forward]
        low = lax.ppermute(
            lax.slice_in_dim(block, block.shape[dim] - width, None, axis=dim), axis, forward
        )
        high = lax.ppermute(lax.slice_in_dim(block, 0, width, axis=dim), axis, backward)
        block = jnp.concatenate([low, block, high], axis=dim)
    return block


def silu_slope(preact):
    sigma = jax.nn.sigmoid(preact)
    return sigma * (1.0 + preact * (1.0 - sigma))


def body(
    read_feats,
    base_codes,
    qual_codes,
    depth_counts,
    base_table,
    qual_table,
    value_weight,
    score_weight,
    conv_weight,
    cotangent,
):
    features = read_feats[0]
    base_local = base_codes[0]
    qual_local = qual_codes[0]
    depth_local = depth_counts[0]
    grad_local = cotangent[0]
    positions, read_count, channels = features.shape
    heads_count = score_weight.shape[1]
    hidden_units = value_weight.shape[0]
    head_width = hidden_units // heads_count
    block_units, kernel_size, out_channels = conv_weight.shape
    half_kernel = kernel_size // 2
    depth_index = lax.axis_index("depth")
    base_hot = (base_local[..., None] == jnp.arange(base_table.shape[0], dtype=jnp.int32)).astype(
        jnp.bfloat16
    )
    qual_hot = (qual_local[..., None] == jnp.arange(qual_table.shape[0], dtype=jnp.int32)).astype(
        jnp.bfloat16
    )
    base_part = jnp.einsum("prb,bc->prc", base_hot, base_table, preferred_element_type=jnp.float32)
    qual_part = jnp.einsum("prq,qc->prc", qual_hot, qual_table, preferred_element_type=jnp.float32)
    features_in = (features.astype(jnp.float32) + base_part + qual_part).astype(jnp.bfloat16)
    preact = jnp.einsum(
        "prc,jc->prj", features_in, value_weight, preferred_element_type=jnp.float32
    )
    values = jax.nn.silu(preact).astype(jnp.bfloat16)
    scores = jnp.einsum(
        "prc,ch->prh", features_in, score_weight, preferred_element_type=jnp.float32
    )
    read_index = depth_index * read_count + jnp.arange(read_count, dtype=jnp.int32)
    live = (read_index[None, :] < depth_local[:, None])[..., None]
    local_top = jnp.max(jnp.where(live, scores, -1e30), axis=1)
    weights = jnp.where(live, jnp.exp(scores - local_top[:, None, :]), 0.0)
    local_total = jnp.sum(weights, axis=1)
    value_heads = values.reshape(positions, read_count, heads_count, head_width)
    local_pool = jnp.sum(weights[..., None] * value_heads.astype(jnp.float32), axis=1)
    joint_top = lax.pmax(local_top, "depth")
    rescale = jnp.exp(local_top - joint_top)
    joint_total, joint_pool = lax.psum(
        (local_total * rescale, local_pool * rescale[..., None]), "depth"
    )
    pooled_exact = joint_pool / joint_total[..., None]
    read_probs = weights * (rescale / joint_total)[:, None, :]
    pooled_round = pooled_exact.reshape(positions, hidden_units).astype(jnp.bfloat16)
    grad_rim = padded(grad_local, (("seq", 0),), half_kernel)
    block_grad = jnp.zeros((positions, block_units), jnp.float32)
    for kernel_tap in range(kernel_size):
        offset = 2 * half_kernel - kernel_tap
        block_grad = block_grad + jnp.einsum(
            "qo,io->qi",
            grad_rim[offset : offset + positions],
            conv_weight[:, kernel_tap, :],
            preferred_element_type=jnp.float32,
        )
    pooled_grad = lax.all_gather(block_grad.astype(jnp.bfloat16), "depth", axis=1, tiled=True)
    grad_heads = pooled_grad.reshape(positions, heads_count, head_width)
    grad_heads_float = grad_heads.astype(jnp.float32)
    prob_grad = jnp.einsum(
        "prhe,phe->prh", value_heads, grad_heads, preferred_element_type=jnp.float32
    )
    row_total = jnp.sum(grad_heads_float * pooled_exact, axis=2)
    score_grad = (read_probs * (prob_grad - row_total[:, None, :])).astype(jnp.bfloat16)
    value_grad = (read_probs[..., None] * grad_heads_float[:, None]).reshape(
        positions, read_count, hidden_units
    ) * silu_slope(preact)
    value_grad = value_grad.astype(jnp.bfloat16)
    score_term = jnp.einsum(
        "prc,prh->ch", features_in, score_grad, preferred_element_type=jnp.float32
    )
    score_weight_grad = lax.psum(score_term, ("depth", "seq", "rep"))
    picked = value_grad
    value_weight_grad = lax.psum_scatter(
        jnp.einsum("prj,prc->jc", picked, features_in, preferred_element_type=jnp.float32),
        ("depth", "seq", "rep"),
        scatter_dimension=0,
        tiled=True,
    )
    my_pool = lax.dynamic_slice_in_dim(pooled_round, depth_index * block_units, block_units, 1)
    grad_all = lax.all_to_all(grad_rim[None], "rep", split_axis=2, concat_axis=0, tiled=True)
    pool_rim = padded(my_pool, (("seq", 0),), half_kernel)
    pool_all = lax.all_gather(pool_rim[None], "rep", axis=0, tiled=True)
    grad_middle = grad_all[:, half_kernel : half_kernel + positions]
    picked = pool_all
    tap_terms = []
    for kernel_tap in range(kernel_size):
        tap_terms.append(
            jnp.einsum(
                "wpi,wpo->io",
                picked[:, kernel_tap : kernel_tap + positions],
                grad_middle,
                preferred_element_type=jnp.float32,
            )
        )
    conv_weight_grad = lax.psum_scatter(
        jnp.stack(tap_terms, axis=1), "seq", scatter_dimension=0, tiled=True
    )
    return (value_weight_grad, score_weight_grad, conv_weight_grad)


def solution(mesh):
    placed = (
        P("rep", "seq", "depth", None),
        P("rep", "seq", "depth"),
        P("rep", "seq", "depth"),
        P("rep", "seq"),
        P(),
        P(),
        P(),
        P(),
        P("depth", None, None),
        P("rep", "seq", None),
    )
    return jax.shard_map(
        body,
        mesh=mesh,
        in_specs=placed,
        out_specs=(P(("depth", "seq", "rep"), None), P(), P(("depth", "seq"), None, "rep")),
        check_vma=False,
    )
```

profile of v0, /device:TPU:4, one launch (start us, length us, event | category | flops | bytes accessed | tf_op | source)
XLA Modules:
  0.0 754.8 jit_solution(11444340473233276324)
XLA Ops:
  7.2 0.0 copy-start
  7.2 0.0 all-reduce.4.cloned.1.call-start
  7.3 0.9 copy.39
  8.1 0.8 copy.40
  8.9 1.6 fusion.32
  10.6 0.1 broadcast_compare_fusion
  10.7 0.0 copy-start.9
  10.7 1.1 fusion.4
  11.8 2.2 select_reduce_fusion
  13.9 17.9 %pmax.7 = f32[64,8]{1,0:T(8,128)} all-reduce(f32[64,8]{1,0:T(8,128)S(1)} %get-tuple-element.15), channel_id=1, replica_groups=mesh['depth'=4,'seq'=32,'rep'=4] {'depth'}, use_global_device_ids=true, to_apply=%region_1.2 | all-reduce | flops 512 | bytes 4096 | tf_op jit(solution)/shard_map/pmax | solution.py:72
  31.8 1.2 fusion.64
  33.0 1.4 copy.42
  34.4 5.9 mul.83
  40.4 9.3 %mul.84 = f32[64,32,1024]{2,1,0:T(8,128)} reshape(f32[64,32,8,128]{3,2,1,0:T(8,128)} %mul.83) | data formatting | bytes 16777216 | tf_op jit(solution)/shard_map/mul | solution.py:71
  49.7 9.4 %multiply_reduce_fusion = (f32[64,1024]{1,0:T(8,128)S(1)}, bf16[64,32,1024]{2,1,0:T(8,128)(2,1)}, f32[64,32,1024]{2,1,0:T(8,128)}) fusion(f32[64,32,1024]{2,1,0:T(8,128)} %mul.84, bf16[64,32,512]{2,1,0:T(8,128)(2,1)S(1)} %fusion.4, bf16[1024,512]{1,0:T(8,128)(2,1)S(1)} %copy-done), kind=kOutput, calls=%fused_computation | convolution fusion | flops 2164195328 | bytes 24379392 | tf_op jit(solution)/shard_map/prc,jc->prj/dot_general | solution.py:58
  59.2 0.9 bitcast_multiply_fusion
  60.0 0.0 all-reduce.4.cloned.1.call-update
  60.1 1.3 collective-permute-start
  61.4 4.5 collective-permute-start.1
  65.9 14.4 %psum.21 = f32[64,8]{1,0:T(8,128)S(1)} all-reduce(f32[64,8]{1,0:T(8,128)S(1)} %get-tuple-element.5), channel_id=1, replica_groups=mesh['depth'=4,'seq'=32,'rep'=4] {'depth'}, use_global_device_ids=true, to_apply=%region_3.4 | all-reduce | flops 512 | bytes 4096 | tf_op jit(solution)/shard_map/psum | solution.py:74
  80.4 1.1 broadcast_multiply_fusion
  81.5 1.8 fusion.22
  83.2 0.4 copy.41
  83.6 4.5 mul.75
  88.2 9.3 %mul.76 = f32[64,32,1024]{2,1,0:T(8,128)} reshape(f32[64,32,8,128]{3,2,1,0:T(8,128)} %mul.75) | data formatting | bytes 16777216 | tf_op jit(solution)/shard_map/mul | solution.py:98
  97.5 0.0 collective-permute-done
  97.5 1.2 fusion.24
  98.6 0.0 collective-permute-done.1
  98.6 1.2 fusion.19
  99.8 1.2 fusion.13
  101.0 1.2 fusion.14
  102.1 12.0 %all_gather.6 = bf16[64,1024]{1,0:T(8,128)(2,1)S(1)} all-gather(bf16[64,256]{1,0:T(8,128)(2,1)S(1)} %fusion.14), channel_id=1, replica_groups=mesh['depth'=4,'seq'=32,'rep'=4] {'depth'}, dimensions={1}, use_global_device_ids=true | all-gather | bytes 163840 | tf_op jit(solution)/shard_map/all_gather | solution.py:90
  114.1 0.2 copy.43
  114.3 0.5 broadcast.45
  114.8 1.4 reduce.1
  116.3 0.9 reshape.95
  117.2 8.0 %all-to-all-start = ((bf16[4,2,4352]{2,1,0:T(2,128)(2,1)}), bf16[4,2,4352]{2,1,0:T(2,128)(2,1)S(1)}, u32[]{:S(2)}, u32[]{:S(2)}) async-start(bf16[4,2,4352]{2,1,0:T(2,128)(2,1)} %reshape.95), calls=%async_computation | async-start | bytes 139264 | tf_op jit(solution)/shard_map/all_to_all | solution.py:114
  125.2 9.5 %fusion.6 = f32[1024,512]{1,0:T(8,128)} fusion(bf16[64,32,512]{2,1,0:T(8,128)(2,1)S(1)} %fusion.4, f32[64,32,1024]{2,1,0:T(8,128)} %get-tuple-element.17, f32[64,32,1024]{2,1,0:T(8,128)} %mul.76, f32[64,1024]{1,0:T(8,128)S(1)} %convert_element_type.46), kind=kOutput, calls=%fused_computation.11 | convolution fusion | flops 2168455168 | bytes 21233664 | tf_op jit(solution)/shard_map/prj,prc->jc/dot_general | solution.py:108
  134.8 0.0 all-reduce.6.cloned.1.call-update
  134.8 0.0 reduce-scatter.2.cloned.1.call-start
  134.8 0.0 all-to-all-done
  134.8 0.4 reshape.96
  135.3 0.8 copy.45
  136.1 1.2 fusion.42
  137.3 0.1 fusion.65
  137.4 2.6 collective-permute-start.2
  140.0 1.3 collective-permute-start.3
  141.3 0.0 collective-permute-done.2
  141.3 4.1 collective-permute-done.3
  145.5 7.2 all-gather.1
  152.7 1.1 fusion.11
  153.8 1.1 fusion.10
  154.9 1.1 fusion.9
  156.0 1.1 fusion.8
  157.1 1.1 fusion.7
  158.3 0.8 copy-done.4
  159.1 0.0 reduce-scatter.2.cloned.1.call-update
  159.1 0.8 reshape.93
  160.0 4.6 fusion
  164.6 0.5 convolution_bitcast_fusion.5
  165.1 109.2 %psum.23 = f32[512,8]{0,1:T(8,128)} all-reduce(f32[512,8]{0,1:T(8,128)S(1)} %convolution_bitcast_fusion.5), channel_id=1, replica_groups=mesh['depth'=4,'seq'=32,'rep'=4] {'depth','seq','rep'}, use_global_device_ids=true, to_apply=%region_8.9 | all-reduce | flops 4096 | bytes 32768 | tf_op jit(solution)/shard_map/psum | solution.py:105
  274.3 336.9 %all-reduce.6.cloned.1.call-done = f32[1024,512]{1,0:T(8,128)} async-done(((f32[1024,512]{1,0:T(8,128)}), f32[1024,512]{1,0:T(8,128)}) %all-reduce.6.cloned.1.call-update) | async-done | bytes 2097168
  611.2 1.3 constant_dynamic-slice_fusion
  612.5 135.8 %reduce-scatter.2.cloned.1.call-done = f32[8,5,128]{2,0,1:T(8,128)} async-done(((f32[256,5,128]{2,0,1:T(8,128)}), f32[8,5,128]{2,0,1:T(8,128)}) %reduce-scatter.2.cloned.1.call-update) | async-done | bytes 20496 | tf_op jit(solution)/shard_map/reduce_scatter | solution.py:129
  (33 shorter events, 0.3 us)
Async XLA Ops:
  7.2 42.5 %copy-start = (bf16[1024,512]{1,0:T(8,128)(2,1)S(1)}, bf16[1024,512]{1,0:T(8,128)(2,1)}, u32[]{:S(2)}) copy-start(bf16[1024,512]{1,0:T(8,128)(2,1)} %param.16) | copy-start | bytes 3145732
  7.2 3.4 copy-start.10
  7.2 3.5 copy-start.8
  7.2 128.9 %all-reduce.4.cloned.1.call-start = ((), (), s32[]{:S(2)}) async-start(), calls=%async_computation.2 | async-start | bytes 524288 | tf_op jit(solution)/shard_map/psum | solution.py:74
  8.9 1.7 copy-start.3
  10.7 1.1 copy-start.9
  33.0 7.4 copy-start.2
  49.7 9.5 %copy-start.7 = (f32[64,8]{1,0:T(8,128)S(1)}, f32[64,8]{1,0:T(8,128)}, u32[]{:S(2)}) copy-start(f32[64,8]{1,0:T(8,128)} %pmax.7) | copy-start | bytes 6148
  49.7 10.4 %copy-start.5 = (bf16[1,64,512]{2,1,0:T(8,128)(2,1)S(1)}, bf16[1,64,512]{2,1,0:T(8,128)(2,1)}, u32[]{:S(2)}) copy-start(bf16[1,64,512]{2,1,0:T(8,128)(2,1)} %param.19) | copy-start | bytes 196612
  60.1 37.4 %collective-permute-start = (bf16[2,512]{1,0:T(2,128)(2,1)S(1)}, bf16[2,512]{1,0:T(2,128)(2,1)S(1)}, u32[]{:S(2)}, u32[]{:S(2)}) collective-permute-start(bf16[2,512]{1,0:T(2,128)(2,1)S(1)} %get-tuple-element.13), channel_id=1, source_target_pairs={{4,0},{8,4},{12,8},{16,12},{20,16},{24,20},{28,24},{32,28},{36,32}... | collective-permute-start | bytes 6152 | tf_op jit(solution)/shard_map/ppermute | solution.py:15
  61.4 37.3 %collective-permute-start.1 = (bf16[2,512]{1,0:T(2,128)(2,1)S(1)}, bf16[2,512]{1,0:T(2,128)(2,1)S(1)}, u32[]{:S(2)}, u32[]{:S(2)}) collective-permute-start(bf16[2,512]{1,0:T(2,128)(2,1)S(1)} %get-tuple-element.14), channel_id=1, source_target_pairs={{0,4},{4,8},{8,12},{12,16},{16,20},{20,24},{24,28},{28,32},{32,36}... | collective-permute-start | bytes 6152 | tf_op jit(solution)/shard_map/ppermute | solution.py:12
  88.1 11.6 %copy-start.6 = (f32[64,256]{1,0:T(8,128)S(1)}, f32[64,256]{1,0:T(8,128)}, u32[]{:S(2)}) copy-start(f32[64,256]{1,0:T(8,128)} %fusion.22) | copy-start | bytes 196612
  117.2 17.7 %all-to-all-start = ((bf16[4,2,4352]{2,1,0:T(2,128)(2,1)}), bf16[4,2,4352]{2,1,0:T(2,128)(2,1)S(1)}, u32[]{:S(2)}, u32[]{:S(2)}) async-start(bf16[4,2,4352]{2,1,0:T(2,128)(2,1)} %reshape.95), calls=%async_computation | async-start | bytes 139264 | tf_op jit(solution)/shard_map/all_to_all | solution.py:114
  125.2 486.0 %all-reduce.6.cloned.1.call-start = ((), (), s32[]{:S(2)}) async-start(), calls=%async_computation.4 | async-start | bytes 4194304
  134.8 613.5 %reduce-scatter.2.cloned.1.call-start = ((), (), s32[]{:S(2)}) async-start(), calls=%async_computation.3 | async-start | bytes 675840 | tf_op jit(solution)/shard_map/reduce_scatter | solution.py:129
  137.4 4.0 collective-permute-start.2
  140.0 5.5 collective-permute-start.3
  158.2 0.9 copy-start.4
  160.0 588.3 %copy-start.1 = (bf16[1024,512]{1,0:T(8,128)(2,1)S(1)}, bf16[1024,512]{1,0:T(8,128)(2,1)}, u32[]{:S(2)}) copy-start(bf16[1024,512]{1,0:T(8,128)(2,1)} %param.16) | copy-start | bytes 3145732
Sparse Core Ops, SparseCore 0:
  60.2 59.8 all-reduce.3
  134.9 476.2 all-reduce.5
  614.8 133.4 reduce-scatter.1
where the time goes:
time: 756 us; the launch traced here: 755 us
  waiting for transfers between devices  477 us (63%)
  blocking collectives  161 us (21%)
  matrix products  40.9 us (5%)
  local copies, waits for them, and re-layouts  38.6 us (5%)
  starting transfers between devices  17.9 us (2%)
  between operations  14.1 us (2%)
    unnamed x4, waiting for transfers between devices  337 us
    reduce_scatter x1, waiting for transfers between devices, body(): lax.psum_scatter(jnp.stack(tap_terms, axis=1), 'seq', scatter_dimension=0...  136 us
    psum x1, blocking collectives, body(): score_weight_grad = lax.psum(score_term, ('depth', 'seq', 'rep'))  109 us
    pmax x1, blocking collectives, body(): joint_top = lax.pmax(local_top, 'depth')  17.9 us
    mul x2, local copies, waits for them, and re-layouts, body(): weights[..., None] * value_heads.astype(jnp.float32)  15.2 us
  transfers between devices with their start and end apart: 8, of which 3 were waited for; matrix products, arithmetic and copies ran while one was open for 7% of the time, Pallas kernels for 0%

commit v1 on v0

v1 whole, which is shorter than its diff:
```python
import jax
import jax.numpy as jnp
from jax import lax
from jax.experimental import pallas as pl
from jax.experimental.pallas import tpu as pltpu
from jax.sharding import Mesh, PartitionSpec as P

AXES = ("depth", "z", "xlo", "xhi", "core")
SEQ = ("z", "xlo")
F32 = jnp.float32
BF16 = jnp.bfloat16
I32 = jnp.int32

TILE = 16
LANES = 128
HEADS = 8
WIDTH = 128
OWN = 2
OWN_UNITS = OWN * WIDTH
UNITS = HEADS * WIDTH
N_DEPTH = 4
N_Z = 16
PLANE = 16


def iota(shape, dim):
    return lax.broadcasted_iota(I32, shape, dim)


def dot(a, b, ca=1, cb=0):
    return lax.dot_general(a, b, (((ca,), (cb,)), ((), ())), preferred_element_type=F32)


def split_pair(value):
    high = value.astype(BF16).astype(F32)
    return high, value - high


def head_spread(lanes, units):
    lane = iota((lanes, units), 0)
    head = iota((lanes, units), 1) // WIDTH
    return ((lane == head) | (lane == head + HEADS)).astype(BF16)


def encode_kernel(
    depth_ref,
    feat_ref,
    codes_ref,
    count_ref,
    table_ref,
    value_ref,
    score_ref,
    features_out,
    values_out,
    slope_out,
    weights_out,
    top_out,
    send_out,
):
    tile, reads, channels = feat_ref.shape
    rows = tile * reads
    code = iota((LANES, rows), 0)
    hot = (code == codes_ref[0, 0:1, :]) | (code == codes_ref[0, 1:2, :] + 8)
    embed = dot(hot.astype(BF16), table_ref[...], 0, 0)
    features = (feat_ref[...].reshape(rows, channels).astype(F32) + embed).astype(BF16)
    features_out[...] = features
    scores = dot(features, score_ref[...]).reshape(tile, reads, LANES)
    read = iota((tile, reads, LANES), 1) + depth_ref[0] * reads
    live = read < count_ref[...][:, None, :]
    top = jnp.max(jnp.where(live, scores, -1e30), axis=1)
    top_high, top_rest = split_pair(top)
    top_low = top_rest.astype(BF16).astype(F32)
    top = top_high + top_low
    weights = jnp.where(live, jnp.exp(scores - top[:, None, :]), 0.0)
    total_high, total_low = split_pair(jnp.sum(weights, axis=1))
    lane = iota((tile, LANES), 1)
    stat = jnp.where(
        lane < 8,
        top_high,
        jnp.where(lane < 16, top_low, jnp.where(lane < 24, total_high, total_low)),
    ).astype(BF16)
    top_out[...] = top
    weights = weights.reshape(rows, LANES)
    weights_out[...] = weights
    high, low = split_pair(weights)
    pair = jnp.where(iota((rows, LANES), 1) < HEADS, high, low).astype(BF16)
    for part in range(N_DEPTH):
        span = slice(part * OWN_UNITS, (part + 1) * OWN_UNITS)
        preact = dot(features, value_ref[span, :], 1, 1)
        lanes = iota((LANES, OWN_UNITS), 0)
        head = iota((LANES, OWN_UNITS), 1) // WIDTH + part * OWN
        spread = ((lanes == head) | (lanes == head + HEADS)).astype(BF16)
        spread = dot(pair, spread)
        sigma = 0.5 * jnp.tanh(0.5 * preact) + 0.5
        values = preact * sigma
        slope = sigma + values * (1.0 - sigma)
        values_out[:, span] = values.astype(BF16)
        slope_out[:, span] = (spread * slope).astype(BF16)
        pool = jnp.sum((spread * values).reshape(tile, reads, OWN_UNITS), axis=1)
        send_out[part, :, 0:OWN_UNITS] = pool.astype(BF16)
        send_out[part, :, OWN_UNITS:] = stat


def encode(depth_index, feats, codes, counts, table, value_weight, score_weight):
    positions, reads, channels = feats.shape
    rows = positions * reads
    step = TILE * reads
    whole = lambda i: (0, 0)
    by_row = lambda i: (i, 0)
    return pl.pallas_call(
        encode_kernel,
        grid=(positions // TILE,),
        in_specs=[
            pl.BlockSpec(memory_space=pltpu.SMEM),
            pl.BlockSpec((TILE, reads, channels), lambda i: (i, 0, 0)),
            pl.BlockSpec((1, 2, step), lambda i: (i, 0, 0)),
            pl.BlockSpec((TILE, LANES), by_row),
            pl.BlockSpec((LANES, channels), whole),
            pl.BlockSpec((UNITS, channels), whole),
            pl.BlockSpec((channels, LANES), whole),
        ],
        out_specs=[
            pl.BlockSpec((step, channels), by_row),
            pl.BlockSpec((step, UNITS), by_row),
            pl.BlockSpec((step, UNITS), by_row),
            pl.BlockSpec((step, LANES), by_row),
            pl.BlockSpec((TILE, LANES), by_row),
            pl.BlockSpec((N_DEPTH, TILE, OWN_UNITS + LANES), lambda i: (0, i, 0)),
        ],
        out_shape=[
            jax.ShapeDtypeStruct((rows, channels), BF16),
            jax.ShapeDtypeStruct((rows, UNITS), BF16),
            jax.ShapeDtypeStruct((rows, UNITS), BF16),
            jax.ShapeDtypeStruct((rows, LANES), F32),
            jax.ShapeDtypeStruct((positions, LANES), F32),
            jax.ShapeDtypeStruct((N_DEPTH, positions, OWN_UNITS + LANES), BF16),
        ],
        compiler_params=pltpu.CompilerParams(vmem_limit_bytes=32 * 2**20),
        cost_estimate=pl.CostEstimate(
            flops=2 * rows * UNITS * (channels + 256),
            bytes_accessed=16 * 2**20,
            transcendentals=rows * UNITS,
        ),
    )(depth_index, feats, codes, counts, table, value_weight, score_weight)


def combine_kernel(depth_ref, recv_ref, grad_ref, payload_out, pooled_out):
    positions = grad_ref.shape[0]
    own = depth_ref[0] * OWN
    lane = iota((LANES, OWN_UNITS), 0)
    head = iota((LANES, OWN_UNITS), 1) // WIDTH + own
    spread_top = ((lane == head) | (lane == head + 8)).astype(BF16)
    spread_total = ((lane == head + 16) | (lane == head + 24)).astype(BF16)
    stats = [recv_ref[d, :, OWN_UNITS:] for d in range(N_DEPTH)]
    tops = [dot(stat, spread_top) for stat in stats]
    top = jnp.maximum(jnp.maximum(tops[0], tops[1]), jnp.maximum(tops[2], tops[3]))
    total = jnp.zeros_like(top)
    pooled = jnp.zeros_like(top)
    for d in range(N_DEPTH):
        scale = jnp.exp(tops[d] - top)
        total += scale * dot(stats[d], spread_total)
        pooled += scale * recv_ref[d, :, 0:OWN_UNITS].astype(F32)
    pooled = pooled / total
    grad = grad_ref[...]
    product = grad.astype(F32) * pooled
    row = iota((OWN_UNITS, OWN_UNITS), 0)
    column = iota((OWN_UNITS, OWN_UNITS), 1)
    source = ((column % 128) // 8) * 16 + (column // 128) * 8 + column % 8
    ordered = dot(pooled.astype(BF16), (row == source).astype(BF16)).astype(BF16)
    pooled_out[0] = ordered[:, 0:128]
    pooled_out[1] = ordered[:, 128:256]
    lane = iota((positions, LANES), 1)
    stat = jnp.zeros((positions, LANES), F32)
    for i in range(OWN):
        span = slice(i * WIDTH, (i + 1) * WIDTH)
        row_total = jnp.sum(product[:, span], axis=1, keepdims=True)
        terms = (top[:, span], total[:, span], jnp.broadcast_to(row_total, (positions, WIDTH)))
        for k, term in enumerate(terms):
            high, low = split_pair(term)
            stat = jnp.where(lane == 4 * k + i, high, stat)
            stat = jnp.where(lane == 4 * k + 2 + i, low, stat)
    stat = stat.astype(BF16)
    for d in range(N_DEPTH):
        payload_out[d, :, 0:OWN_UNITS] = grad
        payload_out[d, :, OWN_UNITS:] = stat


def combine(depth_index, recv, grad):
    positions = grad.shape[0]
    vmem = pl.BlockSpec(memory_space=pltpu.VMEM)
    return pl.pallas_call(
        combine_kernel,
        in_specs=[pl.BlockSpec(memory_space=pltpu.SMEM), vmem, vmem],
        out_specs=[vmem, vmem],
        out_shape=[
            jax.ShapeDtypeStruct(recv.shape, BF16),
            jax.ShapeDtypeStruct((2, positions, 128), BF16),
        ],
        cost_estimate=pl.CostEstimate(flops=10**7, bytes_accessed=500_000, transcendentals=10**5),
    )(depth_index, recv, grad)


def gradient_kernel(
    core_ref,
    payload_ref,
    top_ref,
    weights_ref,
    slope_ref,
    values_ref,
    features_ref,
    mine_out,
    theirs_out,
    total,
    score_total,
):
    step = pl.program_id(0)
    tile = top_ref.shape[0]
    rows, channels = features_ref.shape
    reads = rows // tile
    lane = iota((LANES, LANES), 0)
    target = iota((LANES, LANES), 1)
    joint = [jnp.zeros((tile, LANES), F32) for _ in range(3)]
    for d in range(N_DEPTH):
        stat = payload_ref[d, :, OWN_UNITS:]
        for k in range(3):
            first = (lane // 4 == k) & (target < 2 * HEADS)
            pick = first & (lane % 2 + 2 * d == target % HEADS)
            joint[k] += dot(stat, pick.astype(BF16))
    small = iota((tile, LANES), 1)
    scale = jnp.where(
        small < 2 * HEADS,
        jnp.exp(top_ref[...] - joint[0]) / jnp.where(small < 2 * HEADS, joint[1], 1.0),
        0.0,
    )
    spread = head_spread(LANES, UNITS)
    high, low = split_pair(scale)
    pair = jnp.where(small < HEADS, high, low).astype(BF16)
    scale_units = dot(pair, spread)
    grad = jnp.concatenate(
        [payload_ref[d, :, 0:OWN_UNITS].astype(F32) for d in range(N_DEPTH)], axis=1
    )
    scaled = grad * scale_units
    features = features_ref[...]
    slope = slope_ref[...].astype(F32).reshape(tile, reads, UNITS)
    value_grad = (slope * scaled[:, None, :]).reshape(rows, UNITS).astype(BF16)
    values = values_ref[...].astype(F32).reshape(tile, reads, UNITS)
    product = (values * grad[:, None, :]).reshape(rows, UNITS).astype(BF16)
    prob_grad = dot(product, spread, 1, 1).reshape(tile, reads, LANES)
    weights = weights_ref[...].reshape(tile, reads, LANES)
    score_grad = weights * scale[:, None, :] * (prob_grad - joint[2][:, None, :])
    score_grad = score_grad.reshape(rows, LANES).astype(BF16)

    @pl.when(step == 0)
    def _():
        total[...] = jnp.zeros_like(total)
        score_total[...] = jnp.zeros_like(score_total)

    term = dot(value_grad, features, 0, 0)
    for q in range(4):
        total[q] += term[:, q * 128 : (q + 1) * 128]
    score_total[...] += dot(score_grad, features, 0, 0)

    @pl.when(step == pl.num_programs(0) - 1)
    def _():
        first = core_ref[0] == 0
        for peer in range(PLANE):
            base = (peer // 4) * 256 + (peer % 4) * 4
            for q in range(4):
                for t in range(2):
                    zero = total[q, pl.ds(base + t, N_Z, stride=16), :]
                    one = total[q, pl.ds(base + 2 + t, N_Z, stride=16), :]
                    span = slice(q * 32 + t * 16, q * 32 + t * 16 + 16)
                    mine_out[peer, span, :] = jnp.where(first, zero, one).astype(BF16)
                    theirs_out[peer, span, :] = jnp.where(first, one, zero).astype(BF16)
        score = score_total[0:HEADS, :]
        score = [score[:, q * 128 : (q + 1) * 128] for q in range(4)]
        score = jnp.concatenate(score + [jnp.zeros((96, 128), F32)], axis=0).astype(BF16)
        mine_out[PLANE] = score
        theirs_out[PLANE] = score


def gradients(core_index, payload, top, weights, slope, values, features):
    rows, channels = features.shape
    positions = top.shape[0]
    step = rows // positions * TILE
    by_row = lambda i: (i, 0)
    whole = lambda i: (0, 0, 0)
    shape = (PLANE + 1, 128, 128)
    return pl.pallas_call(
        gradient_kernel,
        grid=(positions // TILE,),
        in_specs=[
            pl.BlockSpec(memory_space=pltpu.SMEM),
            pl.BlockSpec((N_DEPTH, TILE, OWN_UNITS + LANES), lambda i: (0, i, 0)),
            pl.BlockSpec((TILE, LANES), by_row),
            pl.BlockSpec((step, LANES), by_row),
            pl.BlockSpec((step, UNITS), by_row),
            pl.BlockSpec((step, UNITS), by_row),
            pl.BlockSpec((step, channels), by_row),
        ],
        out_specs=[pl.BlockSpec(shape, whole), pl.BlockSpec(shape, whole)],
        out_shape=[jax.ShapeDtypeStruct(shape, BF16)] * 2,
        scratch_shapes=[
            pltpu.VMEM((4, UNITS, 128), F32),
            pltpu.VMEM((LANES, channels), F32),
        ],
        compiler_params=pltpu.CompilerParams(vmem_limit_bytes=32 * 2**20),
        cost_estimate=pl.CostEstimate(
            flops=2 * rows * UNITS * (channels + 256),
            bytes_accessed=16 * 2**20,
            transcendentals=10**4,
        ),
    )(core_index, payload, top, weights, slope, values, features)


def pair_kernel(mine_ref, theirs_ref, send_out):
    score = mine_ref[PLANE, 0:32, :].astype(F32) + theirs_ref[PLANE, 0:32, :].astype(F32)
    score = score.astype(BF16)
    for peer in range(PLANE):
        value = mine_ref[peer].astype(F32) + theirs_ref[peer].astype(F32)
        send_out[peer, 0:128, :] = value.astype(BF16)
        send_out[peer, 128:160, :] = score


def conv_kernel(pooled_ref, grads_ref, part_out):
    peers, positions, _ = pooled_ref.shape
    taps = part_out.shape[1] // 8
    half = taps // 2
    sides = []
    for k in range(taps):
        first = 2 * half - k
        sides.append(
            jnp.concatenate(
                [grads_ref[j].astype(F32)[first : first + positions] for j in range(peers)], axis=0
            ).astype(BF16)
        )
    left = pooled_ref[...].reshape(peers * positions, 128)
    for k in range(taps):
        part = dot(left, sides[k], 0, 0)
        part_out[:, k * 8 : (k + 1) * 8, :] = part.reshape(N_Z, 8, 128)


def line_kernel(recv_ref, conv_ref, send_out, total):
    value = recv_ref[0].astype(F32)
    for peer in range(1, PLANE):
        value += recv_ref[peer].astype(F32)
    total[...] = value
    score = value[128:160]
    for z in range(N_Z):
        block = jnp.concatenate([total[pl.ds(z, 8, stride=16), :], score, conv_ref[z]], axis=0)
        send_out[z] = block.astype(BF16)


def last_kernel(recv_ref, value_out, score_out, conv_out):
    value = recv_ref[0].astype(F32)
    for z in range(1, N_Z):
        value += recv_ref[z].astype(F32)
    for q in range(4):
        span = slice(q * 128, (q + 1) * 128)
        value_out[:, span] = value[2 * q : 2 * q + 2]
        score_out[:, span] = value[8 + 8 * q : 16 + 8 * q]
    for k in range(conv_out.shape[1]):
        conv_out[:, k, :] = value[40 + 8 * k : 48 + 8 * k]


def small_call(kernel, shapes, *operands, scratch=()):
    vmem = pl.BlockSpec(memory_space=pltpu.VMEM)
    single = not isinstance(shapes, list)
    out = pl.pallas_call(
        kernel,
        in_specs=[vmem] * len(operands),
        out_specs=vmem if single else [vmem] * len(shapes),
        out_shape=shapes,
        scratch_shapes=list(scratch),
        cost_estimate=pl.CostEstimate(flops=10**8, bytes_accessed=10**6, transcendentals=0),
    )(*operands)
    return out


def exchange(block, axis):
    return lax.ppermute(block, axis, [(0, 1), (1, 0)])


def body(
    read_feats,
    base_codes,
    qual_codes,
    depth_counts,
    base_table,
    qual_table,
    value_weight,
    score_weight,
    conv_weight,
    cotangent,
):
    _, positions, reads, channels = read_feats.shape
    block_units, taps, outs = conv_weight.shape
    half = taps // 2
    depth_index = lax.axis_index("depth").reshape(1)
    core_index = lax.axis_index("core")
    xhi_index = lax.axis_index("xhi")
    xlo_index = lax.axis_index("xlo")
    rim = positions + 2 * half

    count = lax.axis_size(SEQ)
    forward = [(i, i + 1) for i in range(count - 1)]
    grad_local = cotangent[0]
    low = lax.ppermute(grad_local[-half:], SEQ, forward)
    high = lax.ppermute(grad_local[:half], SEQ, [(b, a) for a, b in forward])
    grad_rim = jnp.concatenate([low, grad_local, high], axis=0)

    empty = LANES - base_table.shape[0] - qual_table.shape[0]
    table = jnp.concatenate([base_table, qual_table, jnp.zeros((empty, channels), BF16)], axis=0)
    score_lanes = jnp.pad(jnp.tile(score_weight, (1, 4)), ((0, 0), (0, LANES - 4 * HEADS)))
    tiles = positions // TILE
    codes = jnp.stack(
        [base_codes[0].reshape(tiles, TILE * reads), qual_codes[0].reshape(tiles, TILE * reads)],
        axis=1,
    )
    counts = jnp.broadcast_to(depth_counts[0][:, None], (positions, LANES))
    features, values, slope, weights, top, pool_send = encode(
        depth_index, read_feats[0], codes, counts, table, value_weight, score_lanes
    )
    pool_recv = lax.all_to_all(pool_send, "depth", split_axis=0, concat_axis=0, tiled=True)

    shifted = [grad_rim[2 * half - k : 2 * half - k + positions] for k in range(taps)]
    block_grad = dot(
        jnp.concatenate(shifted, axis=1), conv_weight.reshape(block_units, taps * outs), 1, 1
    ).astype(BF16)
    payload, pooled = combine(depth_index, pool_recv, block_grad)
    payload = lax.all_to_all(payload, "depth", split_axis=0, concat_axis=0, tiled=True)

    mine, theirs = gradients(
        core_index.reshape(1), payload, top, weights, slope, values, features
    )
    theirs = exchange(theirs, "core")
    plane_send = small_call(
        pair_kernel, jax.ShapeDtypeStruct((PLANE, 160, 128), BF16), mine, theirs
    )
    plane_recv = lax.all_to_all(
        plane_send, ("depth", "xlo", "xhi"), split_axis=0, concat_axis=0, tiled=True
    )

    give = lax.dynamic_index_in_dim(pooled, 1 - xlo_index, 0, keepdims=False)
    keep = lax.dynamic_index_in_dim(pooled, xlo_index, 0, keepdims=False)
    both = jnp.stack([keep, exchange(give, "xlo")])
    both = jnp.concatenate([both, exchange(both, "core")], axis=0)
    pooled = jnp.concatenate([both, exchange(both, "xhi")], axis=0)

    cols = grad_rim.reshape(rim, 2, 2, outs // 4)
    give = lax.dynamic_index_in_dim(cols, 1 - core_index, 2, keepdims=False)
    keep = lax.dynamic_index_in_dim(cols, core_index, 2, keepdims=False)
    both = jnp.stack([keep, exchange(give, "core")])
    give = lax.dynamic_index_in_dim(both, 1 - xhi_index, 2, keepdims=False)
    keep = lax.dynamic_index_in_dim(both, xhi_index, 2, keepdims=False)
    both = jnp.stack([keep, exchange(give, "xhi")])
    both = both.reshape(4, rim, outs // 4)
    grads = jnp.stack([both, exchange(both, "xlo")], axis=1).reshape(8, rim, outs // 4)

    conv_part = small_call(
        conv_kernel, jax.ShapeDtypeStruct((N_Z, 8 * taps, 128), F32), pooled, grads
    )

    line_send = small_call(
        line_kernel,
        jax.ShapeDtypeStruct((N_Z, 40 + 8 * taps, 128), BF16),
        plane_recv,
        conv_part,
        scratch=[pltpu.VMEM((160, 128), F32)],
    )
    line_recv = lax.all_to_all(line_send, "z", split_axis=0, concat_axis=0, tiled=True)
    value_weight_grad, score_weight_grad, conv_weight_grad = small_call(
        last_kernel,
        [
            jax.ShapeDtypeStruct((2, channels), F32),
            jax.ShapeDtypeStruct((HEADS, channels), F32),
            jax.ShapeDtypeStruct((8, taps, 128), F32),
        ],
        line_recv,
    )
    return (value_weight_grad, score_weight_grad.T, conv_weight_grad)


def solution(mesh):
    fine = Mesh(mesh.devices.reshape(N_DEPTH, N_Z, 2, 2, 2), AXES)
    rep = ("xhi", "core")
    placed = (
        P(rep, SEQ, "depth", None),
        P(rep, SEQ, "depth"),
        P(rep, SEQ, "depth"),
        P(rep, SEQ),
        P(),
        P(),
        P(),
        P(),
        P("depth", None, None),
        P(rep, SEQ, None),
    )
    return jax.shard_map(
        body,
        mesh=fine,
        in_specs=placed,
        out_specs=(P(AXES, None), P(), P(("depth",) + SEQ, None, rep)),
        check_vma=False,
    )
```

time: 756 us -> 146 us (0.19)
  the two profiles are of different devices: /device:TPU:4 before, /device:TPU:32 now
where the time goes in v1:
time: 146 us; the launch traced here: 145 us
  starting transfers between devices  40 us (27%)
  blocking collectives  35.2 us (24%)
  Pallas kernels  27.1 us (19%)
  local copies, waits for them, and re-layouts  22 us (15%)
  waiting for transfers between devices  14.9 us (10%)
  other arithmetic  2.48 us (2%)
  matrix products  2.27 us (2%)
    all_to_all x1, blocking collectives, body(): lax.all_to_all(line_send, 'z', split_axis=0, concat_axis=0, tiled=True)  35.2 us
    ppermute x7, starting transfers between devices, exchange(): return lax.ppermute(block, axis, [(0, 1), (1, 0)])  20.5 us
    unnamed x33, local copies, waits for them, and re-layouts  19.9 us
    pallas_call x1, Pallas kernels, gradients(): pl.pallas_call(gradient_kernel, grid=(positions // TILE,), in_specs=[pl.B...  9.47 us
    pallas_call x4, Pallas kernels, small_call(): pl.pallas_call(kernel, in_specs=[vmem] * len(operands), out_specs=vmem if...  7.93 us
    pallas_call x1, Pallas kernels, encode(): pl.pallas_call(encode_kernel, grid=(positions // TILE,), in_specs=[pl.Blo...  7.68 us
    ppermute x7, waiting for transfers between devices, exchange(): return lax.ppermute(block, axis, [(0, 1), (1, 0)])  7.14 us
    all_to_all x1, waiting for transfers between devices, body(): lax.all_to_all(payload, 'depth', split_axis=0, concat_axis=0, tiled=True)  6.25 us
  transfers between devices with their start and end apart: 12, of which 4 were waited for; matrix products, arithmetic and copies ran while one was open for 7% of the time, Pallas kernels for 8%

profile of v1, /device:TPU:32, one launch (start us, length us, event | category | flops | bytes accessed | tf_op | source)
XLA Modules:
  0.0 144.9 jit_solution(7961531207778211314)
XLA Ops:
  0.6 0.0 copy-start
  0.6 0.7 slice_bitcast_fusion
  1.4 3.4 %collective-permute-start.1 = (bf16[2,512]{1,0:T(2,128)(2,1)S(1)}, bf16[2,512]{1,0:T(2,128)(2,1)S(1)}, u32[]{:S(2)}, u32[]{:S(2)}) collective-permute-start(bf16[2,512]{1,0:T(2,128)(2,1)S(1)} %get-tuple-element.42), channel_id=1, source_target_pairs={{0,4},{4,8},{8,12},{12,16},{16,20},{20,24},{24,28},{28,32},{32,36}... | collective-permute-start | bytes 6152 | tf_op jit(solution)/shard_map/ppermute | solution.py:408
  4.8 3.3 %collective-permute-start = (bf16[2,512]{1,0:T(2,128)(2,1)S(1)}, bf16[2,512]{1,0:T(2,128)(2,1)S(1)}, u32[]{:S(2)}, u32[]{:S(2)}) collective-permute-start(bf16[2,512]{1,0:T(2,128)(2,1)S(1)} %get-tuple-element.43), channel_id=1, source_target_pairs={{4,0},{8,4},{12,8},{16,12},{20,16},{24,20},{28,24},{32,28},{36,32}... | collective-permute-start | bytes 6152 | tf_op jit(solution)/shard_map/ppermute | solution.py:409
  8.1 0.8 copy.25
  8.9 0.1 stack_reshape_squeeze.8
  9.0 0.8 copy.26
  9.8 0.1 stack_reshape_squeeze.9
  9.9 0.0 copy-done
  9.9 0.1 copy.29
  10.1 0.1 pad.26.clone
  10.2 1.0 maximum_maximum_fusion.table_ref
  11.2 0.7 broadcast_in_dim.11.count_ref
  11.9 1.6 %copy-done.2 = bf16[1,64,32,512]{3,2,1,0:T(8,128)(2,1)S(1)} copy-done((bf16[1,64,32,512]{3,2,1,0:T(8,128)(2,1)S(1)}, bf16[1,64,32,512]{3,2,1,0:T(8,128)(2,1)}, u32[]{:S(2)}) %copy-start.2) | copy-done | bytes 2097176
  13.5 1.2 copy-done.3
  14.7 7.7 %shard_map.121 = (bf16[2048,512]{1,0:T(8,128)(2,1)S(1)}, bf16[2048,1024]{1,0:T(8,128)(2,1)S(1)}, bf16[2048,1024]{1,0:T(8,128)(2,1)S(1)}, f32[2048,128]{1,0:T(8,1...) custom-call(s32[1]{0:T(128)} %bitcast.1.depth_ref, bf16[64,32,512]{2,1,0:T(8,128)(2,1)S(1)} %bitcast.37, ...), custom_call_target="tpu_custom_call" | custom-call | flops 3221225472 | bytes 16777216 | tf_op jit(solution)/shard_map/pallas_call | solution.py:110
  22.4 2.0 %copy-done.4 = bf16[2048,1024]{1,0:T(8,128)(2,1)} copy-done((bf16[2048,1024]{1,0:T(8,128)(2,1)}, bf16[2048,1024]{1,0:T(8,128)(2,1)S(1)}, u32[]{:S(2)}) %copy-start.4) | copy-done | bytes 4194328
  24.4 2.0 %copy-done.6 = bf16[2048,1024]{1,0:T(8,128)(2,1)} copy-done((bf16[2048,1024]{1,0:T(8,128)(2,1)}, bf16[2048,1024]{1,0:T(8,128)(2,1)S(1)}, u32[]{:S(2)}) %copy-start.6) | copy-done | bytes 4194328
  26.4 4.5 %all-to-all-start = ((bf16[4,64,384]{2,1,0:T(8,128)(2,1)}), bf16[4,64,384]{2,1,0:T(8,128)(2,1)S(1)}, u32[]{:S(2)}, u32[]{:S(2)}) async-start(bf16[4,64,384]{2,1,0:T(8,128)(2,1)} %get-tuple-element.16), calls=%async_computation | async-start | bytes 393216 | tf_op jit(solution)/shard_map/all_to_all | solution.py:424
  30.9 2.5 %copy.30 = bf16[256,5,512]{0,2,1:T(8,128)(2,1)} copy(bf16[256,5,512]{2,0,1:T(8,128)(2,1)} %param.18) | data formatting | bytes 2621440 | tf_op args[8]
  33.3 0.0 collective-permute-done
  33.3 0.0 copy-done.9
  33.4 0.0 collective-permute-done.1
  33.5 2.3 %convolution_convert_fusion.grad_ref = bf16[64,256]{1,0:T(8,128)(2,1)} fusion(bf16[64,2560]{1,0:T(8,128)(2,1)S(1)} %fusion.4, bf16[256,2560]{0,1:T(8,128)(2,1)} %bitcast.38), kind=kOutput, calls=%fused_computation | convolution fusion | flops 83902464 | bytes 1671168 | tf_op jit(solution)/shard_map/dot_general | solution.py:31
  35.7 1.4 all-to-all-done.recv_ref
  37.2 0.7 copy-done.10
  37.9 2.0 %shard_map.122 = (bf16[4,64,384]{2,1,0:T(8,128)(2,1)}, bf16[2,64,128]{2,1,0:T(8,128)(2,1)}) custom-call(s32[1]{0:T(128)} %bitcast.1.depth_ref, bf16[4,64,384]{2,1,0:T(8,128)(2,1)} %copy-done.10, bf16[64,256]{1,0:T(8,128)(2,1)} %convolution_convert_fusion.grad_ref), custom_call_target="tpu_custom_call" | custom-call | flops 10000000 | bytes 500000 | tf_op jit(solution)/shard_map/pallas_call | solution.py:191
  39.9 3.4 %all-to-all-start.1 = ((bf16[4,64,384]{2,1,0:T(8,128)(2,1)}), bf16[4,64,384]{2,1,0:T(8,128)(2,1)S(1)}, u32[]{:S(2)}, u32[]{:S(2)}) async-start(bf16[4,64,384]{2,1,0:T(8,128)(2,1)} %get-tuple-element.17), calls=%async_computation.1 | async-start | bytes 393216 | tf_op jit(solution)/shard_map/all_to_all | solution.py:431
  43.3 6.3 %all-to-all-done.1.payload_ref = bf16[4,64,384]{2,1,0:T(8,128)(2,1)S(1)} async-done(((bf16[4,64,384]{2,1,0:T(8,128)(2,1)}), bf16[4,64,384]{2,1,0:T(8,128)(2,1)S(1)}, u32[]{:S(2)}, u32[]{:S(2)}) %all-to-all-start.1) | async-done | bytes 196640 | tf_op jit(solution)/shard_map/all_to_all | solution.py:431
  49.6 2.2 %copy-done.5 = bf16[2048,1024]{1,0:T(8,128)(2,1)S(1)} copy-done((bf16[2048,1024]{1,0:T(8,128)(2,1)S(1)}, bf16[2048,1024]{1,0:T(8,128)(2,1)}, u32[]{:S(2)}) %copy-start.5) | copy-done | bytes 4194328
  51.7 2.2 %copy-done.7 = bf16[2048,1024]{1,0:T(8,128)(2,1)S(1)} copy-done((bf16[2048,1024]{1,0:T(8,128)(2,1)S(1)}, bf16[2048,1024]{1,0:T(8,128)(2,1)}, u32[]{:S(2)}) %copy-start.7) | copy-done | bytes 4194328
  53.9 9.5 %shard_map.123 = (bf16[17,128,128]{2,1,0:T(8,128)(2,1)S(1)}, bf16[17,128,128]{2,1,0:T(8,128)(2,1)S(1)}) custom-call(s32[1]{0:T(128)} %bitcast.core_ref, bf16[4,64,384]{2,1,0:T(8,128)(2,1)S(1)} %all-to-all-done.1.payload_ref, f32[64,128]{1,0:T(8,128)S(1)} %get-tuple-element.18.top_ref, f32[2048,128]{1,0:T(8,128)S(1)} %get-tuple-element.19.weights_ref, ...), custom_call_target="tpu_custom_call" | custom-call | flops 3221225472 | bytes 16777216 | tf_op jit(solution)/shard_map/pallas_call | solution.py:289
  63.4 0.0 copy-start.1
  63.4 0.8 copy-done.1
  64.2 1.9 %collective-permute-start.2 = (bf16[17,128,128]{2,1,0:T(8,128)(2,1)S(1)}, bf16[17,128,128]{2,1,0:T(8,128)(2,1)S(1)}, u32[]{:S(2)}, u32[]{:S(2)}) collective-permute-start(bf16[17,128,128]{2,1,0:T(8,128)(2,1)S(1)} %get-tuple-element.24), channel_id=1, source_target_pairs={{0,1},{1,0},{2,3},{3,2},{4,5},{5,4},{6,7},{7,6},{8,9},{9,8},{10,11... | collective-permute-start | bytes 1671176 | tf_op jit(solution)/shard_map/ppermute | solution.py:381
  66.2 0.1 constant_dynamic-update-slice_fusion.2
  66.3 0.2 constant_dynamic-slice_fusion
  66.4 2.4 %collective-permute-start.6 = (bf16[68,2,128]{2,0,1:T(8,128)(2,1)S(1)}, bf16[68,2,128]{2,0,1:T(8,128)(2,1)S(1)}, u32[]{:S(2)}, u32[]{:S(2)}) collective-permute-start(bf16[68,2,128]{2,0,1:T(8,128)(2,1)S(1)} %bitcast.51), channel_id=1, source_target_pairs={{0,1},{1,0},{2,3},{3,2},{4,5},{5,4},{6,7},{7,6},{8,9},{9,8},{10,11... | collective-permute-start | bytes 104456 | tf_op jit(solution)/shard_map/ppermute | solution.py:381
  68.9 0.0 copy-done.12
  68.9 2.5 %collective-permute-start.3 = (bf16[64,128]{1,0:T(8,128)(2,1)S(1)}, bf16[64,128]{1,0:T(8,128)(2,1)S(1)}, u32[]{:S(2)}, u32[]{:S(2)}) collective-permute-start(bf16[64,128]{1,0:T(8,128)(2,1)S(1)} %get-tuple-element.45), channel_id=1, source_target_pairs={{0,4},{4,0},{1,5},{5,1},{2,6},{6,2},{3,7},{7,3},{8,12},{12,8},{9,1... | collective-permute-start | bytes 49160 | tf_op jit(solution)/shard_map/ppermute | solution.py:381
  71.4 0.0 collective-permute-done.2.theirs_ref
  71.4 0.0 copy-start.11
  71.4 0.8 copy-done.11
  72.2 2.2 %shard_map.124 = bf16[16,160,128]{2,1,0:T(8,128)(2,1)} custom-call(bf16[17,128,128]{2,1,0:T(8,128)(2,1)} %copy-done.1, bf16[17,128,128]{2,1,0:T(8,128)(2,1)} %copy-done.11), custom_call_target="tpu_custom_call" | custom-call | flops 100000000 | bytes 1000000 | tf_op jit(solution)/shard_map/pallas_call | solution.py:369
  74.4 5.0 %all-to-all-start.2 = ((bf16[16,160,128]{2,1,0:T(8,128)(2,1)}), bf16[16,160,128]{2,1,0:T(8,128)(2,1)S(1)}, u32[]{:S(2)}, u32[]{:S(2)}) async-start(bf16[16,160,128]{2,1,0:T(8,128)(2,1)} %shard_map.124), calls=%async_computation.2 | async-start | bytes 1310720 | tf_op jit(solution)/shard_map/all_to_all | solution.py:440
  79.4 0.0 collective-permute-done.6
  79.4 5.3 %collective-permute-start.7 = (bf16[2,68,128]{2,1,0:T(8,128)(2,1)S(1)}, bf16[2,68,128]{2,1,0:T(8,128)(2,1)S(1)}, u32[]{:S(2)}, u32[]{:S(2)}) collective-permute-start(bf16[2,68,128]{2,1,0:T(8,128)(2,1)S(1)} %get-tuple-element.39), channel_id=1, source_target_pairs={{0,2},{2,0},{1,3},{3,1},{4,6},{6,4},{5,7},{7,5},{8,10},{10,8},{9,1... | collective-permute-start | bytes 104456 | tf_op jit(solution)/shard_map/ppermute | solution.py:381
  84.8 0.0 collective-permute-done.3
  84.8 1.9 %collective-permute-start.4 = (bf16[2,64,128]{2,1,0:T(8,128)(2,1)S(1)}, bf16[2,64,128]{2,1,0:T(8,128)(2,1)S(1)}, u32[]{:S(2)}, u32[]{:S(2)}) collective-permute-start(bf16[2,64,128]{2,1,0:T(8,128)(2,1)S(1)} %pad_maximum_fusion.6), channel_id=1, source_target_pairs={{0,1},{1,0},{2,3},{3,2},{4,5},{5,4},{6,7},{7,6},{8,9},{9,8},{10,11... | collective-permute-start | bytes 98312 | tf_op jit(solution)/shard_map/ppermute | solution.py:381
  86.7 4.1 %collective-permute-done.7 = bf16[2,68,128]{2,1,0:T(8,128)(2,1)S(1)} collective-permute-done((bf16[2,68,128]{2,1,0:T(8,128)(2,1)S(1)}, bf16[2,68,128]{2,1,0:T(8,128)(2,1)S(1)}, u32[]{:S(2)}, u32[]{:S(2)}) %collective-permute-start.7) | collective-permute-done | bytes 34848 | tf_op jit(solution)/shard_map/ppermute | solution.py:381
  90.9 2.5 %collective-permute-start.8 = (bf16[4,68,128]{2,1,0:T(8,128)(2,1)S(1)}, bf16[4,68,128]{2,1,0:T(8,128)(2,1)S(1)}, u32[]{:S(2)}, u32[]{:S(2)}) collective-permute-start(bf16[4,68,128]{2,1,0:T(8,128)(2,1)S(1)} %bitcast.44), channel_id=1, source_target_pairs={{0,4},{4,0},{1,5},{5,1},{2,6},{6,2},{3,7},{7,3},{8,12},{12,8},{9,1... | collective-permute-start | bytes 208904 | tf_op jit(solution)/shard_map/ppermute | solution.py:381
  93.4 0.0 collective-permute-done.4
  93.4 4.0 %collective-permute-start.5 = (bf16[4,64,128]{2,1,0:T(8,128)(2,1)S(1)}, bf16[4,64,128]{2,1,0:T(8,128)(2,1)S(1)}, u32[]{:S(2)}, u32[]{:S(2)}) collective-permute-start(bf16[4,64,128]{2,1,0:T(8,128)(2,1)S(1)} %pad_maximum_fusion.5), channel_id=1, source_target_pairs={{0,2},{2,0},{1,3},{3,1},{4,6},{6,4},{5,7},{7,5},{8,10},{10,8},{9,1... | collective-permute-start | bytes 196616 | tf_op jit(solution)/shard_map/ppermute | solution.py:381
  97.4 0.0 collective-permute-done.8
  97.4 0.7 pad_maximum_fusion
  98.1 3.0 %collective-permute-done.5 = bf16[4,64,128]{2,1,0:T(8,128)(2,1)S(1)} collective-permute-done((bf16[4,64,128]{2,1,0:T(8,128)(2,1)S(1)}, bf16[4,64,128]{2,1,0:T(8,128)(2,1)S(1)}, u32[]{:S(2)}, u32[]{:S(2)}) %collective-permute-start.5) | collective-permute-done | bytes 65568 | tf_op jit(solution)/shard_map/ppermute | solution.py:381
  101.1 0.7 pad_maximum_fusion.1.pooled_ref
  101.7 2.1 %shard_map.125.conv_ref = f32[16,40,128]{2,1,0:T(8,128)} custom-call(bf16[8,64,128]{2,1,0:T(8,128)(2,1)} %pad_maximum_fusion.1.pooled_ref, bf16[8,68,128]{2,1,0:T(8,128)(2,1)} %bitcast.43), custom_call_target="tpu_custom_call" | custom-call | flops 100000000 | bytes 1000000 | tf_op jit(solution)/shard_map/pallas_call | solution.py:369
  103.8 0.0 all-to-all-done.2.recv_ref
  103.8 0.8 copy-done.8
  104.7 2.0 %shard_map.126 = bf16[16,80,128]{2,1,0:T(8,128)(2,1)} custom-call(bf16[16,160,128]{2,1,0:T(8,128)(2,1)} %copy-done.8, f32[16,40,128]{2,1,0:T(8,128)} %shard_map.125.conv_ref), custom_call_target="tpu_custom_call" | custom-call | flops 100000000 | bytes 1000000 | tf_op jit(solution)/shard_map/pallas_call | solution.py:369
  106.7 35.2 %all_to_all.20.recv_ref = bf16[16,80,128]{2,1,0:T(8,128)(2,1)} all-to-all(bf16[16,80,128]{2,1,0:T(8,128)(2,1)} %shard_map.126), channel_id=1, replica_groups=mesh['depth'=4,'z'=16,'xlo'=2,'xhi'=2,'core'=2] {'z'}, dimensions={0} | all-to-all | bytes 655360 | tf_op jit(solution)/shard_map/all_to_all | solution.py:471
  141.9 1.6 %shard_map.127 = (f32[2,512]{1,0:T(2,128)}, f32[8,512]{1,0:T(8,128)}, f32[8,5,128]{2,1,0:T(8,128)}) custom-call(bf16[16,80,128]{2,1,0:T(8,128)(2,1)} %all_to_all.20.recv_ref), custom_call_target="tpu_custom_call" | custom-call | flops 100000000 | bytes 1000000 | tf_op jit(solution)/shard_map/pallas_call | solution.py:369
  143.6 1.4 copy.34
  (31 shorter events, 0.3 us)
Async XLA Ops:
  0.6 9.3 %copy-start = (bf16[512,8]{0,1:T(8,128)(2,1)S(1)}, bf16[512,8]{0,1:T(8,128)(2,1)}, u32[]{:S(2)}) copy-start(bf16[512,8]{0,1:T(8,128)(2,1)} %param.17) | copy-start | bytes 24580
  1.4 32.0 %collective-permute-start.1 = (bf16[2,512]{1,0:T(2,128)(2,1)S(1)}, bf16[2,512]{1,0:T(2,128)(2,1)S(1)}, u32[]{:S(2)}, u32[]{:S(2)}) collective-permute-start(bf16[2,512]{1,0:T(2,128)(2,1)S(1)} %get-tuple-element.42), channel_id=1, source_target_pairs={{0,4},{4,8},{8,12},{12,16},{16,20},{20,24},{24,28},{28,32},{32,36}... | collective-permute-start | bytes 6152 | tf_op jit(solution)/shard_map/ppermute | solution.py:408
  4.8 28.6 %collective-permute-start = (bf16[2,512]{1,0:T(2,128)(2,1)S(1)}, bf16[2,512]{1,0:T(2,128)(2,1)S(1)}, u32[]{:S(2)}, u32[]{:S(2)}) collective-permute-start(bf16[2,512]{1,0:T(2,128)(2,1)S(1)} %get-tuple-element.43), channel_id=1, source_target_pairs={{4,0},{8,4},{12,8},{16,12},{20,16},{24,20},{28,24},{32,28},{36,32}... | collective-permute-start | bytes 6152 | tf_op jit(solution)/shard_map/ppermute | solution.py:409
  11.9 1.6 %copy-start.2 = (bf16[1,64,32,512]{3,2,1,0:T(8,128)(2,1)S(1)}, bf16[1,64,32,512]{3,2,1,0:T(8,128)(2,1)}, u32[]{:S(2)}) copy-start(bf16[1,64,32,512]{3,2,1,0:T(8,128)(2,1)} %param.10) | copy-start | bytes 6291460
  13.5 1.2 copy-start.3
  22.4 2.0 %copy-start.4 = (bf16[2048,1024]{1,0:T(8,128)(2,1)}, bf16[2048,1024]{1,0:T(8,128)(2,1)S(1)}, u32[]{:S(2)}) copy-start(bf16[2048,1024]{1,0:T(8,128)(2,1)S(1)} %get-tuple-element.21.values_ref) | copy-start | bytes 12582916
  24.4 2.0 %copy-start.6 = (bf16[2048,1024]{1,0:T(8,128)(2,1)}, bf16[2048,1024]{1,0:T(8,128)(2,1)S(1)}, u32[]{:S(2)}) copy-start(bf16[2048,1024]{1,0:T(8,128)(2,1)S(1)} %get-tuple-element.20.slope_ref) | copy-start | bytes 12582916
  26.4 10.8 %all-to-all-start = ((bf16[4,64,384]{2,1,0:T(8,128)(2,1)}), bf16[4,64,384]{2,1,0:T(8,128)(2,1)S(1)}, u32[]{:S(2)}, u32[]{:S(2)}) async-start(bf16[4,64,384]{2,1,0:T(8,128)(2,1)} %get-tuple-element.16), calls=%async_computation | async-start | bytes 393216 | tf_op jit(solution)/shard_map/all_to_all | solution.py:424
  30.8 2.5 %copy-start.9 = (bf16[1,64,512]{2,1,0:T(8,128)(2,1)S(1)}, bf16[1,64,512]{2,1,0:T(8,128)(2,1)}, u32[]{:S(2)}) copy-start(bf16[1,64,512]{2,1,0:T(8,128)(2,1)} %param.19) | copy-start | bytes 196612
  37.2 0.7 copy-start.10
  39.9 9.7 %all-to-all-start.1 = ((bf16[4,64,384]{2,1,0:T(8,128)(2,1)}), bf16[4,64,384]{2,1,0:T(8,128)(2,1)S(1)}, u32[]{:S(2)}, u32[]{:S(2)}) async-start(bf16[4,64,384]{2,1,0:T(8,128)(2,1)} %get-tuple-element.17), calls=%async_computation.1 | async-start | bytes 393216 | tf_op jit(solution)/shard_map/all_to_all | solution.py:431
  49.6 2.2 %copy-start.5 = (bf16[2048,1024]{1,0:T(8,128)(2,1)S(1)}, bf16[2048,1024]{1,0:T(8,128)(2,1)}, u32[]{:S(2)}) copy-start(bf16[2048,1024]{1,0:T(8,128)(2,1)} %copy-done.4) | copy-start | bytes 12582916
  51.7 2.2 %copy-start.7 = (bf16[2048,1024]{1,0:T(8,128)(2,1)S(1)}, bf16[2048,1024]{1,0:T(8,128)(2,1)}, u32[]{:S(2)}) copy-start(bf16[2048,1024]{1,0:T(8,128)(2,1)} %copy-done.6) | copy-start | bytes 12582916
  53.9 14.9 %copy-start.12 = (bf16[2,64,128]{2,1,0:T(8,128)(2,1)S(1)}, bf16[2,64,128]{2,1,0:T(8,128)(2,1)}, u32[]{:S(2)}) copy-start(bf16[2,64,128]{2,1,0:T(8,128)(2,1)} %get-tuple-element.25) | copy-start | bytes 98308
  63.4 0.8 copy-start.1
  64.2 7.2 %collective-permute-start.2 = (bf16[17,128,128]{2,1,0:T(8,128)(2,1)S(1)}, bf16[17,128,128]{2,1,0:T(8,128)(2,1)S(1)}, u32[]{:S(2)}, u32[]{:S(2)}) collective-permute-start(bf16[17,128,128]{2,1,0:T(8,128)(2,1)S(1)} %get-tuple-element.24), channel_id=1, source_target_pairs={{0,1},{1,0},{2,3},{3,2},{4,5},{5,4},{6,7},{7,6},{8,9},{9,8},{10,11... | collective-permute-start | bytes 1671176 | tf_op jit(solution)/shard_map/ppermute | solution.py:381
  66.4 13.0 %collective-permute-start.6 = (bf16[68,2,128]{2,0,1:T(8,128)(2,1)S(1)}, bf16[68,2,128]{2,0,1:T(8,128)(2,1)S(1)}, u32[]{:S(2)}, u32[]{:S(2)}) collective-permute-start(bf16[68,2,128]{2,0,1:T(8,128)(2,1)S(1)} %bitcast.51), channel_id=1, source_target_pairs={{0,1},{1,0},{2,3},{3,2},{4,5},{5,4},{6,7},{7,6},{8,9},{9,8},{10,11... | collective-permute-start | bytes 104456 | tf_op jit(solution)/shard_map/ppermute | solution.py:381
  68.9 15.9 %collective-permute-start.3 = (bf16[64,128]{1,0:T(8,128)(2,1)S(1)}, bf16[64,128]{1,0:T(8,128)(2,1)S(1)}, u32[]{:S(2)}, u32[]{:S(2)}) collective-permute-start(bf16[64,128]{1,0:T(8,128)(2,1)S(1)} %get-tuple-element.45), channel_id=1, source_target_pairs={{0,4},{4,0},{1,5},{5,1},{2,6},{6,2},{3,7},{7,3},{8,12},{12,8},{9,1... | collective-permute-start | bytes 49160 | tf_op jit(solution)/shard_map/ppermute | solution.py:381
  71.4 0.8 copy-start.11
  74.4 29.4 %all-to-all-start.2 = ((bf16[16,160,128]{2,1,0:T(8,128)(2,1)}), bf16[16,160,128]{2,1,0:T(8,128)(2,1)S(1)}, u32[]{:S(2)}, u32[]{:S(2)}) async-start(bf16[16,160,128]{2,1,0:T(8,128)(2,1)} %shard_map.124), calls=%async_computation.2 | async-start | bytes 1310720 | tf_op jit(solution)/shard_map/all_to_all | solution.py:440
  79.4 11.4 %collective-permute-start.7 = (bf16[2,68,128]{2,1,0:T(8,128)(2,1)S(1)}, bf16[2,68,128]{2,1,0:T(8,128)(2,1)S(1)}, u32[]{:S(2)}, u32[]{:S(2)}) collective-permute-start(bf16[2,68,128]{2,1,0:T(8,128)(2,1)S(1)} %get-tuple-element.39), channel_id=1, source_target_pairs={{0,2},{2,0},{1,3},{3,1},{4,6},{6,4},{5,7},{7,5},{8,10},{10,8},{9,1... | collective-permute-start | bytes 104456 | tf_op jit(solution)/shard_map/ppermute | solution.py:381
  84.8 8.6 %collective-permute-start.4 = (bf16[2,64,128]{2,1,0:T(8,128)(2,1)S(1)}, bf16[2,64,128]{2,1,0:T(8,128)(2,1)S(1)}, u32[]{:S(2)}, u32[]{:S(2)}) collective-permute-start(bf16[2,64,128]{2,1,0:T(8,128)(2,1)S(1)} %pad_maximum_fusion.6), channel_id=1, source_target_pairs={{0,1},{1,0},{2,3},{3,2},{4,5},{5,4},{6,7},{7,6},{8,9},{9,8},{10,11... | collective-permute-start | bytes 98312 | tf_op jit(solution)/shard_map/ppermute | solution.py:381
  90.9 6.5 %collective-permute-start.8 = (bf16[4,68,128]{2,1,0:T(8,128)(2,1)S(1)}, bf16[4,68,128]{2,1,0:T(8,128)(2,1)S(1)}, u32[]{:S(2)}, u32[]{:S(2)}) collective-permute-start(bf16[4,68,128]{2,1,0:T(8,128)(2,1)S(1)} %bitcast.44), channel_id=1, source_target_pairs={{0,4},{4,0},{1,5},{5,1},{2,6},{6,2},{3,7},{7,3},{8,12},{12,8},{9,1... | collective-permute-start | bytes 208904 | tf_op jit(solution)/shard_map/ppermute | solution.py:381
  93.4 7.7 %collective-permute-start.5 = (bf16[4,64,128]{2,1,0:T(8,128)(2,1)S(1)}, bf16[4,64,128]{2,1,0:T(8,128)(2,1)S(1)}, u32[]{:S(2)}, u32[]{:S(2)}) collective-permute-start(bf16[4,64,128]{2,1,0:T(8,128)(2,1)S(1)} %pad_maximum_fusion.5), channel_id=1, source_target_pairs={{0,2},{2,0},{1,3},{3,1},{4,6},{6,4},{5,7},{7,5},{8,10},{10,8},{9,1... | collective-permute-start | bytes 196616 | tf_op jit(solution)/shard_map/ppermute | solution.py:381
  103.8 0.8 copy-start.8

commit v2 on v1

v2 whole, which is shorter than its diff:
```python
import jax
import jax.numpy as jnp
from jax import lax
from jax.experimental import pallas as pl
from jax.experimental.pallas import tpu as pltpu
from jax.sharding import Mesh, PartitionSpec as P

AXES = ("depth", "z", "xlo", "xhi", "core")
SEQ = ("z", "xlo")
F32 = jnp.float32
BF16 = jnp.bfloat16
I32 = jnp.int32

TILE = 16
LANES = 128
HEADS = 8
WIDTH = 128
OWN = 2
OWN_UNITS = OWN * WIDTH
UNITS = HEADS * WIDTH
RIM = 80
N_DEPTH = 4
N_Z = 16
PLANE = 16


def iota(shape, dim):
    return lax.broadcasted_iota(I32, shape, dim)


def dot(a, b, ca=1, cb=0):
    return lax.dot_general(a, b, (((ca,), (cb,)), ((), ())), preferred_element_type=F32)


def split_pair(value):
    high = value.astype(BF16).astype(F32)
    return high, value - high


def encode_kernel(
    depth_ref,
    feat_hbm,
    value_hbm,
    base_codes_ref,
    qual_codes_ref,
    count_ref,
    base_ref,
    qual_ref,
    score_ref,
    bulk_out,
    weights_out,
    top_out,
    send_out,
    feat_buf,
    value_buf,
    bulk,
    in_sems,
    out_sems,
):
    positions, reads, channels = feat_buf.shape
    tiles = positions // TILE
    rows = TILE * reads
    copies, stores = [], []
    for i in range(tiles):
        span = pl.ds(i * TILE, TILE)
        copies.append(pltpu.make_async_copy(feat_hbm.at[span], feat_buf.at[span], in_sems.at[i]))
        span = pl.ds(i * rows, rows)
        stores.append(pltpu.make_async_copy(bulk.at[span], bulk_out.at[span], out_sems.at[i]))
    copies.append(pltpu.make_async_copy(value_hbm, value_buf, in_sems.at[tiles]))
    for i in (0, tiles) + tuple(range(1, tiles)):
        copies[i].start()
    n_qual, n_base = qual_ref.shape[0], base_ref.shape[0]
    place = (iota((LANES, n_qual), 0) == iota((LANES, n_qual), 1)).astype(BF16)
    table = dot(place, qual_ref[...])
    place = (iota((LANES, n_base), 0) == iota((LANES, n_base), 1) + 96).astype(BF16)
    table = (table + dot(place, base_ref[...])).astype(BF16)
    slot = iota((LANES, HEADS), 0)
    place = (slot % HEADS == iota((LANES, HEADS), 1)) & (slot < 4 * HEADS)
    score_weight = dot(place.astype(BF16), score_ref[...]).astype(BF16)
    ones = jnp.ones((positions, LANES), BF16)
    spreads = []
    for part in range(N_DEPTH):
        lanes = iota((LANES, OWN_UNITS), 0)
        head = iota((LANES, OWN_UNITS), 1) // WIDTH + part * OWN
        spreads.append(((lanes == head) | (lanes == head + HEADS)).astype(BF16))
    base_codes = base_codes_ref[...].astype(F32)
    qual_codes = qual_codes_ref[...].astype(F32)
    counts = count_ref[...].astype(F32)
    lane = iota((rows, LANES), 1).astype(F32)
    for i in range(tiles):
        span = slice(i * TILE, (i + 1) * TILE)
        row_span = slice(i * rows, (i + 1) * rows)
        shape = (TILE, reads, positions)
        at = iota(shape, 2) == iota(shape, 0) + i * TILE
        base = jnp.where(at, base_codes[None], 0.0).reshape(rows, positions).astype(BF16)
        qual = jnp.where(at, qual_codes[None], 0.0).reshape(rows, positions).astype(BF16)
        shape = (TILE, positions)
        at = iota(shape, 1) == iota(shape, 0) + i * TILE
        count = dot(jnp.where(at, counts, 0.0).astype(BF16), ones)
        hot = (dot(qual, ones) == lane) | (dot(base, ones) + 96.0 == lane)
        embed = dot(hot.astype(BF16), table)
        copies[i].wait()
        features = feat_buf[span].reshape(rows, channels).astype(F32) + embed
        features = features.astype(BF16)
        bulk[row_span, 2 * UNITS :] = features
        scores = dot(features, score_weight, 1, 1).reshape(TILE, reads, LANES)
        read = iota((TILE, reads, LANES), 1) + depth_ref[0] * reads
        live = read < count.astype(I32)[:, None, :]
        top = jnp.max(jnp.where(live, scores, -1e30), axis=1)
        top_high, top_rest = split_pair(top)
        top_low = top_rest.astype(BF16).astype(F32)
        top = top_high + top_low
        weights = jnp.where(live, jnp.exp(scores - top[:, None, :]), 0.0)
        total_high, total_low = split_pair(jnp.sum(weights, axis=1))
        small = iota((TILE, LANES), 1)
        stat = jnp.where(
            small < 8,
            top_high,
            jnp.where(small < 16, top_low, jnp.where(small < 24, total_high, total_low)),
        ).astype(BF16)
        top_out[span, :] = top
        weights = weights.reshape(rows, LANES)
        weights_out[row_span, :] = weights
        high, low = split_pair(weights)
        pair = jnp.where(iota((rows, LANES), 1) < HEADS, high, low).astype(BF16)
        if i == 0:
            copies[tiles].wait()
        for part in range(N_DEPTH):
            cols = slice(part * OWN_UNITS, (part + 1) * OWN_UNITS)
            preact = dot(features, value_buf[cols, :], 1, 1).astype(BF16)
            spread = dot(pair, spreads[part]).astype(BF16)
            sigma = 0.5 * jnp.tanh(0.5 * preact) + 0.5
            values = preact * sigma
            slope = sigma + values * (1.0 - sigma)
            bulk[row_span, cols] = spread * slope
            bulk[row_span, UNITS + part * OWN_UNITS : UNITS + (part + 1) * OWN_UNITS] = values
            pool = (spread * values).astype(F32).reshape(TILE, reads, OWN_UNITS)
            send_out[part, span, 0:OWN_UNITS] = jnp.sum(pool, axis=1).astype(BF16)
            send_out[part, span, OWN_UNITS:] = stat
        stores[i].start()
    for store in stores:
        store.wait()


VMEM = pl.BlockSpec(memory_space=pltpu.VMEM)
SMEM = pl.BlockSpec(memory_space=pltpu.SMEM)
HBM = pl.BlockSpec(memory_space=pltpu.HBM)
ANY = pl.BlockSpec(memory_space=pl.ANY)


def in_hbm(*arrays):
    return [pltpu.with_memory_space_constraint(array, pltpu.HBM) for array in arrays]


def encode(depth_index, feats, value_weight, *rest):
    positions, reads, channels = feats.shape
    rows = positions * reads
    width = 2 * UNITS + channels
    return pl.pallas_call(
        encode_kernel,
        in_specs=[SMEM, HBM, HBM] + [VMEM] * 6,
        out_specs=[HBM] + [VMEM] * 3,
        out_shape=[
            pltpu.HBM((rows, width), BF16),
            jax.ShapeDtypeStruct((rows, LANES), F32),
            jax.ShapeDtypeStruct((positions, LANES), F32),
            jax.ShapeDtypeStruct((N_DEPTH, positions, OWN_UNITS + LANES), BF16),
        ],
        scratch_shapes=[
            pltpu.VMEM(feats.shape, BF16),
            pltpu.VMEM(value_weight.shape, BF16),
            pltpu.VMEM((rows, width), BF16),
            pltpu.SemaphoreType.DMA((positions // TILE + 1,)),
            pltpu.SemaphoreType.DMA((positions // TILE,)),
        ],
        compiler_params=pltpu.CompilerParams(vmem_limit_bytes=36 * 2**20),
        cost_estimate=pl.CostEstimate(
            flops=2 * rows * UNITS * (channels + 256),
            bytes_accessed=16 * 2**20,
            transcendentals=rows * UNITS,
        ),
    )(depth_index, *in_hbm(feats, value_weight, *rest))


def rim_kernel(low_ref, local_ref, high_ref, weight_ref, grad_out, cols_out):
    positions, outs = local_ref.shape
    taps = weight_ref.shape[0]
    half = taps // 2
    rows = cols_out.shape[1]
    rim = jnp.concatenate(
        [
            low_ref[...].astype(F32),
            local_ref[...].astype(F32),
            high_ref[...].astype(F32),
            jnp.zeros((rows - positions - 2 * half, outs), F32),
        ],
        axis=0,
    ).astype(BF16)
    grad = jnp.zeros((positions, OWN_UNITS), F32)
    for k in range(taps):
        first = 2 * half - k
        grad += dot(rim, weight_ref[k], 1, 1)[first : first + positions]
    grad_out[...] = grad.astype(BF16)
    for i in range(cols_out.shape[0]):
        cols_out[i] = rim[:, i * 128 : (i + 1) * 128]


def combine_kernel(depth_ref, recv_ref, grad_ref, cols_ref, payload_out, gather_out):
    positions = grad_ref.shape[0]
    own = depth_ref[0] * OWN
    lane = iota((LANES, OWN_UNITS), 0)
    head = iota((LANES, OWN_UNITS), 1) // WIDTH + own
    spread_top = ((lane == head) | (lane == head + 8)).astype(BF16)
    spread_total = ((lane == head + 16) | (lane == head + 24)).astype(BF16)
    stats = [recv_ref[d, :, OWN_UNITS:] for d in range(N_DEPTH)]
    tops = [dot(stat, spread_top) for stat in stats]
    top = jnp.maximum(jnp.maximum(tops[0], tops[1]), jnp.maximum(tops[2], tops[3]))
    total = jnp.zeros_like(top)
    pooled = jnp.zeros_like(top)
    for d in range(N_DEPTH):
        scale = jnp.exp(tops[d] - top)
        total += scale * dot(stats[d], spread_total)
        pooled += scale * recv_ref[d, :, 0:OWN_UNITS].astype(F32)
    pooled = pooled / total
    grad = grad_ref[...]
    product = grad.astype(F32) * pooled
    row = iota((OWN_UNITS, OWN_UNITS), 0)
    column = iota((OWN_UNITS, OWN_UNITS), 1)
    source = ((column % 128) // 8) * 16 + (column // 128) * 8 + column % 8
    ordered = dot(pooled.astype(BF16), (row == source).astype(BF16))
    ordered = ordered.astype(BF16)
    for peer in range(8):
        xlo = peer // 4
        gather_out[peer, 0:positions, :] = ordered[:, xlo * 128 : (xlo + 1) * 128]
        gather_out[peer, positions:, :] = cols_ref[peer % 4]
    lane = iota((positions, LANES), 1)
    stat = jnp.zeros((positions, LANES), F32)
    for i in range(OWN):
        span = slice(i * WIDTH, (i + 1) * WIDTH)
        row_total = jnp.sum(product[:, span], axis=1, keepdims=True)
        terms = (top[:, span], total[:, span], jnp.broadcast_to(row_total, (positions, WIDTH)))
        for k, term in enumerate(terms):
            high, low = split_pair(term)
            stat = jnp.where(lane == 4 * k + i, high, stat)
            stat = jnp.where(lane == 4 * k + 2 + i, low, stat)
    stat = stat.astype(BF16)
    for d in range(N_DEPTH):
        payload_out[d, :, 0:OWN_UNITS] = grad
        payload_out[d, :, OWN_UNITS:] = stat


def gradient_kernel(
    core_ref,
    payload_ref,
    top_ref,
    weights_ref,
    bulk_hbm,
    mine_out,
    theirs_out,
    total,
    slope_buf,
    values_buf,
    features_buf,
    sems,
):
    positions = top_ref.shape[0]
    rows, channels = features_buf.shape
    reads = rows // positions
    copies = [
        pltpu.make_async_copy(bulk_hbm.at[:, pl.ds(2 * UNITS, channels)], features_buf, sems.at[0])
    ]
    for d in range(N_DEPTH):
        for k, buf in enumerate((slope_buf, values_buf)):
            cols = pl.ds(k * UNITS + d * OWN_UNITS, OWN_UNITS)
            copies.append(
                pltpu.make_async_copy(bulk_hbm.at[:, cols], buf.at[d], sems.at[1 + 2 * d + k])
            )
    for i in [1, 0] + list(range(2, len(copies))):
        copies[i].start()
    lane = iota((LANES, LANES), 0)
    target = iota((LANES, LANES), 1)
    joint = [jnp.zeros((positions, LANES), F32) for _ in range(3)]
    for d in range(N_DEPTH):
        stat = payload_ref[d, :, OWN_UNITS:]
        for k in range(3):
            first = (lane // 4 == k) & (target < 2 * HEADS)
            pick = first & (lane % 2 + 2 * d == target % HEADS)
            joint[k] += dot(stat, pick.astype(BF16))
    small = iota((positions, LANES), 1)
    scale = jnp.where(
        small < 2 * HEADS,
        jnp.exp(top_ref[...] - joint[0]) / jnp.where(small < 2 * HEADS, joint[1], 1.0),
        0.0,
    )
    high, low = split_pair(scale)
    pair = jnp.where(small < HEADS, high, low).astype(BF16)
    first = core_ref[0] == 0

    def by_read(block):
        shape = (positions, 16, OWN_UNITS)
        return jnp.broadcast_to(block[:, None, :], shape).astype(BF16)[:, None]

    split = (positions, reads // 16, 16, OWN_UNITS)
    prob_grad = jnp.zeros((rows, LANES), F32)
    for d in range(N_DEPTH):
        cols = slice(d * OWN_UNITS, (d + 1) * OWN_UNITS)
        lanes = iota((LANES, OWN_UNITS), 0)
        head = iota((LANES, OWN_UNITS), 1) // WIDTH + d * OWN
        spread = ((lanes == head) | (lanes == head + HEADS)).astype(BF16)
        grad = payload_ref[d, :, 0:OWN_UNITS].astype(F32)
        scaled = by_read(grad * dot(pair, spread))
        copies[1 + 2 * d].wait()
        value_grad = (slope_buf[d].reshape(split) * scaled).reshape(rows, OWN_UNITS)
        if d == 0:
            copies[0].wait()
        term = dot(value_grad, features_buf[...], 0, 0)
        for q in range(4):
            total[q, cols, :] = term[:, q * 128 : (q + 1) * 128]
        copies[2 + 2 * d].wait()
        product = (values_buf[d].reshape(split) * by_read(grad)).reshape(rows, OWN_UNITS)
        prob_grad += dot(product, spread, 1, 1)
        for peer in range(4 * d, 4 * d + 4):
            base = d * OWN_UNITS + (peer % 4) * 4
            for q in range(4):
                for t in range(2):
                    zero = total[q, pl.ds(base + t, N_Z, stride=16), :]
                    one = total[q, pl.ds(base + 2 + t, N_Z, stride=16), :]
                    span = slice(q * 32 + t * 16, q * 32 + t * 16 + 16)
                    mine_out[peer, span, :] = jnp.where(first, zero, one).astype(BF16)
                    theirs_out[peer, span, :] = jnp.where(first, one, zero).astype(BF16)
    weights = weights_ref[...].reshape(positions, reads, LANES)
    prob_grad = prob_grad.reshape(positions, reads, LANES)
    score_grad = weights * scale[:, None, :] * (prob_grad - joint[2][:, None, :])
    score_grad = score_grad.reshape(rows, LANES).astype(BF16)
    score = dot(score_grad, features_buf[...], 0, 0)[0:HEADS]
    score = [score[:, q * 128 : (q + 1) * 128] for q in range(4)]
    score = jnp.concatenate(score + [jnp.zeros((96, 128), F32)], axis=0).astype(BF16)
    mine_out[PLANE] = score
    theirs_out[PLANE] = score


def gradients(core_index, payload, top, weights, bulk, channels):
    rows = bulk.shape[0]
    shape = (PLANE + 1, 128, 128)
    return pl.pallas_call(
        gradient_kernel,
        in_specs=[SMEM] + [VMEM] * 3 + [HBM],
        out_specs=[VMEM, VMEM],
        out_shape=[jax.ShapeDtypeStruct(shape, BF16)] * 2,
        scratch_shapes=[
            pltpu.VMEM((4, UNITS, 128), F32),
            pltpu.VMEM((N_DEPTH, rows, OWN_UNITS), BF16),
            pltpu.VMEM((N_DEPTH, rows, OWN_UNITS), BF16),
            pltpu.VMEM((rows, channels), BF16),
            pltpu.SemaphoreType.DMA((1 + 2 * N_DEPTH,)),
        ],
        compiler_params=pltpu.CompilerParams(vmem_limit_bytes=36 * 2**20),
        cost_estimate=pl.CostEstimate(
            flops=2 * rows * UNITS * (channels + 256),
            bytes_accessed=16 * 2**20,
            transcendentals=10**4,
        ),
    )(core_index, payload, top, weights, *in_hbm(bulk))


def pair_kernel(mine_ref, theirs_ref, send_out):
    score = mine_ref[PLANE, 0:32, :].astype(F32) + theirs_ref[PLANE, 0:32, :].astype(F32)
    score = score.astype(BF16)
    for peer in range(PLANE):
        value = mine_ref[peer].astype(F32) + theirs_ref[peer].astype(F32)
        send_out[peer, 0:128, :] = value.astype(BF16)
        send_out[peer, 128:160, :] = score


def conv_kernel(recv_ref, part_out):
    peers = recv_ref.shape[0]
    positions = recv_ref.shape[1] - RIM
    taps = part_out.shape[1] // 8
    half = taps // 2
    left = recv_ref[:, 0:positions, :].reshape(peers * positions, 128)
    grads = [recv_ref[j, positions:, :].astype(F32) for j in range(peers)]
    for k in range(taps):
        first = 2 * half - k
        shifted = jnp.concatenate([grad[first : first + positions] for grad in grads], axis=0)
        part = dot(left, shifted.astype(BF16), 0, 0)
        part_out[:, k * 8 : (k + 1) * 8, :] = part.reshape(N_Z, 8, 128)


def line_kernel(recv_ref, conv_ref, send_out, total):
    value = recv_ref[0].astype(F32)
    for peer in range(1, PLANE):
        value += recv_ref[peer].astype(F32)
    total[...] = value
    score = value[128:160]
    for z in range(N_Z):
        block = jnp.concatenate([total[pl.ds(z, 8, stride=16), :], score, conv_ref[z]], axis=0)
        send_out[z] = block.astype(BF16)


def last_kernel(recv_ref, value_out, score_out, conv_out):
    value = recv_ref[0].astype(F32)
    for z in range(1, N_Z):
        value += recv_ref[z].astype(F32)
    for q in range(4):
        span = slice(q * 128, (q + 1) * 128)
        value_out[:, span] = value[2 * q : 2 * q + 2]
        score_out[:, span] = value[8 + 8 * q : 16 + 8 * q]
    for k in range(conv_out.shape[0]):
        conv_out[k] = value[40 + 8 * k : 48 + 8 * k]


def small_call(kernel, shapes, *operands, specs=None, scratch=(), mib=6):
    single = not isinstance(shapes, list)
    return pl.pallas_call(
        kernel,
        in_specs=specs or [VMEM] * len(operands),
        out_specs=VMEM if single else [VMEM] * len(shapes),
        out_shape=shapes,
        scratch_shapes=list(scratch),
        compiler_params=pltpu.CompilerParams(vmem_limit_bytes=mib * 2**20),
        cost_estimate=pl.CostEstimate(flops=10**8, bytes_accessed=10**6, transcendentals=0),
    )(*operands)


def exchange(block, axis):
    return lax.ppermute(block, axis, [(0, 1), (1, 0)])


def body(
    read_feats,
    base_codes,
    qual_codes,
    depth_counts,
    base_table,
    qual_table,
    value_weight,
    score_weight,
    conv_weight,
    cotangent,
):
    _, positions, reads, channels = read_feats.shape
    block_units, taps, outs = conv_weight.shape
    half = taps // 2
    depth_index = lax.axis_index("depth")
    core_index = lax.axis_index("core")
    def shaped(*shape, kind=BF16):
        return jax.ShapeDtypeStruct(shape, kind)

    count = lax.axis_size(SEQ)
    forward = [(i, i + 1) for i in range(count - 1)]
    grad_local = cotangent[0]
    low = lax.ppermute(grad_local[-half:], SEQ, forward)
    high = lax.ppermute(grad_local[:half], SEQ, [(b, a) for a, b in forward])

    bulk, weights, top, pool_send = encode(
        depth_index.reshape(1),
        read_feats[0],
        value_weight,
        base_codes[0].T,
        qual_codes[0].T,
        depth_counts,
        base_table,
        qual_table,
        score_weight.T,
    )
    pool_recv = lax.all_to_all(pool_send, "depth", split_axis=0, concat_axis=0, tiled=True)

    block_grad, cols = small_call(
        rim_kernel,
        [shaped(positions, block_units), shaped(4, RIM, 128)],
        low,
        grad_local,
        high,
        conv_weight.transpose(1, 0, 2),
    )
    payload, gather_send = small_call(
        combine_kernel,
        [shaped(*pool_send.shape), shaped(8, positions + RIM, 128)],
        depth_index.reshape(1),
        pool_recv,
        block_grad,
        cols,
        specs=[SMEM] + [VMEM] * 3,
    )
    payload = lax.all_to_all(payload, "depth", split_axis=0, concat_axis=0, tiled=True)

    payload, gather_send = lax.optimization_barrier((payload, gather_send))
    gather_recv = lax.all_to_all(
        gather_send, ("xlo", "xhi", "core"), split_axis=0, concat_axis=0, tiled=True
    )

    mine, theirs = gradients(core_index.reshape(1), payload, top, weights, bulk, channels)
    theirs = exchange(theirs, "core")
    plane_send = small_call(pair_kernel, shaped(PLANE, 160, 128), mine, theirs)
    plane_recv = lax.all_to_all(
        plane_send, ("depth", "xlo", "xhi"), split_axis=0, concat_axis=0, tiled=True
    )
    conv_part = small_call(conv_kernel, shaped(N_Z, 8 * taps, 128, kind=F32), gather_recv)

    line_send = small_call(
        line_kernel,
        shaped(N_Z, 40 + 8 * taps, 128),
        plane_recv,
        conv_part,
        scratch=[pltpu.VMEM((160, 128), F32)],
    )
    line_recv = lax.all_to_all(line_send, "z", split_axis=0, concat_axis=0, tiled=True)
    value_weight_grad, score_weight_grad, conv_weight_grad = small_call(
        last_kernel,
        [
            shaped(2, channels, kind=F32),
            shaped(HEADS, channels, kind=F32),
            shaped(taps, 8, 128, kind=F32),
        ],
        line_recv,
    )
    return (value_weight_grad, score_weight_grad.T, conv_weight_grad.transpose(1, 0, 2))


def solution(mesh):
    fine = Mesh(mesh.devices.reshape(N_DEPTH, N_Z, 2, 2, 2), AXES)
    rep = ("xhi", "core")
    placed = (
        P(rep, SEQ, "depth", None),
        P(rep, SEQ, "depth"),
        P(rep, SEQ, "depth"),
        P(rep, SEQ),
        P(),
        P(),
        P(),
        P(),
        P("depth", None, None),
        P(rep, SEQ, None),
    )
    return jax.shard_map(
        body,
        mesh=fine,
        in_specs=placed,
        out_specs=(P(AXES, None), P(), P(("depth",) + SEQ, None, rep)),
        check_vma=False,
    )
```

time: 146 us -> 114 us (0.78)
  the two profiles are of different devices: /device:TPU:32 before, /device:TPU:64 now
where the time goes in v2:
time: 114 us; the launch traced here: 113 us
  blocking collectives  35.3 us (31%)
  waiting for transfers between devices  28.1 us (25%)
  starting transfers between devices  24.7 us (22%)
  Pallas kernels  24.2 us (21%)
    all_to_all x1, blocking collectives, body(): lax.all_to_all(line_send, 'z', split_axis=0, concat_axis=0, tiled=True)  35.3 us
    all_to_all x1, waiting for transfers between devices, body(): lax.all_to_all(plane_send, ('depth', 'xlo', 'xhi'), split_axis=0, concat_...  11.7 us
    pallas_call x1, Pallas kernels, encode(): pl.pallas_call(encode_kernel, in_specs=[SMEM, HBM, HBM] + [VMEM] * 6, out...  11.3 us
    pallas_call x1, Pallas kernels, gradients(): pl.pallas_call(gradient_kernel, in_specs=[SMEM] + [VMEM] * 3 + [HBM], out...  9.09 us
    all_to_all x1, waiting for transfers between devices, body(): lax.all_to_all(gather_send, ('xlo', 'xhi', 'core'), split_axis=0, concat_...  6.63 us
    all_to_all x1, waiting for transfers between devices, body(): lax.all_to_all(payload, 'depth', split_axis=0, concat_axis=0, tiled=True)  6.33 us
    all_to_all x1, starting transfers between devices, body(): lax.all_to_all(payload, 'depth', split_axis=0, concat_axis=0, tiled=True)  4.8 us
    all_to_all x1, starting transfers between devices, body(): lax.all_to_all(pool_send, 'depth', split_axis=0, concat_axis=0, tiled=True)  4.48 us
  transfers between devices with their start and end apart: 7, of which 4 were waited for; matrix products, arithmetic and copies ran while one was open for 0% of the time, Pallas kernels for 2%

profile of v2, /device:TPU:64, one launch (start us, length us, event | category | flops | bytes accessed | tf_op | source)
XLA Modules:
  0.0 113.1 jit_solution(12186590477172099052)
XLA Ops:
  0.6 0.0 copy-start.1
  0.7 0.0 copy-start
  0.7 11.3 %shard_map.121 = (bf16[2048,2560]{1,0:T(8,128)(2,1)}, f32[2048,128]{1,0:T(8,128)S(1)}, f32[64,128]{1,0:T(8,128)S(1)}, bf16[4,64,384]{2,1,0:T(8,128)(2,1)}) custom-call(s32[1]{0:T(128)} %bitcast.1.depth_ref, bf16[64,32,512]{2,1,0:T(8,128)(2,1)} %bitcast.20, bf16[1024,512]{1,0:T(8,128)(2,1)} %value_hbm.1, s32[32,64]{1,0:T(8,128)} %bitcast.21, ...), custom_call_target="tpu_custom_call" | custom-call | flops 3221225472 | bytes 16777216 | tf_op jit(solution)/shard_map/pallas_call | solution.py:159
  12.0 4.5 %all-to-all-start = ((bf16[4,64,384]{2,1,0:T(8,128)(2,1)}), bf16[4,64,384]{2,1,0:T(8,128)(2,1)S(1)}, u32[]{:S(2)}, u32[]{:S(2)}) async-start(bf16[4,64,384]{2,1,0:T(8,128)(2,1)} %get-tuple-element.18), calls=%async_computation | async-start | bytes 393216 | tf_op jit(solution)/shard_map/all_to_all | solution.py:466
  16.4 0.0 copy-done.1
  16.4 2.9 %collective-permute-start.1 = (bf16[2,512]{1,0:T(2,128)(2,1)S(1)}, bf16[2,512]{1,0:T(2,128)(2,1)S(1)}, u32[]{:S(2)}, u32[]{:S(2)}) collective-permute-start(bf16[2,512]{1,0:T(2,128)(2,1)S(1)} %get-tuple-element.33), channel_id=1, source_target_pairs={{4,0},{8,4},{12,8},{16,12},{20,16},{24,20},{28,24},{32,28},{36,32}... | collective-permute-start | bytes 6152 | tf_op jit(solution)/shard_map/ppermute | solution.py:453
  19.4 2.9 %collective-permute-start = (bf16[2,512]{1,0:T(2,128)(2,1)S(1)}, bf16[2,512]{1,0:T(2,128)(2,1)S(1)}, u32[]{:S(2)}, u32[]{:S(2)}) collective-permute-start(bf16[2,512]{1,0:T(2,128)(2,1)S(1)} %get-tuple-element.34), channel_id=1, source_target_pairs={{0,4},{4,8},{8,12},{12,16},{16,20},{20,24},{24,28},{28,32},{32,36}... | collective-permute-start | bytes 6152 | tf_op jit(solution)/shard_map/ppermute | solution.py:452
  22.3 0.0 collective-permute-done.1.high_ref
  22.3 3.5 %collective-permute-done.low_ref = bf16[2,512]{1,0:T(2,128)(2,1)S(1)} collective-permute-done((bf16[2,512]{1,0:T(2,128)(2,1)S(1)}, bf16[2,512]{1,0:T(2,128)(2,1)S(1)}, u32[]{:S(2)}, u32[]{:S(2)}) %collective-permute-start) | collective-permute-done | bytes 2080 | tf_op jit(solution)/shard_map/ppermute | solution.py:452
  25.8 0.0 copy-done
  25.8 0.5 shard_map.122
  26.3 0.0 all-to-all-done.recv_ref
  26.3 1.2 %shard_map.123 = (bf16[4,64,384]{2,1,0:T(8,128)(2,1)}, bf16[8,144,128]{2,1,0:T(8,128)(2,1)}) custom-call(s32[1]{0:T(128)} %bitcast.1.depth_ref, bf16[4,64,384]{2,1,0:T(8,128)(2,1)S(1)} %all-to-all-done.recv_ref, bf16[64,256]{1,0:T(8,128)(2,1)S(1)} %get-tuple-element.19.grad_ref, bf16[4,80,128]{2,1,0:T(8,128)(2,1)S(1)} %get-tuple-element.20.cols_ref), custom_call_target="tpu_custom_call" | custom-call | flops 100000000 | bytes 1000000 | tf_op jit(solution)/shard_map/pallas_call | solution.py:414
  27.5 4.8 %all-to-all-start.1 = ((bf16[4,64,384]{2,1,0:T(8,128)(2,1)}), bf16[4,64,384]{2,1,0:T(8,128)(2,1)S(1)}, u32[]{:S(2)}, u32[]{:S(2)}) async-start(bf16[4,64,384]{2,1,0:T(8,128)(2,1)} %get-tuple-element.21), calls=%async_computation.1 | async-start | bytes 393216 | tf_op jit(solution)/shard_map/all_to_all | solution.py:485
  32.3 6.3 %all-to-all-done.1.payload_ref = bf16[4,64,384]{2,1,0:T(8,128)(2,1)S(1)} async-done(((bf16[4,64,384]{2,1,0:T(8,128)(2,1)}), bf16[4,64,384]{2,1,0:T(8,128)(2,1)S(1)}, u32[]{:S(2)}, u32[]{:S(2)}) %all-to-all-start.1) | async-done | bytes 196640 | tf_op jit(solution)/shard_map/all_to_all | solution.py:485
  38.6 9.1 %shard_map.124 = (bf16[17,128,128]{2,1,0:T(8,128)(2,1)S(1)}, bf16[17,128,128]{2,1,0:T(8,128)(2,1)S(1)}) custom-call(s32[1]{0:T(128)} %bitcast.core_ref, bf16[4,64,384]{2,1,0:T(8,128)(2,1)S(1)} %all-to-all-done.1.payload_ref, f32[64,128]{1,0:T(8,128)S(1)} %get-tuple-element.24.top_ref, f32[2048,128]{1,0:T(8,128)S(1)} %get-tuple-element.25.weights_ref, ...), custom_call_target="tpu_custom_call" | custom-call | flops 3221225472 | bytes 16777216 | tf_op jit(solution)/shard_map/pallas_call | solution.py:345
  47.7 1.9 %collective-permute-start.2 = (bf16[17,128,128]{2,1,0:T(8,128)(2,1)S(1)}, bf16[17,128,128]{2,1,0:T(8,128)(2,1)S(1)}, u32[]{:S(2)}, u32[]{:S(2)}) collective-permute-start(bf16[17,128,128]{2,1,0:T(8,128)(2,1)S(1)} %get-tuple-element.28), channel_id=1, source_target_pairs={{0,1},{1,0},{2,3},{3,2},{4,5},{5,4},{6,7},{7,6},{8,9},{9,8},{10,11... | collective-permute-start | bytes 1671176 | tf_op jit(solution)/shard_map/ppermute | solution.py:426
  49.6 4.1 %all-to-all-start.3 = ((bf16[8,144,128]{2,1,0:T(8,128)(2,1)}), bf16[8,144,128]{2,1,0:T(8,128)(2,1)S(1)}, u32[]{:S(2)}, u32[]{:S(2)}) async-start(bf16[8,144,128]{2,1,0:T(8,128)(2,1)} %get-tuple-element.29), calls=%async_computation.3 | async-start | bytes 589824 | tf_op jit(solution)/shard_map/all_to_all | solution.py:488
  53.7 0.0 collective-permute-done.2.theirs_ref
  53.7 1.0 shard_map.125
  54.7 6.6 %all-to-all-done.3.recv_ref = bf16[8,144,128]{2,1,0:T(8,128)(2,1)S(1)} async-done(((bf16[8,144,128]{2,1,0:T(8,128)(2,1)}), bf16[8,144,128]{2,1,0:T(8,128)(2,1)S(1)}, u32[]{:S(2)}, u32[]{:S(2)}) %all-to-all-start.3) | async-done | bytes 294944 | tf_op jit(solution)/shard_map/all_to_all | solution.py:488
  61.3 3.6 %all-to-all-start.2 = ((bf16[16,160,128]{2,1,0:T(8,128)(2,1)}), bf16[16,160,128]{2,1,0:T(8,128)(2,1)S(1)}, u32[]{:S(2)}, u32[]{:S(2)}) async-start(bf16[16,160,128]{2,1,0:T(8,128)(2,1)} %shard_map.125), calls=%async_computation.2 | async-start | bytes 1310720 | tf_op jit(solution)/shard_map/all_to_all | solution.py:495
  64.9 0.4 shard_map.126.conv_ref
  65.3 11.7 %all-to-all-done.2.recv_ref = bf16[16,160,128]{2,1,0:T(8,128)(2,1)S(1)} async-done(((bf16[16,160,128]{2,1,0:T(8,128)(2,1)}), bf16[16,160,128]{2,1,0:T(8,128)(2,1)S(1)}, u32[]{:S(2)}, u32[]{:S(2)}) %all-to-all-start.2) | async-done | bytes 655392 | tf_op jit(solution)/shard_map/all_to_all | solution.py:495
  77.0 0.1 shard_map.127
  77.1 35.3 %all_to_all.25.recv_ref = bf16[16,80,128]{2,1,0:T(8,128)(2,1)S(1)} all-to-all(bf16[16,80,128]{2,1,0:T(8,128)(2,1)S(1)} %shard_map.127), channel_id=1, replica_groups=mesh['depth'=4,'z'=16,'xlo'=2,'xhi'=2,'core'=2] {'z'}, dimensions={0} | all-to-all | bytes 655360 | tf_op jit(solution)/shard_map/all_to_all | solution.py:507
  112.4 0.7 shard_map.128
  (1 shorter events, 0.0 us)
Async XLA Ops:
  0.6 15.8 %copy-start.1 = (bf16[1,64,512]{2,1,0:T(8,128)(2,1)S(1)}, bf16[1,64,512]{2,1,0:T(8,128)(2,1)}, u32[]{:S(2)}) copy-start(bf16[1,64,512]{2,1,0:T(8,128)(2,1)} %param.19) | copy-start | bytes 196612
  0.7 25.1 %copy-start = (bf16[256,5,512]{2,0,1:T(8,128)(2,1)S(1)}, bf16[256,5,512]{2,0,1:T(8,128)(2,1)}, u32[]{:S(2)}) copy-start(bf16[256,5,512]{2,0,1:T(8,128)(2,1)} %param.18) | copy-start | bytes 3932164
  12.0 14.4 %all-to-all-start = ((bf16[4,64,384]{2,1,0:T(8,128)(2,1)}), bf16[4,64,384]{2,1,0:T(8,128)(2,1)S(1)}, u32[]{:S(2)}, u32[]{:S(2)}) async-start(bf16[4,64,384]{2,1,0:T(8,128)(2,1)} %get-tuple-element.18), calls=%async_computation | async-start | bytes 393216 | tf_op jit(solution)/shard_map/all_to_all | solution.py:466
  16.4 5.9 %collective-permute-start.1 = (bf16[2,512]{1,0:T(2,128)(2,1)S(1)}, bf16[2,512]{1,0:T(2,128)(2,1)S(1)}, u32[]{:S(2)}, u32[]{:S(2)}) collective-permute-start(bf16[2,512]{1,0:T(2,128)(2,1)S(1)} %get-tuple-element.33), channel_id=1, source_target_pairs={{4,0},{8,4},{12,8},{16,12},{20,16},{24,20},{28,24},{32,28},{36,32}... | collective-permute-start | bytes 6152 | tf_op jit(solution)/shard_map/ppermute | solution.py:453
  19.4 6.4 %collective-permute-start = (bf16[2,512]{1,0:T(2,128)(2,1)S(1)}, bf16[2,512]{1,0:T(2,128)(2,1)S(1)}, u32[]{:S(2)}, u32[]{:S(2)}) collective-permute-start(bf16[2,512]{1,0:T(2,128)(2,1)S(1)} %get-tuple-element.34), channel_id=1, source_target_pairs={{0,4},{4,8},{8,12},{12,16},{16,20},{20,24},{24,28},{28,32},{32,36}... | collective-permute-start | bytes 6152 | tf_op jit(solution)/shard_map/ppermute | solution.py:452
  27.5 11.1 %all-to-all-start.1 = ((bf16[4,64,384]{2,1,0:T(8,128)(2,1)}), bf16[4,64,384]{2,1,0:T(8,128)(2,1)S(1)}, u32[]{:S(2)}, u32[]{:S(2)}) async-start(bf16[4,64,384]{2,1,0:T(8,128)(2,1)} %get-tuple-element.21), calls=%async_computation.1 | async-start | bytes 393216 | tf_op jit(solution)/shard_map/all_to_all | solution.py:485
  47.7 6.0 %collective-permute-start.2 = (bf16[17,128,128]{2,1,0:T(8,128)(2,1)S(1)}, bf16[17,128,128]{2,1,0:T(8,128)(2,1)S(1)}, u32[]{:S(2)}, u32[]{:S(2)}) collective-permute-start(bf16[17,128,128]{2,1,0:T(8,128)(2,1)S(1)} %get-tuple-element.28), channel_id=1, source_target_pairs={{0,1},{1,0},{2,3},{3,2},{4,5},{5,4},{6,7},{7,6},{8,9},{9,8},{10,11... | collective-permute-start | bytes 1671176 | tf_op jit(solution)/shard_map/ppermute | solution.py:426
  49.6 11.7 %all-to-all-start.3 = ((bf16[8,144,128]{2,1,0:T(8,128)(2,1)}), bf16[8,144,128]{2,1,0:T(8,128)(2,1)S(1)}, u32[]{:S(2)}, u32[]{:S(2)}) async-start(bf16[8,144,128]{2,1,0:T(8,128)(2,1)} %get-tuple-element.29), calls=%async_computation.3 | async-start | bytes 589824 | tf_op jit(solution)/shard_map/all_to_all | solution.py:488
  61.3 15.6 %all-to-all-start.2 = ((bf16[16,160,128]{2,1,0:T(8,128)(2,1)}), bf16[16,160,128]{2,1,0:T(8,128)(2,1)S(1)}, u32[]{:S(2)}, u32[]{:S(2)}) async-start(bf16[16,160,128]{2,1,0:T(8,128)(2,1)} %shard_map.125), calls=%async_computation.2 | async-start | bytes 1310720 | tf_op jit(solution)/shard_map/all_to_all | solution.py:495

commit v3 on v2

v3 whole, which is shorter than its diff:
```python
import jax
import jax.numpy as jnp
from jax import lax
from jax.experimental import pallas as pl
from jax.experimental.pallas import tpu as pltpu
from jax.sharding import Mesh, PartitionSpec as P

AXES = ("depth", "z", "xlo", "xhi", "core")
SEQ = ("z", "xlo")
F32 = jnp.float32
BF16 = jnp.bfloat16
I32 = jnp.int32

TILE = 16
LANES = 128
HEADS = 8
WIDTH = 128
OWN = 2
OWN_UNITS = OWN * WIDTH
UNITS = HEADS * WIDTH
RIM = 80
N_DEPTH = 4
N_Z = 16
PLANE = 16


def iota(shape, dim):
    return lax.broadcasted_iota(I32, shape, dim)


def dot(a, b, ca=1, cb=0):
    return lax.dot_general(a, b, (((ca,), (cb,)), ((), ())), preferred_element_type=F32)


def split_pair(value):
    high = value.astype(BF16).astype(F32)
    return high, value - high


def encode_kernel(
    depth_ref,
    count_ref,
    feat_hbm,
    value_hbm,
    base_codes_ref,
    qual_codes_ref,
    base_ref,
    qual_ref,
    score_ref,
    features_out,
    slope_out,
    values_out,
    pair_out,
    top_out,
    stat_out,
    pool_out,
    feat_buf,
    value_buf,
    features_buf,
    slope_buf,
    values_buf,
    hot_buf,
    embed_buf,
    score_buf,
    stat_buf,
    pair_buf,
    preact_buf,
    spread_buf,
    in_sems,
    out_sems,
):
    positions, reads, channels = feat_buf.shape
    tiles = positions // TILE
    rows = TILE * reads
    copies = []
    for i in range(tiles):
        span = pl.ds(i * TILE, TILE)
        copies.append(pltpu.make_async_copy(feat_hbm.at[span], feat_buf.at[span], in_sems.at[i]))
    copies.append(pltpu.make_async_copy(value_hbm, value_buf, in_sems.at[tiles]))
    for i in (0, tiles) + tuple(range(1, tiles)):
        copies[i].start()
    n_qual, n_base = qual_ref.shape[0], base_ref.shape[0]
    place = (iota((LANES, n_qual), 0) == iota((LANES, n_qual), 1)).astype(BF16)
    table = dot(place, qual_ref[...])
    place = (iota((LANES, n_base), 0) == iota((LANES, n_base), 1) + 96).astype(BF16)
    table = (table + dot(place, base_ref[...])).astype(BF16)
    slot = iota((LANES, HEADS), 0)
    place = (slot % HEADS == iota((LANES, HEADS), 1)) & (slot < 4 * HEADS)
    score_weight = dot(place.astype(BF16), score_ref[...]).astype(BF16)
    spreads = []
    for part in range(N_DEPTH):
        lanes = iota((LANES, OWN_UNITS), 0)
        head = iota((LANES, OWN_UNITS), 1) // WIDTH + part * OWN
        spreads.append(((lanes == head) | (lanes == head + HEADS)).astype(BF16))
    lane = iota((reads, LANES), 1)
    read = iota((reads, LANES), 0) + depth_ref[0] * reads
    for i in range(tiles):
        first_row = i * rows
        for p in range(TILE):
            at = i * TILE + p
            qual = jnp.broadcast_to(qual_codes_ref[:, at : at + 1], (reads, LANES))
            base = jnp.broadcast_to(base_codes_ref[:, at : at + 1], (reads, LANES))
            hot = (lane == qual) | (lane == base + 96)
            hot_buf[p * reads : (p + 1) * reads, :] = hot.astype(BF16)
        embed_buf[...] = dot(hot_buf[...], table)
        copies[i].wait()
        for p in range(TILE):
            near = slice(p * reads, (p + 1) * reads)
            feature = feat_buf[i * TILE + p].astype(F32) + embed_buf[near, :]
            far = slice(first_row + p * reads, first_row + (p + 1) * reads)
            features_buf[far, :] = feature.astype(BF16)
    stores = [pltpu.make_async_copy(features_buf, features_out, out_sems.at[0])]
    stores[0].start()
    features = features_buf[...]
    score_buf[...] = dot(features, score_weight, 1, 1)
    for p in range(positions):
        near = slice(p * reads, (p + 1) * reads)
        scores = score_buf[near, :]
        live = read < count_ref[p]
        top = jnp.max(jnp.where(live, scores, -1e30), axis=0, keepdims=True)
        top_high, top_rest = split_pair(top)
        top_low = top_rest.astype(BF16).astype(F32)
        top = top_high + top_low
        weights = jnp.where(live, jnp.exp(scores - top), 0.0)
        total_high, total_low = split_pair(jnp.sum(weights, axis=0, keepdims=True))
        small = lane[0:1]
        stat_buf[p : p + 1, :] = jnp.where(
            small < 8,
            top_high,
            jnp.where(small < 16, top_low, jnp.where(small < 24, total_high, total_low)),
        )
        top_out[p : p + 1, :] = top
        high, low = split_pair(weights)
        pair_buf[near, :] = jnp.where(lane < HEADS, high, low).astype(BF16)
    stores.append(pltpu.make_async_copy(pair_buf, pair_out, out_sems.at[1 + 2 * N_DEPTH]))
    stores[1].start()
    copies[tiles].wait()
    stat_out[...] = stat_buf[...].astype(BF16)

    def multiply(part):
        cols = slice(part * OWN_UNITS, (part + 1) * OWN_UNITS)
        preact_buf[part % 2] = dot(features, value_buf[cols, :], 1, 1)
        spread_buf[part % 2] = dot(pair_buf[...], spreads[part])

    multiply(0)
    for part in range(N_DEPTH):
        if part + 1 < N_DEPTH:
            multiply(part + 1)
        cols = slice(part * OWN_UNITS, (part + 1) * OWN_UNITS)
        for p in range(positions):
            near = slice(p * reads, (p + 1) * reads)
            preact = preact_buf[part % 2, near, :].astype(BF16)
            spread = spread_buf[part % 2, near, :].astype(BF16)
            sigma = 0.5 * jnp.tanh(0.5 * preact) + 0.5
            values = preact * sigma
            slope = sigma + values * (1.0 - sigma)
            slope_buf[part, near, :] = spread * slope
            values_buf[part, near, :] = values
            pool = jnp.sum((spread * values).astype(F32), axis=0, keepdims=True)
            pool_out[p : p + 1, cols] = pool
        for k, (buf, out) in enumerate(((slope_buf, slope_out), (values_buf, values_out))):
            store = pltpu.make_async_copy(buf.at[part], out.at[part], out_sems.at[1 + 2 * part + k])
            store.start()
            stores.append(store)
    for store in stores:
        store.wait()


VMEM = pl.BlockSpec(memory_space=pltpu.VMEM)
SMEM = pl.BlockSpec(memory_space=pltpu.SMEM)
HBM = pl.BlockSpec(memory_space=pltpu.HBM)
ANY = pl.BlockSpec(memory_space=pl.ANY)


def in_hbm(*arrays):
    return [pltpu.with_memory_space_constraint(array, pltpu.HBM) for array in arrays]


def encode(depth_index, counts, feats, value_weight, *rest):
    positions, reads, channels = feats.shape
    rows = positions * reads
    step = TILE * reads
    return pl.pallas_call(
        encode_kernel,
        in_specs=[SMEM, SMEM, HBM, HBM] + [VMEM] * 5,
        out_specs=[HBM] * 4 + [VMEM] * 3,
        out_shape=[
            pltpu.HBM((rows, channels), BF16),
            pltpu.HBM((N_DEPTH, rows, OWN_UNITS), BF16),
            pltpu.HBM((N_DEPTH, rows, OWN_UNITS), BF16),
            pltpu.HBM((rows, LANES), BF16),
            jax.ShapeDtypeStruct((positions, LANES), F32),
            jax.ShapeDtypeStruct((positions, LANES), BF16),
            jax.ShapeDtypeStruct((positions, UNITS), F32),
        ],
        scratch_shapes=[
            pltpu.VMEM(feats.shape, BF16),
            pltpu.VMEM(value_weight.shape, BF16),
            pltpu.VMEM((rows, channels), BF16),
            pltpu.VMEM((N_DEPTH, rows, OWN_UNITS), BF16),
            pltpu.VMEM((N_DEPTH, rows, OWN_UNITS), BF16),
            pltpu.VMEM((step, LANES), BF16),
            pltpu.VMEM((step, channels), F32),
            pltpu.VMEM((rows, LANES), F32),
            pltpu.VMEM((positions, LANES), F32),
            pltpu.VMEM((rows, LANES), BF16),
            pltpu.VMEM((2, rows, OWN_UNITS), F32),
            pltpu.VMEM((2, rows, OWN_UNITS), F32),
            pltpu.SemaphoreType.DMA((positions // TILE + 1,)),
            pltpu.SemaphoreType.DMA((2 + 2 * N_DEPTH,)),
        ],
        compiler_params=pltpu.CompilerParams(vmem_limit_bytes=36 * 2**20),
        cost_estimate=pl.CostEstimate(
            flops=2 * rows * UNITS * (channels + 256),
            bytes_accessed=16 * 2**20,
            transcendentals=rows * UNITS,
        ),
    )(depth_index, *in_hbm(counts, feats, value_weight, *rest))


def rim_kernel(low_ref, local_ref, high_ref, weight_ref, stat_ref, payload_out, cols_out):
    positions, outs = local_ref.shape
    taps = weight_ref.shape[0]
    half = taps // 2
    rows = cols_out.shape[1]
    low, high = low_ref[...].astype(F32), high_ref[...].astype(F32)
    local = local_ref[...].astype(F32)
    pad = jnp.zeros((rows - positions - 2 * half, outs), F32)
    rim = jnp.concatenate([low, local, high, pad], axis=0).astype(BF16)
    cols = jnp.concatenate([local, low, high, pad], axis=0).astype(BF16)
    grad = jnp.zeros((positions, OWN_UNITS), F32)
    for k in range(taps):
        first = 2 * half - k
        grad += dot(rim, weight_ref[k], 1, 1)[first : first + positions]
    for d in range(N_DEPTH):
        payload_out[d, :, 0:OWN_UNITS] = grad.astype(BF16)
        payload_out[d, :, OWN_UNITS:] = stat_ref[...]
    for i in range(cols_out.shape[0]):
        cols_out[i] = cols[:, i * 128 : (i + 1) * 128]


def joint_stats(payload_ref, top):
    positions = payload_ref.shape[1]
    lane = iota((LANES, LANES), 0)
    target = iota((LANES, LANES), 1)
    wanted = target < 2 * HEADS
    pick_top = (wanted & (lane < 16) & (lane % HEADS == target % HEADS)).astype(BF16)
    pick_total = wanted & (lane >= 16) & (lane < 32) & (lane % HEADS == target % HEADS)
    stats = [payload_ref[d, :, OWN_UNITS:] for d in range(N_DEPTH)]
    tops = [dot(stat, pick_top) for stat in stats]
    joint = jnp.maximum(jnp.maximum(tops[0], tops[1]), jnp.maximum(tops[2], tops[3]))
    total = jnp.zeros_like(joint)
    for d in range(N_DEPTH):
        total += jnp.exp(tops[d] - joint) * dot(stats[d], pick_total.astype(BF16))
    small = iota((positions, LANES), 1) < 2 * HEADS
    total = jnp.where(small, total, 1.0)
    return jnp.where(small, jnp.exp(jnp.where(small, top - joint, 0.0)) / total, 0.0)


def paired(value):
    high, low = split_pair(value)
    return jnp.where(iota(value.shape, 1) < HEADS, high, low).astype(BF16)


def spread_of(d):
    lanes = iota((LANES, OWN_UNITS), 0)
    head = iota((LANES, OWN_UNITS), 1) // WIDTH + d * OWN
    return ((lanes == head) | (lanes == head + HEADS)).astype(BF16)


def share_kernel(depth_ref, payload_ref, top_ref, pool_ref, cols_ref, send_out, scale_out):
    positions = top_ref.shape[0]
    quarter = positions // N_DEPTH
    scale = joint_stats(payload_ref, top_ref[...])
    scale_out[...] = scale
    pair = paired(scale)
    row = iota((OWN_UNITS, OWN_UNITS), 0)
    column = iota((OWN_UNITS, OWN_UNITS), 1)
    source = ((column % 128) // 8) * 16 + (column // 128) * 8 + column % 8
    order = (row == source).astype(BF16)
    lane = iota((positions, LANES), 1)
    totals = jnp.zeros((positions, LANES), F32)
    for d in range(N_DEPTH):
        part = pool_ref[:, d * OWN_UNITS : (d + 1) * OWN_UNITS] * dot(pair, spread_of(d))
        product = payload_ref[d, :, 0:OWN_UNITS].astype(F32) * part
        for i in range(OWN):
            span = slice(i * WIDTH, (i + 1) * WIDTH)
            total = jnp.sum(product[:, span], axis=1, keepdims=True)
            totals = jnp.where(lane == d * OWN + i, total, totals)
        part = dot(part.astype(BF16), order).astype(BF16)
        for peer in range(8):
            xlo = peer // 4
            send_out[8 * d + peer, 0:positions, :] = part[:, xlo * 128 : (xlo + 1) * 128]
    same = (iota((positions, LANES), 0) == iota((positions, LANES), 1)).astype(BF16)
    other = (iota((positions, LANES), 0) + positions == iota((positions, LANES), 1)).astype(BF16)
    high, low = split_pair(totals)
    turned = dot(high.astype(BF16), same, 0, 0) + dot(low.astype(BF16), other, 0, 0)
    extra = [turned[0:HEADS], None, jnp.zeros((4, LANES), F32)]
    own = pl.multiple_of(depth_ref[0] * quarter, quarter)
    for peer in range(4):
        rim = cols_ref[peer, positions : positions + 16, :].astype(F32)
        extra[1] = rim[0:4]
        rest = jnp.concatenate(extra, axis=0).astype(BF16)
        local = cols_ref[peer, pl.ds(own, quarter), :]
        for block in range(2 * N_DEPTH):
            index = 4 * block + peer
            send_out[index, positions : positions + quarter, :] = local
            send_out[index, positions + quarter :, :] = rest


def gradient_kernel(
    core_ref,
    payload_ref,
    scale_ref,
    features_hbm,
    slope_hbm,
    values_hbm,
    pair_hbm,
    mine_out,
    theirs_out,
    probs_hbm,
    total,
    slope_buf,
    values_buf,
    features_buf,
    grad_buf,
    scaled_buf,
    prob_buf,
    pair_buf,
    weights_buf,
    sems,
):
    positions = scale_ref.shape[0]
    rows = features_buf.shape[0]
    reads = rows // positions
    copies = [pltpu.make_async_copy(features_hbm, features_buf, sems.at[0])]
    for d in range(N_DEPTH):
        for k, (ref, buf) in enumerate(((slope_hbm, slope_buf), (values_hbm, values_buf))):
            copies.append(pltpu.make_async_copy(ref.at[d], buf.at[d], sems.at[1 + 2 * d + k]))
    copies.append(pltpu.make_async_copy(pair_hbm, pair_buf, sems.at[1 + 2 * N_DEPTH]))
    for i in [1, 0] + list(range(2, len(copies))):
        copies[i].start()
    pair = paired(scale_ref[...])
    first = core_ref[0] == 0

    def by_read(buf, p):
        shape = (16, OWN_UNITS)
        return jnp.broadcast_to(buf[p : p + 1, :], shape).astype(BF16)[None]

    split = (reads // 16, 16, OWN_UNITS)

    def multiply(buf, d, factor):
        for p in range(positions):
            span = slice(p * reads, (p + 1) * reads)
            term = buf[d, span, :].reshape(split) * by_read(factor, p)
            buf[d, span, :] = term.reshape(reads, OWN_UNITS)

    def set_factors(d):
        grad = payload_ref[d, :, 0:OWN_UNITS].astype(F32)
        grad_buf[d % 2] = grad
        scaled_buf[d % 2] = grad * dot(pair, spread_of(d))

    def pack(d):
        for peer in range(4 * d, 4 * d + 4):
            base = d * OWN_UNITS + (peer % 4) * 4
            for q in range(4):
                for t in range(2):
                    zero = total[q, pl.ds(base + t, N_Z, stride=16), :]
                    one = total[q, pl.ds(base + 2 + t, N_Z, stride=16), :]
                    span = slice(q * 32 + t * 16, q * 32 + t * 16 + 16)
                    mine_out[peer, span, :] = jnp.where(first, zero, one).astype(BF16)
                    theirs_out[peer, span, :] = jnp.where(first, one, zero).astype(BF16)

    set_factors(0)
    copies[1].wait()
    multiply(slope_buf, 0, scaled_buf.at[0])
    copies[0].wait()
    for d in range(N_DEPTH):
        cols = slice(d * OWN_UNITS, (d + 1) * OWN_UNITS)
        copies[2 + 2 * d].wait()
        if d + 1 < N_DEPTH:
            copies[3 + 2 * d].wait()
            set_factors(d + 1)
        term = dot(slope_buf[d], features_buf[...], 0, 0)
        for q in range(4):
            total[q, cols, :] = term[:, q * 128 : (q + 1) * 128]
        if d + 1 < N_DEPTH:
            multiply(slope_buf, d + 1, scaled_buf.at[(d + 1) % 2])
        multiply(values_buf, d, grad_buf.at[d % 2])
        if d:
            pack(d - 1)
        term = dot(values_buf[d], spread_of(d), 1, 1)
        if d == 0:
            prob_buf[...] = term
        else:
            prob_buf[...] += term
    copies[1 + 2 * N_DEPTH].wait()
    lane = iota((LANES, LANES), 0)
    target = iota((LANES, LANES), 1)
    both = (lane < 16) & (target < 16) & (lane % HEADS == target % HEADS)
    weights_buf[...] = dot(pair_buf[...], both.astype(BF16))
    lane = iota((reads, LANES), 1)
    for p in range(positions):
        span = slice(p * reads, (p + 1) * reads)
        probs = weights_buf[span, :] * scale_ref[p : p + 1, :]
        prob_buf[span, :] = jnp.where(lane < HEADS, probs * prob_buf[span, :], probs)
    store = pltpu.make_async_copy(prob_buf, probs_hbm, sems.at[2 + 2 * N_DEPTH])
    store.start()
    pack(N_DEPTH - 1)
    store.wait()


def gradients(core_index, payload, scale, features, *rest):
    rows, channels = features.shape
    positions = scale.shape[0]
    shape = (PLANE + 1, 128, 128)
    return pl.pallas_call(
        gradient_kernel,
        in_specs=[SMEM] + [VMEM] * 2 + [HBM] * 4,
        out_specs=[VMEM, VMEM, HBM],
        out_shape=[
            jax.ShapeDtypeStruct(shape, BF16),
            jax.ShapeDtypeStruct(shape, BF16),
            pltpu.HBM((rows, LANES), F32),
        ],
        scratch_shapes=[
            pltpu.VMEM((4, UNITS, 128), F32),
            pltpu.VMEM((N_DEPTH, rows, OWN_UNITS), BF16),
            pltpu.VMEM((N_DEPTH, rows, OWN_UNITS), BF16),
            pltpu.VMEM((rows, channels), BF16),
            pltpu.VMEM((2, positions, OWN_UNITS), F32),
            pltpu.VMEM((2, positions, OWN_UNITS), F32),
            pltpu.VMEM((rows, LANES), F32),
            pltpu.VMEM((rows, LANES), BF16),
            pltpu.VMEM((rows, LANES), F32),
            pltpu.SemaphoreType.DMA((3 + 2 * N_DEPTH,)),
        ],
        compiler_params=pltpu.CompilerParams(vmem_limit_bytes=36 * 2**20),
        cost_estimate=pl.CostEstimate(
            flops=2 * rows * UNITS * (channels + 256),
            bytes_accessed=16 * 2**20,
            transcendentals=10**4,
        ),
    )(core_index, payload, scale, *in_hbm(features, *rest))


def score_kernel(
    place_ref,
    recv_ref,
    probs_hbm,
    features_hbm,
    _held,
    theirs_out,
    score_out,
    slot,
    probs_buf,
    features_buf,
    score_buf,
    row_buf,
    sems,
):
    rows = probs_buf.shape[0]
    positions = recv_ref.shape[1] - 32
    reads = rows // positions
    load = [
        pltpu.make_async_copy(probs_hbm, probs_buf, sems.at[0]),
        pltpu.make_async_copy(features_hbm, features_buf, sems.at[1]),
    ]
    load[0].start()
    load[1].start()
    row = jnp.zeros((16, LANES), F32)
    for d in range(N_DEPTH):
        row += recv_ref[8 * d + place_ref[0], positions + 16 : positions + 32, :].astype(F32)
    high, low = split_pair(row)
    pick = iota((16, LANES), 0) == iota((16, LANES), 1)
    pick = (pick & (iota((16, LANES), 0) < HEADS)).astype(BF16)
    turned = dot(high.astype(BF16), pick, 0, 0) + dot(low.astype(BF16), pick, 0, 0)
    row_buf[...] = turned[0:positions] + turned[positions : 2 * positions]
    load[0].wait()
    for p in range(positions):
        span = slice(p * reads, (p + 1) * reads)
        term = probs_buf[span, :]
        probs = pltpu.roll(term, LANES - HEADS, 1)
        score_buf[span, :] = (term - probs * row_buf[p : p + 1, :]).astype(BF16)
    load[1].wait()
    score = dot(score_buf[...], features_buf[...], 0, 0)[0:HEADS]
    score = [score[:, q * 128 : (q + 1) * 128] for q in range(4)]
    score = jnp.concatenate(score + [jnp.zeros((96, 128), F32)], axis=0).astype(BF16)
    slot[...] = score
    score_out[...] = score
    copy = pltpu.make_async_copy(slot, theirs_out.at[PLANE], sems.at[2])
    copy.start()
    copy.wait()


def scores(place, recv, probs, features, theirs):
    rows, channels = features.shape
    positions = recv.shape[1] - 32
    return pl.pallas_call(
        score_kernel,
        in_specs=[SMEM, VMEM, HBM, HBM, ANY],
        out_specs=[ANY, VMEM],
        out_shape=[
            jax.ShapeDtypeStruct(theirs.shape, BF16),
            jax.ShapeDtypeStruct((128, 128), BF16),
        ],
        input_output_aliases={4: 0},
        scratch_shapes=[
            pltpu.VMEM((128, 128), BF16),
            pltpu.VMEM((rows, LANES), F32),
            pltpu.VMEM((rows, channels), BF16),
            pltpu.VMEM((rows, LANES), BF16),
            pltpu.VMEM((positions, LANES), F32),
            pltpu.SemaphoreType.DMA((3,)),
        ],
        compiler_params=pltpu.CompilerParams(vmem_limit_bytes=16 * 2**20),
        cost_estimate=pl.CostEstimate(flops=10**8, bytes_accessed=10**6, transcendentals=0),
    )(place, recv, *in_hbm(probs, features), theirs)


def pair_kernel(mine_ref, score_ref, theirs_ref, send_out):
    score = score_ref[0:32, :].astype(F32) + theirs_ref[PLANE, 0:32, :].astype(F32)
    score = score.astype(BF16)
    for peer in range(PLANE):
        value = mine_ref[peer].astype(F32) + theirs_ref[peer].astype(F32)
        send_out[peer, 0:128, :] = value.astype(BF16)
        send_out[peer, 128:160, :] = score


def conv_kernel(recv_ref, part_out):
    positions = recv_ref.shape[1] - 32
    taps = part_out.shape[1] // 8
    half = taps // 2
    left, grads = [], []
    for j in range(8):
        pooled = recv_ref[j, 0:positions, :].astype(F32)
        local = [recv_ref[j, positions : positions + 16, :]]
        for d in range(1, N_DEPTH):
            pooled += recv_ref[8 * d + j, 0:positions, :].astype(F32)
            local.append(recv_ref[8 * d + j, positions : positions + 16, :])
        left.append(pooled.astype(BF16))
        rest = recv_ref[j, positions + 16 : positions + 32, :].astype(F32)
        low, high = rest[8 : 8 + half], rest[8 + half : 8 + 2 * half]
        grads.append(jnp.concatenate([low] + [x.astype(F32) for x in local] + [high], axis=0))
    left = jnp.concatenate(left, axis=0)
    for k in range(taps):
        first = 2 * half - k
        shifted = jnp.concatenate([grad[first : first + positions] for grad in grads], axis=0)
        part = dot(left, shifted.astype(BF16), 0, 0)
        part_out[:, k * 8 : (k + 1) * 8, :] = part.reshape(N_Z, 8, 128)


def line_kernel(recv_ref, conv_ref, send_out, total):
    value = recv_ref[0].astype(F32)
    for peer in range(1, PLANE):
        value += recv_ref[peer].astype(F32)
    total[...] = value
    score = value[128:160]
    for z in range(N_Z):
        block = jnp.concatenate([total[pl.ds(z, 8, stride=16), :], score, conv_ref[z]], axis=0)
        send_out[z] = block.astype(BF16)


def last_kernel(recv_ref, value_out, score_out, conv_out):
    value = recv_ref[0].astype(F32)
    for z in range(1, N_Z):
        value += recv_ref[z].astype(F32)
    for q in range(4):
        span = slice(q * 128, (q + 1) * 128)
        value_out[:, span] = value[2 * q : 2 * q + 2]
        score_out[:, span] = value[8 + 8 * q : 16 + 8 * q]
    for k in range(conv_out.shape[0]):
        conv_out[k] = value[40 + 8 * k : 48 + 8 * k]


def small_call(kernel, shapes, *operands, specs=None, scratch=(), mib=6):
    single = not isinstance(shapes, list)
    return pl.pallas_call(
        kernel,
        in_specs=specs or [VMEM] * len(operands),
        out_specs=VMEM if single else [VMEM] * len(shapes),
        out_shape=shapes,
        scratch_shapes=list(scratch),
        compiler_params=pltpu.CompilerParams(vmem_limit_bytes=mib * 2**20),
        cost_estimate=pl.CostEstimate(flops=10**6, bytes_accessed=10**5, transcendentals=0),
    )(*operands)


def exchange(block, axis):
    return lax.ppermute(block, axis, [(0, 1), (1, 0)])


def body(
    read_feats,
    base_codes,
    qual_codes,
    depth_counts,
    base_table,
    qual_table,
    value_weight,
    score_weight,
    conv_weight,
    cotangent,
):
    _, positions, reads, channels = read_feats.shape
    block_units, taps, outs = conv_weight.shape
    half = taps // 2
    depth_index = lax.axis_index("depth")
    core_index = lax.axis_index("core")
    def shaped(*shape, kind=BF16):
        return jax.ShapeDtypeStruct(shape, kind)

    count = lax.axis_size(SEQ)
    forward = [(i, i + 1) for i in range(count - 1)]
    grad_local = cotangent[0]
    low = lax.ppermute(grad_local[-half:], SEQ, forward)
    high = lax.ppermute(grad_local[:half], SEQ, [(b, a) for a, b in forward])

    features, slope, values, pair, top, stat, pool = encode(
        depth_index.reshape(1),
        depth_counts[0],
        read_feats[0],
        value_weight,
        base_codes[0].T,
        qual_codes[0].T,
        base_table,
        qual_table,
        score_weight.T,
    )

    payload, cols = small_call(
        rim_kernel,
        [shaped(N_DEPTH, positions, OWN_UNITS + LANES), shaped(4, RIM, 128)],
        low,
        grad_local,
        high,
        conv_weight.transpose(1, 0, 2),
        stat,
    )
    payload = lax.all_to_all(payload, "depth", split_axis=0, concat_axis=0, tiled=True)

    send, scale = small_call(
        share_kernel,
        [
            shaped(8 * N_DEPTH, positions + 32, 128),
            shaped(positions, LANES, kind=F32),
        ],
        depth_index.reshape(1),
        payload,
        top,
        pool,
        cols,
        specs=[SMEM] + [VMEM] * 4,
    )
    recv = lax.all_to_all(
        send, ("depth", "xlo", "xhi", "core"), split_axis=0, concat_axis=0, tiled=True
    )

    mine, theirs, probs = gradients(
        core_index.reshape(1), payload, scale, features, slope, values, pair
    )
    place = lax.axis_index(("xlo", "xhi", "core")).reshape(1)
    theirs, score = scores(place, recv, probs, features, theirs)
    theirs = exchange(theirs, "core")
    plane_send = small_call(pair_kernel, shaped(PLANE, 160, 128), mine, score, theirs)
    plane_recv = lax.all_to_all(
        plane_send, ("depth", "xlo", "xhi"), split_axis=0, concat_axis=0, tiled=True
    )
    conv_part = small_call(conv_kernel, shaped(N_Z, 8 * taps, 128, kind=F32), recv)

    line_send = small_call(
        line_kernel,
        shaped(N_Z, 40 + 8 * taps, 128),
        plane_recv,
        conv_part,
        scratch=[pltpu.VMEM((160, 128), F32)],
    )
    line_recv = lax.all_to_all(line_send, "z", split_axis=0, concat_axis=0, tiled=True)
    value_weight_grad, score_weight_grad, conv_weight_grad = small_call(
        last_kernel,
        [
            shaped(2, channels, kind=F32),
            shaped(HEADS, channels, kind=F32),
            shaped(taps, 8, 128, kind=F32),
        ],
        line_recv,
    )
    return (value_weight_grad, score_weight_grad.T, conv_weight_grad.transpose(1, 0, 2))


def solution(mesh):
    fine = Mesh(mesh.devices.reshape(N_DEPTH, N_Z, 2, 2, 2), AXES)
    rep = ("xhi", "core")
    placed = (
        P(rep, SEQ, "depth", None),
        P(rep, SEQ, "depth"),
        P(rep, SEQ, "depth"),
        P(rep, SEQ),
        P(),
        P(),
        P(),
        P(),
        P("depth", None, None),
        P(rep, SEQ, None),
    )
    return jax.shard_map(
        body,
        mesh=fine,
        in_specs=placed,
        out_specs=(P(AXES, None), P(), P(("depth",) + SEQ, None, rep)),
        check_vma=False,
    )
```

time: 114 us -> 111 us (0.974)
  the two profiles are of different devices: /device:TPU:64 before, /device:TPU:2 now
where the time goes in v3:
time: 111 us
  blocking collectives  43.4 us (39%)
  Pallas kernels  27.4 us (25%)
  starting transfers between devices  22.8 us (21%)
  waiting for transfers between devices  15.4 us (14%)
    all_to_all x1, blocking collectives, body(): lax.all_to_all(line_send, 'z', split_axis=0, concat_axis=0, tiled=True)  34.8 us
    pallas_call x1, Pallas kernels, encode(): pl.pallas_call(encode_kernel, in_specs=[SMEM, SMEM, HBM, HBM] + [VMEM] *...  11.1 us
    all_to_all x1, waiting for transfers between devices, body(): lax.all_to_all(plane_send, ('depth', 'xlo', 'xhi'), split_axis=0, concat_...  10.4 us
    pallas_call x1, Pallas kernels, gradients(): pl.pallas_call(gradient_kernel, in_specs=[SMEM] + [VMEM] * 2 + [HBM] * 4,...  9.5 us
    all_to_all x1, blocking collectives, body(): lax.all_to_all(payload, 'depth', split_axis=0, concat_axis=0, tiled=True)  8.69 us
    ppermute x1, starting transfers between devices, body(): high = lax.ppermute(grad_local[:half], SEQ, [(b, a) for a, b in forward])  7.8 us
    all_to_all x1, starting transfers between devices, body(): lax.all_to_all(send, ('depth', 'xlo', 'xhi', 'core'), split_axis=0, conca...  5.6 us
    all_to_all x1, starting transfers between devices, body(): lax.all_to_all(plane_send, ('depth', 'xlo', 'xhi'), split_axis=0, concat_...  5.58 us
  transfers between devices with their start and end apart: 5, of which 3 were waited for; matrix products, arithmetic and copies ran while one was open for 0% of the time, Pallas kernels for 19%

profile of v3, /device:TPU:2, one launch (start us, length us, event | category | flops | bytes accessed | tf_op | source)
XLA Modules:
  0.0 110.6 jit_solution(9274424386538213602)
XLA Ops:
  0.6 0.7 slice_bitcast_fusion
  1.4 7.8 %collective-permute-start.1 = (bf16[2,512]{1,0:T(2,128)(2,1)S(1)}, bf16[2,512]{1,0:T(2,128)(2,1)S(1)}, u32[]{:S(2)}, u32[]{:S(2)}) collective-permute-start(bf16[2,512]{1,0:T(2,128)(2,1)S(1)} %get-tuple-element.41), channel_id=1, source_target_pairs={{4,0},{8,4},{12,8},{16,12},{20,16},{24,20},{28,24},{32,28},{36,32}... | collective-permute-start | bytes 6152 | tf_op jit(solution)/shard_map/ppermute | solution.py:617
  9.2 1.9 %collective-permute-start = (bf16[2,512]{1,0:T(2,128)(2,1)S(1)}, bf16[2,512]{1,0:T(2,128)(2,1)S(1)}, u32[]{:S(2)}, u32[]{:S(2)}) collective-permute-start(bf16[2,512]{1,0:T(2,128)(2,1)S(1)} %get-tuple-element.42), channel_id=1, source_target_pairs={{0,4},{4,8},{8,12},{12,16},{16,20},{20,24},{24,28},{28,32},{32,36}... | collective-permute-start | bytes 6152 | tf_op jit(solution)/shard_map/ppermute | solution.py:616
  11.1 0.0 copy-start
  11.1 0.0 copy-start.1
  11.1 11.1 %shard_map.121 = (bf16[2048,512]{1,0:T(8,128)(2,1)}, bf16[4,2048,256]{2,1,0:T(8,128)(2,1)}, bf16[4,2048,256]{2,1,0:T(8,128)(2,1)}, bf16[2048,128]{1,0:T(8,128)(2...) custom-call(s32[1]{0:T(128)} %bitcast.5.depth_ref, s32[64]{0:T(128)} %bitcast.28, ...), custom_call_target="tpu_custom_call" | custom-call | flops 3221225472 | bytes 16777216 | tf_op jit(solution)/shard_map/pallas_call | solution.py:183
  22.2 0.0 collective-permute-done.1.high_ref
  22.2 0.0 collective-permute-done.low_ref
  22.2 0.0 copy-done
  22.2 0.0 copy-done.1
  22.2 0.5 shard_map.122
  22.8 8.7 %all_to_all.20.payload_ref = bf16[4,64,384]{2,1,0:T(8,128)(2,1)S(1)} all-to-all(bf16[4,64,384]{2,1,0:T(8,128)(2,1)S(1)} %get-tuple-element.23), channel_id=1, replica_groups=mesh['depth'=4,'z'=16,'xlo'=2,'xhi'=2,'core'=2] {'depth'}, dimensions={0} | all-to-all | bytes 393216 | tf_op jit(solution)/shard_map/all_to_all | solution.py:640
  31.5 1.7 %shard_map.123 = (bf16[32,96,128]{2,1,0:T(8,128)(2,1)}, f32[64,128]{1,0:T(8,128)S(1)}) custom-call(s32[1]{0:T(128)} %bitcast.5.depth_ref, bf16[4,64,384]{2,1,0:T(8,128)(2,1)S(1)} %all_to_all.20.payload_ref, f32[64,128]{1,0:T(8,128)S(1)} %get-tuple-element.24.top_ref, f32[64,1024]{1,0:T(8,128)S(1)} %get-tuple-element.25.pool_ref, ...), custom_call_target="tpu_custom_call" | custom-call | flops 1000000 | bytes 100000 | tf_op jit(solution)/shard_map/pallas_call | solution.py:578
  33.1 5.6 %all-to-all-start.1 = ((bf16[32,96,128]{2,1,0:T(8,128)(2,1)}), bf16[32,96,128]{2,1,0:T(8,128)(2,1)S(1)}, u32[]{:S(2)}, u32[]{:S(2)}) async-start(bf16[32,96,128]{2,1,0:T(8,128)(2,1)} %get-tuple-element.33), calls=%async_computation.1 | async-start | bytes 1572864 | tf_op jit(solution)/shard_map/all_to_all | solution.py:655
  38.8 9.5 %shard_map.124 = (bf16[17,128,128]{2,1,0:T(8,128)(2,1)S(1)}, bf16[17,128,128]{2,1,0:T(8,128)(2,1)S(1)}, f32[2048,128]{1,0:T(8,128)}) custom-call(s32[1]{0:T(128)} %bitcast.core_ref, bf16[4,64,384]{2,1,0:T(8,128)(2,1)S(1)} %all_to_all.20.payload_ref, f32[64,128]{1,0:T(8,128)S(1)} %get-tuple-element.27.scale_ref, ...), custom_call_target="tpu_custom_call" | custom-call | flops 3221225472 | bytes 16777216 | tf_op jit(solution)/shard_map/pallas_call | solution.py:417
  48.3 3.1 %all-to-all-done.1.recv_ref = bf16[32,96,128]{2,1,0:T(8,128)(2,1)S(1)} async-done(((bf16[32,96,128]{2,1,0:T(8,128)(2,1)}), bf16[32,96,128]{2,1,0:T(8,128)(2,1)S(1)}, u32[]{:S(2)}, u32[]{:S(2)}) %all-to-all-start.1) | async-done | bytes 786464 | tf_op jit(solution)/shard_map/all_to_all | solution.py:655
  51.4 2.4 %shard_map.125 = (bf16[17,128,128]{2,1,0:T(8,128)(2,1)S(1)}, bf16[128,128]{1,0:T(8,128)(2,1)S(1)}) custom-call(s32[1]{0:T(128)} %bitcast.13.place_ref, bf16[32,96,128]{2,1,0:T(8,128)(2,1)S(1)} %all-to-all-done.1.recv_ref, f32[2048,128]{1,0:T(8,128)} %get-tuple-element.34.probs_hbm, ...), custom_call_target="tpu_custom_call", output_to_operand_aliasing={{0}: (4, {})} | custom-call | flops 100000000 | bytes 1000000 | tf_op jit(solution)/shard_map/pallas_call | solution.py:499
  53.8 1.9 %collective-permute-start.2 = (bf16[17,128,128]{2,1,0:T(8,128)(2,1)S(1)}, bf16[17,128,128]{2,1,0:T(8,128)(2,1)S(1)}, u32[]{:S(2)}, u32[]{:S(2)}) collective-permute-start(bf16[17,128,128]{2,1,0:T(8,128)(2,1)S(1)} %get-tuple-element.37), channel_id=1, source_target_pairs={{0,1},{1,0},{2,3},{3,2},{4,5},{5,4},{6,7},{7,6},{8,9},{9,8},{10,11... | collective-permute-start | bytes 1671176 | tf_op jit(solution)/shard_map/ppermute | solution.py:590
  55.8 1.9 %collective-permute-done.2.theirs_ref = bf16[17,128,128]{2,1,0:T(8,128)(2,1)S(1)} collective-permute-done((bf16[17,128,128]{2,1,0:T(8,128)(2,1)S(1)}, bf16[17,128,128]{2,1,0:T(8,128)(2,1)S(1)}, u32[]{:S(2)}, u32[]{:S(2)}) %collective-permute-start.2) | collective-permute-done | bytes 557088 | tf_op jit(solution)/shard_map/ppermute | solution.py:590
  57.7 1.0 shard_map.126
  58.6 5.6 %all-to-all-start.2 = ((bf16[16,160,128]{2,1,0:T(8,128)(2,1)}), bf16[16,160,128]{2,1,0:T(8,128)(2,1)S(1)}, u32[]{:S(2)}, u32[]{:S(2)}) async-start(bf16[16,160,128]{2,1,0:T(8,128)(2,1)} %shard_map.126), calls=%async_computation.2 | async-start | bytes 1310720 | tf_op jit(solution)/shard_map/all_to_all | solution.py:666
  64.2 0.4 shard_map.127.conv_ref
  64.7 10.4 %all-to-all-done.2.recv_ref = bf16[16,160,128]{2,1,0:T(8,128)(2,1)S(1)} async-done(((bf16[16,160,128]{2,1,0:T(8,128)(2,1)}), bf16[16,160,128]{2,1,0:T(8,128)(2,1)S(1)}, u32[]{:S(2)}, u32[]{:S(2)}) %all-to-all-start.2) | async-done | bytes 655392 | tf_op jit(solution)/shard_map/all_to_all | solution.py:666
  75.1 0.1 shard_map.128
  75.2 34.8 %all_to_all.21.recv_ref = bf16[16,80,128]{2,1,0:T(8,128)(2,1)S(1)} all-to-all(bf16[16,80,128]{2,1,0:T(8,128)(2,1)S(1)} %shard_map.128), channel_id=1, replica_groups=mesh['depth'=4,'z'=16,'xlo'=2,'xhi'=2,'core'=2] {'z'}, dimensions={0} | all-to-all | bytes 655360 | tf_op jit(solution)/shard_map/all_to_all | solution.py:678
  109.9 0.7 shard_map.129
Async XLA Ops:
  1.4 20.9 %collective-permute-start.1 = (bf16[2,512]{1,0:T(2,128)(2,1)S(1)}, bf16[2,512]{1,0:T(2,128)(2,1)S(1)}, u32[]{:S(2)}, u32[]{:S(2)}) collective-permute-start(bf16[2,512]{1,0:T(2,128)(2,1)S(1)} %get-tuple-element.41), channel_id=1, source_target_pairs={{4,0},{8,4},{12,8},{16,12},{20,16},{24,20},{28,24},{32,28},{36,32}... | collective-permute-start | bytes 6152 | tf_op jit(solution)/shard_map/ppermute | solution.py:617
  9.2 13.0 %collective-permute-start = (bf16[2,512]{1,0:T(2,128)(2,1)S(1)}, bf16[2,512]{1,0:T(2,128)(2,1)S(1)}, u32[]{:S(2)}, u32[]{:S(2)}) collective-permute-start(bf16[2,512]{1,0:T(2,128)(2,1)S(1)} %get-tuple-element.42), channel_id=1, source_target_pairs={{0,4},{4,8},{8,12},{12,16},{16,20},{20,24},{24,28},{28,32},{32,36}... | collective-permute-start | bytes 6152 | tf_op jit(solution)/shard_map/ppermute | solution.py:616
  11.1 11.1 %copy-start = (bf16[256,5,512]{2,0,1:T(8,128)(2,1)S(1)}, bf16[256,5,512]{2,0,1:T(8,128)(2,1)}, u32[]{:S(2)}) copy-start(bf16[256,5,512]{2,0,1:T(8,128)(2,1)} %param.18) | copy-start | bytes 3932164
  11.1 11.1 %copy-start.1 = (bf16[1,64,512]{2,1,0:T(8,128)(2,1)S(1)}, bf16[1,64,512]{2,1,0:T(8,128)(2,1)}, u32[]{:S(2)}) copy-start(bf16[1,64,512]{2,1,0:T(8,128)(2,1)} %param.19) | copy-start | bytes 196612
  33.1 18.2 %all-to-all-start.1 = ((bf16[32,96,128]{2,1,0:T(8,128)(2,1)}), bf16[32,96,128]{2,1,0:T(8,128)(2,1)S(1)}, u32[]{:S(2)}, u32[]{:S(2)}) async-start(bf16[32,96,128]{2,1,0:T(8,128)(2,1)} %get-tuple-element.33), calls=%async_computation.1 | async-start | bytes 1572864 | tf_op jit(solution)/shard_map/all_to_all | solution.py:655
  53.8 3.9 %collective-permute-start.2 = (bf16[17,128,128]{2,1,0:T(8,128)(2,1)S(1)}, bf16[17,128,128]{2,1,0:T(8,128)(2,1)S(1)}, u32[]{:S(2)}, u32[]{:S(2)}) collective-permute-start(bf16[17,128,128]{2,1,0:T(8,128)(2,1)S(1)} %get-tuple-element.37), channel_id=1, source_target_pairs={{0,1},{1,0},{2,3},{3,2},{4,5},{5,4},{6,7},{7,6},{8,9},{9,8},{10,11... | collective-permute-start | bytes 1671176 | tf_op jit(solution)/shard_map/ppermute | solution.py:590
  58.6 16.4 %all-to-all-start.2 = ((bf16[16,160,128]{2,1,0:T(8,128)(2,1)}), bf16[16,160,128]{2,1,0:T(8,128)(2,1)S(1)}, u32[]{:S(2)}, u32[]{:S(2)}) async-start(bf16[16,160,128]{2,1,0:T(8,128)(2,1)} %shard_map.126), calls=%async_computation.2 | async-start | bytes 1310720 | tf_op jit(solution)/shard_map/all_to_all | solution.py:666

commit v4 on v3

--- a/solution.py
+++ b/solution.py
@@ -41,32 +41,22 @@
     depth_ref,
     count_ref,
     feat_hbm,
-    value_hbm,
     base_codes_ref,
     qual_codes_ref,
     base_ref,
     qual_ref,
     score_ref,
     features_out,
-    slope_out,
-    values_out,
     pair_out,
     top_out,
     stat_out,
-    pool_out,
     feat_buf,
-    value_buf,
     features_buf,
-    slope_buf,
-    values_buf,
     hot_buf,
     embed_buf,
     score_buf,
     stat_buf,
-    pair_buf,
-    preact_buf,
-    spread_buf,
-    in_sems,
+    sems,
     out_sems,
 ):
     positions, reads, channels = feat_buf.shape
@@ -75,10 +65,9 @@
     copies = []
     for i in range(tiles):
         span = pl.ds(i * TILE, TILE)
-        copies.append(pltpu.make_async_copy(feat_hbm.at[span], feat_buf.at[span], in_sems.at[i]))
-    copies.append(pltpu.make_async_copy(value_hbm, value_buf, in_sems.at[tiles]))
-    for i in (0, tiles) + tuple(range(1, tiles)):
+        copies.append(pltpu.make_async_copy(feat_hbm.at[span], feat_buf.at[span], sems.at[i]))
         copies[i].start()
+    stores = []
     n_qual, n_base = qual_ref.shape[0], base_ref.shape[0]
     place = (iota((LANES, n_qual), 0) == iota((LANES, n_qual), 1)).astype(BF16)
     table = dot(place, qual_ref[...])
@@ -87,11 +76,6 @@
     slot = iota((LANES, HEADS), 0)
     place = (slot % HEADS == iota((LANES, HEADS), 1)) & (slot < 4 * HEADS)
     score_weight = dot(place.astype(BF16), score_ref[...]).astype(BF16)
-    spreads = []
-    for part in range(N_DEPTH):
-        lanes = iota((LANES, OWN_UNITS), 0)
-        head = iota((LANES, OWN_UNITS), 1) // WIDTH + part * OWN
-        spreads.append(((lanes == head) | (lanes == head + HEADS)).astype(BF16))
     lane = iota((reads, LANES), 1)
     read = iota((reads, LANES), 0) + depth_ref[0] * reads
     for i in range(tiles):
@@ -109,8 +93,11 @@
             feature = feat_buf[i * TILE + p].astype(F32) + embed_buf[near, :]
             far = slice(first_row + p * reads, first_row + (p + 1) * reads)
             features_buf[far, :] = feature.astype(BF16)
-    stores = [pltpu.make_async_copy(features_buf, features_out, out_sems.at[0])]
-    stores[0].start()
+        at = pl.ds(first_row, rows)
+        stores.append(
+            pltpu.make_async_copy(features_buf.at[at], features_out.at[at], out_sems.at[i])
+        )
+        stores[i].start()
     features = features_buf[...]
     score_buf[...] = dot(features, score_weight, 1, 1)
     for p in range(positions):
@@ -131,16 +118,48 @@
         )
         top_out[p : p + 1, :] = top
         high, low = split_pair(weights)
-        pair_buf[near, :] = jnp.where(lane < HEADS, high, low).astype(BF16)
-    stores.append(pltpu.make_async_copy(pair_buf, pair_out, out_sems.at[1 + 2 * N_DEPTH]))
-    stores[1].start()
-    copies[tiles].wait()
+        pair_out[near, :] = jnp.where(lane < HEADS, high, low).astype(BF16)
     stat_out[...] = stat_buf[...].astype(BF16)
+    for store in stores:
+        store.wait()
+
+
+def value_kernel(
+    pair_ref,
+    features_hbm,
+    value_hbm,
+    pair_out,
+    slope_out,
+    values_out,
+    pool_out,
+    features_buf,
+    value_buf,
+    slope_buf,
+    values_buf,
+    preact_buf,
+    spread_buf,
+    load_sems,
+    sems,
+):
+    positions = pool_out.shape[0]
+    reads = features_buf.shape[0] // positions
+    load = [
+        pltpu.make_async_copy(features_hbm, features_buf, load_sems.at[0]),
+        pltpu.make_async_copy(value_hbm, value_buf, load_sems.at[1]),
+    ]
+    for copy in load:
+        copy.start()
+    spread_buf[0] = dot(pair_ref[...], spread_of(0))
+    for copy in load:
+        copy.wait()
+    stores = [pltpu.make_async_copy(pair_ref, pair_out, sems.at[1])]
+    stores[0].start()
 
     def multiply(part):
         cols = slice(part * OWN_UNITS, (part + 1) * OWN_UNITS)
-        preact_buf[part % 2] = dot(features, value_buf[cols, :], 1, 1)
-        spread_buf[part % 2] = dot(pair_buf[...], spreads[part])
+        preact_buf[part % 2] = dot(features_buf[...], value_buf[cols, :], 1, 1)
+        if part:
+            spread_buf[part % 2] = dot(pair_ref[...], spread_of(part))
 
     multiply(0)
     for part in range(N_DEPTH):
@@ -158,10 +177,14 @@
             values_buf[part, near, :] = values
             pool = jnp.sum((spread * values).astype(F32), axis=0, keepdims=True)
             pool_out[p : p + 1, cols] = pool
-        for k, (buf, out) in enumerate(((slope_buf, slope_out), (values_buf, values_out))):
-            store = pltpu.make_async_copy(buf.at[part], out.at[part], out_sems.at[1 + 2 * part + k])
-            store.start()
-            stores.append(store)
+            if (p + 1) % (positions // 2) == 0:
+                side = (p + 1) // (positions // 2) - 1
+                at = pl.ds(side * (positions // 2) * reads, positions // 2 * reads)
+                pairs = ((slope_buf, slope_out), (values_buf, values_out))
+                for k, (buf, out) in enumerate(pairs):
+                    sem = sems.at[2 + 4 * part + 2 * side + k]
+                    stores.append(pltpu.make_async_copy(buf.at[part, at], out.at[part, at], sem))
+                    stores[-1].start()
     for store in stores:
         store.wait()
 
@@ -176,54 +199,75 @@
     return [pltpu.with_memory_space_constraint(array, pltpu.HBM) for array in arrays]
 
 
-def encode(depth_index, counts, feats, value_weight, *rest):
+def encode(depth_index, counts, feats, *rest):
     positions, reads, channels = feats.shape
     rows = positions * reads
     step = TILE * reads
     return pl.pallas_call(
         encode_kernel,
-        in_specs=[SMEM, SMEM, HBM, HBM] + [VMEM] * 5,
-        out_specs=[HBM] * 4 + [VMEM] * 3,
+        in_specs=[SMEM, SMEM, HBM] + [VMEM] * 5,
+        out_specs=[HBM] + [VMEM] * 3,
         out_shape=[
             pltpu.HBM((rows, channels), BF16),
-            pltpu.HBM((N_DEPTH, rows, OWN_UNITS), BF16),
-            pltpu.HBM((N_DEPTH, rows, OWN_UNITS), BF16),
-            pltpu.HBM((rows, LANES), BF16),
+            jax.ShapeDtypeStruct((rows, LANES), BF16),
             jax.ShapeDtypeStruct((positions, LANES), F32),
             jax.ShapeDtypeStruct((positions, LANES), BF16),
-            jax.ShapeDtypeStruct((positions, UNITS), F32),
         ],
         scratch_shapes=[
             pltpu.VMEM(feats.shape, BF16),
-            pltpu.VMEM(value_weight.shape, BF16),
             pltpu.VMEM((rows, channels), BF16),
-            pltpu.VMEM((N_DEPTH, rows, OWN_UNITS), BF16),
-            pltpu.VMEM((N_DEPTH, rows, OWN_UNITS), BF16),
             pltpu.VMEM((step, LANES), BF16),
             pltpu.VMEM((step, channels), F32),
             pltpu.VMEM((rows, LANES), F32),
             pltpu.VMEM((positions, LANES), F32),
-            pltpu.VMEM((rows, LANES), BF16),
+            pltpu.SemaphoreType.DMA((positions // TILE,)),
+            pltpu.SemaphoreType.DMA((positions // TILE,)),
+        ],
+        compiler_params=pltpu.CompilerParams(vmem_limit_bytes=20 * 2**20),
+        cost_estimate=pl.CostEstimate(
+            flops=2 * rows * channels * 256, bytes_accessed=4 * 2**20, transcendentals=rows * LANES
+        ),
+    )(depth_index, *in_hbm(counts, feats, *rest))
+
+
+def make_values(features, pair, value_weight, positions):
+    rows, channels = features.shape
+    return pl.pallas_call(
+        value_kernel,
+        in_specs=[VMEM, HBM, HBM],
+        out_specs=[HBM] * 3 + [VMEM],
+        out_shape=[
+            pltpu.HBM((rows, LANES), BF16),
+            pltpu.HBM((N_DEPTH, rows, OWN_UNITS), BF16),
+            pltpu.HBM((N_DEPTH, rows, OWN_UNITS), BF16),
+            jax.ShapeDtypeStruct((positions, UNITS), F32),
+        ],
+        scratch_shapes=[
+            pltpu.VMEM((rows, channels), BF16),
+            pltpu.VMEM(value_weight.shape, BF16),
+            pltpu.VMEM((N_DEPTH, rows, OWN_UNITS), BF16),
+            pltpu.VMEM((N_DEPTH, rows, OWN_UNITS), BF16),
             pltpu.VMEM((2, rows, OWN_UNITS), F32),
             pltpu.VMEM((2, rows, OWN_UNITS), F32),
-            pltpu.SemaphoreType.DMA((positions // TILE + 1,)),
-            pltpu.SemaphoreType.DMA((2 + 2 * N_DEPTH,)),
-        ],
-        compiler_params=pltpu.CompilerParams(vmem_limit_bytes=36 * 2**20),
+            pltpu.SemaphoreType.DMA((2,)),
+            pltpu.SemaphoreType.DMA((2 + 4 * N_DEPTH,)),
+        ],
+        compiler_params=pltpu.CompilerParams(vmem_limit_bytes=32 * 2**20),
         cost_estimate=pl.CostEstimate(
             flops=2 * rows * UNITS * (channels + 256),
             bytes_accessed=16 * 2**20,
             transcendentals=rows * UNITS,
         ),
-    )(depth_index, *in_hbm(counts, feats, value_weight, *rest))
-
-
-def rim_kernel(low_ref, local_ref, high_ref, weight_ref, stat_ref, payload_out, cols_out):
+    )(pair, *in_hbm(features, value_weight))
+
+
+def rim_kernel(before_ref, local_ref, after_ref, weight_ref, stat_ref, payload_out, cols_out):
     positions, outs = local_ref.shape
     taps = weight_ref.shape[0]
     half = taps // 2
     rows = cols_out.shape[1]
-    low, high = low_ref[...].astype(F32), high_ref[...].astype(F32)
+    low = before_ref[positions - 16 :, :].astype(F32)[16 - half :]
+    high = after_ref[0:16, :].astype(F32)[:half]
     local = local_ref[...].astype(F32)
     pad = jnp.zeros((rows - positions - 2 * half, outs), F32)
     rim = jnp.concatenate([low, local, high, pad], axis=0).astype(BF16)
@@ -413,7 +457,7 @@
 def gradients(core_index, payload, scale, features, *rest):
     rows, channels = features.shape
     positions = scale.shape[0]
-    shape = (PLANE + 1, 128, 128)
+    shape = (PLANE, 128, 128)
     return pl.pallas_call(
         gradient_kernel,
         in_specs=[SMEM] + [VMEM] * 2 + [HBM] * 4,
@@ -449,10 +493,7 @@
     recv_ref,
     probs_hbm,
     features_hbm,
-    _held,
-    theirs_out,
     score_out,
-    slot,
     probs_buf,
     features_buf,
     score_buf,
@@ -485,41 +526,31 @@
     load[1].wait()
     score = dot(score_buf[...], features_buf[...], 0, 0)[0:HEADS]
     score = [score[:, q * 128 : (q + 1) * 128] for q in range(4)]
-    score = jnp.concatenate(score + [jnp.zeros((96, 128), F32)], axis=0).astype(BF16)
-    slot[...] = score
-    score_out[...] = score
-    copy = pltpu.make_async_copy(slot, theirs_out.at[PLANE], sems.at[2])
-    copy.start()
-    copy.wait()
-
-
-def scores(place, recv, probs, features, theirs):
+    score_out[...] = jnp.concatenate(score, axis=0).astype(BF16)
+
+
+def scores(place, recv, probs, features):
     rows, channels = features.shape
     positions = recv.shape[1] - 32
     return pl.pallas_call(
         score_kernel,
-        in_specs=[SMEM, VMEM, HBM, HBM, ANY],
-        out_specs=[ANY, VMEM],
-        out_shape=[
-            jax.ShapeDtypeStruct(theirs.shape, BF16),
-            jax.ShapeDtypeStruct((128, 128), BF16),
-        ],
-        input_output_aliases={4: 0},
+        in_specs=[SMEM, VMEM, HBM, HBM],
+        out_specs=VMEM,
+        out_shape=jax.ShapeDtypeStruct((4 * HEADS, 128), BF16),
         scratch_shapes=[
-            pltpu.VMEM((128, 128), BF16),
             pltpu.VMEM((rows, LANES), F32),
             pltpu.VMEM((rows, channels), BF16),
             pltpu.VMEM((rows, LANES), BF16),
             pltpu.VMEM((positions, LANES), F32),
-            pltpu.SemaphoreType.DMA((3,)),
+            pltpu.SemaphoreType.DMA((2,)),
         ],
         compiler_params=pltpu.CompilerParams(vmem_limit_bytes=16 * 2**20),
         cost_estimate=pl.CostEstimate(flops=10**8, bytes_accessed=10**6, transcendentals=0),
-    )(place, recv, *in_hbm(probs, features), theirs)
-
-
-def pair_kernel(mine_ref, score_ref, theirs_ref, send_out):
-    score = score_ref[0:32, :].astype(F32) + theirs_ref[PLANE, 0:32, :].astype(F32)
+    )(place, recv, *in_hbm(probs, features))
+
+
+def pair_kernel(mine_ref, theirs_ref, score_ref, other_ref, send_out):
+    score = score_ref[...].astype(F32) + other_ref[...].astype(F32)
     score = score.astype(BF16)
     for peer in range(PLANE):
         value = mine_ref[peer].astype(F32) + theirs_ref[peer].astype(F32)
@@ -604,7 +635,6 @@
 ):
     _, positions, reads, channels = read_feats.shape
     block_units, taps, outs = conv_weight.shape
-    half = taps // 2
     depth_index = lax.axis_index("depth")
     core_index = lax.axis_index("core")
     def shaped(*shape, kind=BF16):
@@ -613,14 +643,13 @@
     count = lax.axis_size(SEQ)
     forward = [(i, i + 1) for i in range(count - 1)]
     grad_local = cotangent[0]
-    low = lax.ppermute(grad_local[-half:], SEQ, forward)
-    high = lax.ppermute(grad_local[:half], SEQ, [(b, a) for a, b in forward])
-
-    features, slope, values, pair, top, stat, pool = encode(
+    before = lax.ppermute(grad_local, SEQ, forward)
+    after = lax.ppermute(grad_local, SEQ, [(b, a) for a, b in forward])
+
+    features, pair, top, stat = encode(
         depth_index.reshape(1),
         depth_counts[0],
         read_feats[0],
-        value_weight,
         base_codes[0].T,
         qual_codes[0].T,
         base_table,
@@ -631,13 +660,15 @@
     payload, cols = small_call(
         rim_kernel,
         [shaped(N_DEPTH, positions, OWN_UNITS + LANES), shaped(4, RIM, 128)],
-        low,
+        before,
         grad_local,
-        high,
+        after,
         conv_weight.transpose(1, 0, 2),
         stat,
     )
     payload = lax.all_to_all(payload, "depth", split_axis=0, concat_axis=0, tiled=True)
+
+    pair, slope, values, pool = make_values(features, pair, value_weight, positions)
 
     send, scale = small_call(
         share_kernel,
@@ -660,9 +691,12 @@
         core_index.reshape(1), payload, scale, features, slope, values, pair
     )
     place = lax.axis_index(("xlo", "xhi", "core")).reshape(1)
-    theirs, score = scores(place, recv, probs, features, theirs)
     theirs = exchange(theirs, "core")
-    plane_send = small_call(pair_kernel, shaped(PLANE, 160, 128), mine, score, theirs)
+    score = scores(place, recv, probs, features)
+    other = exchange(score, "core")
+    plane_send = small_call(
+        pair_kernel, shaped(PLANE, 160, 128), mine, theirs, score, other
+    )
     plane_recv = lax.all_to_all(
         plane_send, ("depth", "xlo", "xhi"), split_axis=0, concat_axis=0, tiled=True
     )

time: 111 us -> 109 us (0.982)
  the two profiles are of different devices: /device:TPU:2 before, /device:TPU:32 now
where the time goes in v4:
time: 109 us
  blocking collectives  35.3 us (32%)
  Pallas kernels  29.8 us (27%)
  starting transfers between devices  25.9 us (24%)
  waiting for transfers between devices  16.9 us (16%)
    all_to_all x1, blocking collectives, body(): lax.all_to_all(line_send, 'z', split_axis=0, concat_axis=0, tiled=True)  35.3 us
    all_to_all x1, waiting for transfers between devices, body(): lax.all_to_all(plane_send, ('depth', 'xlo', 'xhi'), split_axis=0, concat_...  11.8 us
    pallas_call x1, Pallas kernels, gradients(): pl.pallas_call(gradient_kernel, in_specs=[SMEM] + [VMEM] * 2 + [HBM] * 4,...  9.5 us
    pallas_call x1, Pallas kernels, make_values(): pl.pallas_call(value_kernel, in_specs=[VMEM, HBM, HBM], out_specs=[HBM] *...  7.83 us
    all_to_all x1, starting transfers between devices, body(): lax.all_to_all(send, ('depth', 'xlo', 'xhi', 'core'), split_axis=0, conca...  7.27 us
    pallas_call x6, Pallas kernels, small_call(): pl.pallas_call(kernel, in_specs=specs or [VMEM] * len(operands), out_spec...  5.07 us
    pallas_call x1, Pallas kernels, encode(): pl.pallas_call(encode_kernel, in_specs=[SMEM, SMEM, HBM] + [VMEM] * 5, ou...  5.02 us
    ppermute x2, starting transfers between devices, exchange(): return lax.ppermute(block, axis, [(0, 1), (1, 0)])  4.76 us
  transfers between devices with their start and end apart: 7, of which 4 were waited for; matrix products, arithmetic and copies ran while one was open for 0% of the time, Pallas kernels for 23%

profile of v4, /device:TPU:32, one launch (start us, length us, event | category | flops | bytes accessed | tf_op | source)
XLA Modules:
  0.0 108.7 jit_solution(15047217814336129132)
XLA Ops:
  0.6 0.0 copy-start.1
  0.6 0.0 copy-start
  0.7 3.1 %collective-permute-start.1 = (bf16[64,512]{1,0:T(8,128)(2,1)}, bf16[64,512]{1,0:T(8,128)(2,1)S(1)}, u32[]{:S(2)}, u32[]{:S(2)}) collective-permute-start(bf16[64,512]{1,0:T(8,128)(2,1)} %bitcast.17), channel_id=1, source_target_pairs={{4,0},{8,4},{12,8},{16,12},{20,16},{24,20},{28,24},{32,28},{36,32}... | collective-permute-start | bytes 196616 | tf_op jit(solution)/shard_map/ppermute | solution.py:647
  3.7 2.9 %collective-permute-start = (bf16[64,512]{1,0:T(8,128)(2,1)}, bf16[64,512]{1,0:T(8,128)(2,1)S(1)}, u32[]{:S(2)}, u32[]{:S(2)}) collective-permute-start(bf16[64,512]{1,0:T(8,128)(2,1)} %bitcast.18), channel_id=1, source_target_pairs={{0,4},{4,8},{8,12},{12,16},{16,20},{20,24},{24,28},{28,32},{32,36}... | collective-permute-start | bytes 196616 | tf_op jit(solution)/shard_map/ppermute | solution.py:646
  6.6 5.0 %shard_map.121 = (bf16[2048,512]{1,0:T(8,128)(2,1)}, bf16[2048,128]{1,0:T(8,128)(2,1)S(1)}, f32[64,128]{1,0:T(8,128)S(1)}, bf16[64,128]{1,0:T(8,128)(2,1)S(1)}) custom-call(s32[1]{0:T(128)} %bitcast.3.depth_ref, s32[64]{0:T(128)} %bitcast.24, bf16[64,32,512]{2,1,0:T(8,128)(2,1)} %bitcast.20, s32[32,64]{1,0:T(8,128)} %bitcast.21, s32[32,64]{1,0:T(8,128)} %bitcast.22, ...), custom_call_target="tpu_custom_call" | custom-call | flops 536870912 | bytes 4194304 | tf_op jit(solution)/shard_map/pallas_call | solution.py:206
  11.7 0.0 collective-permute-done.1.after_ref
  11.7 2.3 %collective-permute-done.before_ref = bf16[64,512]{1,0:T(8,128)(2,1)S(1)} collective-permute-done((bf16[64,512]{1,0:T(8,128)(2,1)}, bf16[64,512]{1,0:T(8,128)(2,1)S(1)}, u32[]{:S(2)}, u32[]{:S(2)}) %collective-permute-start) | collective-permute-done | bytes 65568 | tf_op jit(solution)/shard_map/ppermute | solution.py:646
  14.0 0.0 copy-done.1
  14.0 0.0 copy-done
  14.0 1.2 %shard_map.122 = (bf16[4,64,384]{2,1,0:T(8,128)(2,1)}, bf16[4,80,128]{2,1,0:T(8,128)(2,1)S(1)}) custom-call(bf16[64,512]{1,0:T(8,128)(2,1)S(1)} %collective-permute-done.before_ref, bf16[64,512]{1,0:T(8,128)(2,1)S(1)} %bitcast.19, bf16[64,512]{1,0:T(8,128)(2,1)S(1)} %collective-permute-done.1.after_ref, bf16[5,256,512]{2,1,0:T(8,128)(2,1)S(1)} %bitcast.16, ...), custom_call_target="tpu_custom_call" | custom-call | flops 1000000 | bytes 100000 | tf_op jit(solution)/shard_map/pallas_call | solution.py:609
  15.2 3.4 %all-to-all-start = ((bf16[4,64,384]{2,1,0:T(8,128)(2,1)}), bf16[4,64,384]{2,1,0:T(8,128)(2,1)S(1)}, u32[]{:S(2)}, u32[]{:S(2)}) async-start(bf16[4,64,384]{2,1,0:T(8,128)(2,1)} %get-tuple-element.22), calls=%async_computation | async-start | bytes 393216 | tf_op jit(solution)/shard_map/all_to_all | solution.py:669
  18.6 7.8 %shard_map.123 = (bf16[2048,128]{1,0:T(8,128)(2,1)}, bf16[4,2048,256]{2,1,0:T(8,128)(2,1)}, bf16[4,2048,256]{2,1,0:T(8,128)(2,1)}, f32[64,1024]{1,0:T(8,128)S(1)}) custom-call(bf16[2048,128]{1,0:T(8,128)(2,1)S(1)} %get-tuple-element.24.pair_ref, bf16[2048,512]{1,0:T(8,128)(2,1)} %get-tuple-element.25.features_hbm, bf16[1024,512]{1,0:T(8,128)(2,1)} %value_hbm.1), custom_call_target="tpu_custom_call" | custom-call | flops 3221225472 | bytes 16777216 | tf_op jit(solution)/shard_map/pallas_call | solution.py:235
  26.4 0.0 all-to-all-done.payload_ref
  26.4 1.7 %shard_map.124 = (bf16[32,96,128]{2,1,0:T(8,128)(2,1)}, f32[64,128]{1,0:T(8,128)S(1)}) custom-call(s32[1]{0:T(128)} %bitcast.3.depth_ref, bf16[4,64,384]{2,1,0:T(8,128)(2,1)S(1)} %all-to-all-done.payload_ref, f32[64,128]{1,0:T(8,128)S(1)} %get-tuple-element.23.top_ref, f32[64,1024]{1,0:T(8,128)S(1)} %get-tuple-element.26.pool_ref, ...), custom_call_target="tpu_custom_call" | custom-call | flops 1000000 | bytes 100000 | tf_op jit(solution)/shard_map/pallas_call | solution.py:609
  28.1 7.3 %all-to-all-start.1 = ((bf16[32,96,128]{2,1,0:T(8,128)(2,1)}), bf16[32,96,128]{2,1,0:T(8,128)(2,1)S(1)}, u32[]{:S(2)}, u32[]{:S(2)}) async-start(bf16[32,96,128]{2,1,0:T(8,128)(2,1)} %get-tuple-element.34), calls=%async_computation.1 | async-start | bytes 1572864 | tf_op jit(solution)/shard_map/all_to_all | solution.py:686
  35.4 9.5 %shard_map.125 = (bf16[16,128,128]{2,1,0:T(8,128)(2,1)S(1)}, bf16[16,128,128]{2,1,0:T(8,128)(2,1)S(1)}, f32[2048,128]{1,0:T(8,128)}) custom-call(s32[1]{0:T(128)} %bitcast.core_ref, bf16[4,64,384]{2,1,0:T(8,128)(2,1)S(1)} %all-to-all-done.payload_ref, f32[64,128]{1,0:T(8,128)S(1)} %get-tuple-element.28.scale_ref, ...), custom_call_target="tpu_custom_call" | custom-call | flops 3221225472 | bytes 16777216 | tf_op jit(solution)/shard_map/pallas_call | solution.py:461
  44.9 2.0 %collective-permute-start.2 = (bf16[16,128,128]{2,1,0:T(8,128)(2,1)S(1)}, bf16[16,128,128]{2,1,0:T(8,128)(2,1)S(1)}, u32[]{:S(2)}, u32[]{:S(2)}) collective-permute-start(bf16[16,128,128]{2,1,0:T(8,128)(2,1)S(1)} %get-tuple-element.33), channel_id=1, source_target_pairs={{0,1},{1,0},{2,3},{3,2},{4,5},{5,4},{6,7},{7,6},{8,9},{9,8},{10,11... | collective-permute-start | bytes 1572872 | tf_op jit(solution)/shard_map/ppermute | solution.py:621
  46.9 2.0 %all-to-all-done.1.recv_ref = bf16[32,96,128]{2,1,0:T(8,128)(2,1)S(1)} async-done(((bf16[32,96,128]{2,1,0:T(8,128)(2,1)}), bf16[32,96,128]{2,1,0:T(8,128)(2,1)S(1)}, u32[]{:S(2)}, u32[]{:S(2)}) %all-to-all-start.1) | async-done | bytes 786464 | tf_op jit(solution)/shard_map/all_to_all | solution.py:686
  48.9 2.4 %shard_map.126.score_ref = bf16[32,128]{1,0:T(8,128)(2,1)S(1)} custom-call(s32[1]{0:T(128)} %bitcast.11.place_ref, bf16[32,96,128]{2,1,0:T(8,128)(2,1)S(1)} %all-to-all-done.1.recv_ref, f32[2048,128]{1,0:T(8,128)} %get-tuple-element.35.probs_hbm, bf16[2048,512]{1,0:T(8,128)(2,1)} %get-tuple-element.25.features_hbm), custom_call_target="tpu_custom_call" | custom-call | flops 100000000 | bytes 1000000 | tf_op jit(solution)/shard_map/pallas_call | solution.py:535
  51.3 2.8 %collective-permute-start.3 = (bf16[32,128]{1,0:T(8,128)(2,1)S(1)}, bf16[32,128]{1,0:T(8,128)(2,1)S(1)}, u32[]{:S(2)}, u32[]{:S(2)}) collective-permute-start(bf16[32,128]{1,0:T(8,128)(2,1)S(1)} %shard_map.126.score_ref), channel_id=1, source_target_pairs={{0,1},{1,0},{2,3},{3,2},{4,5},{5,4},{6,7},{7,6},{8,9},{9,8},{10,11... | collective-permute-start | bytes 24584 | tf_op jit(solution)/shard_map/ppermute | solution.py:621
  54.1 0.0 collective-permute-done.2.theirs_ref
  54.1 0.8 collective-permute-done.3.other_ref
  54.9 1.0 shard_map.127
  55.9 4.5 %all-to-all-start.2 = ((bf16[16,160,128]{2,1,0:T(8,128)(2,1)}), bf16[16,160,128]{2,1,0:T(8,128)(2,1)S(1)}, u32[]{:S(2)}, u32[]{:S(2)}) async-start(bf16[16,160,128]{2,1,0:T(8,128)(2,1)} %shard_map.127), calls=%async_computation.2 | async-start | bytes 1310720 | tf_op jit(solution)/shard_map/all_to_all | solution.py:700
  60.4 0.4 shard_map.128.conv_ref
  60.8 11.8 %all-to-all-done.2.recv_ref = bf16[16,160,128]{2,1,0:T(8,128)(2,1)S(1)} async-done(((bf16[16,160,128]{2,1,0:T(8,128)(2,1)}), bf16[16,160,128]{2,1,0:T(8,128)(2,1)S(1)}, u32[]{:S(2)}, u32[]{:S(2)}) %all-to-all-start.2) | async-done | bytes 655392 | tf_op jit(solution)/shard_map/all_to_all | solution.py:700
  72.6 0.1 shard_map.129
  72.7 35.3 %all_to_all.20.recv_ref = bf16[16,80,128]{2,1,0:T(8,128)(2,1)S(1)} all-to-all(bf16[16,80,128]{2,1,0:T(8,128)(2,1)S(1)} %shard_map.129), channel_id=1, replica_groups=mesh['depth'=4,'z'=16,'xlo'=2,'xhi'=2,'core'=2] {'z'}, dimensions={0} | all-to-all | bytes 655360 | tf_op jit(solution)/shard_map/all_to_all | solution.py:712
  108.0 0.7 shard_map.130
Async XLA Ops:
  0.6 13.4 %copy-start.1 = (bf16[1,64,512]{2,1,0:T(8,128)(2,1)S(1)}, bf16[1,64,512]{2,1,0:T(8,128)(2,1)}, u32[]{:S(2)}) copy-start(bf16[1,64,512]{2,1,0:T(8,128)(2,1)} %param.19) | copy-start | bytes 196612
  0.6 13.4 %copy-start = (bf16[256,5,512]{2,0,1:T(8,128)(2,1)S(1)}, bf16[256,5,512]{2,0,1:T(8,128)(2,1)}, u32[]{:S(2)}) copy-start(bf16[256,5,512]{2,0,1:T(8,128)(2,1)} %param.18) | copy-start | bytes 3932164
  0.7 11.0 %collective-permute-start.1 = (bf16[64,512]{1,0:T(8,128)(2,1)}, bf16[64,512]{1,0:T(8,128)(2,1)S(1)}, u32[]{:S(2)}, u32[]{:S(2)}) collective-permute-start(bf16[64,512]{1,0:T(8,128)(2,1)} %bitcast.17), channel_id=1, source_target_pairs={{4,0},{8,4},{12,8},{16,12},{20,16},{24,20},{28,24},{32,28},{36,32}... | collective-permute-start | bytes 196616 | tf_op jit(solution)/shard_map/ppermute | solution.py:647
  3.7 10.3 %collective-permute-start = (bf16[64,512]{1,0:T(8,128)(2,1)}, bf16[64,512]{1,0:T(8,128)(2,1)S(1)}, u32[]{:S(2)}, u32[]{:S(2)}) collective-permute-start(bf16[64,512]{1,0:T(8,128)(2,1)} %bitcast.18), channel_id=1, source_target_pairs={{0,4},{4,8},{8,12},{12,16},{16,20},{20,24},{24,28},{28,32},{32,36}... | collective-permute-start | bytes 196616 | tf_op jit(solution)/shard_map/ppermute | solution.py:646
  15.2 11.2 %all-to-all-start = ((bf16[4,64,384]{2,1,0:T(8,128)(2,1)}), bf16[4,64,384]{2,1,0:T(8,128)(2,1)S(1)}, u32[]{:S(2)}, u32[]{:S(2)}) async-start(bf16[4,64,384]{2,1,0:T(8,128)(2,1)} %get-tuple-element.22), calls=%async_computation | async-start | bytes 393216 | tf_op jit(solution)/shard_map/all_to_all | solution.py:669
  28.1 20.8 %all-to-all-start.1 = ((bf16[32,96,128]{2,1,0:T(8,128)(2,1)}), bf16[32,96,128]{2,1,0:T(8,128)(2,1)S(1)}, u32[]{:S(2)}, u32[]{:S(2)}) async-start(bf16[32,96,128]{2,1,0:T(8,128)(2,1)} %get-tuple-element.34), calls=%async_computation.1 | async-start | bytes 1572864 | tf_op jit(solution)/shard_map/all_to_all | solution.py:686
  44.9 9.2 %collective-permute-start.2 = (bf16[16,128,128]{2,1,0:T(8,128)(2,1)S(1)}, bf16[16,128,128]{2,1,0:T(8,128)(2,1)S(1)}, u32[]{:S(2)}, u32[]{:S(2)}) collective-permute-start(bf16[16,128,128]{2,1,0:T(8,128)(2,1)S(1)} %get-tuple-element.33), channel_id=1, source_target_pairs={{0,1},{1,0},{2,3},{3,2},{4,5},{5,4},{6,7},{7,6},{8,9},{9,8},{10,11... | collective-permute-start | bytes 1572872 | tf_op jit(solution)/shard_map/ppermute | solution.py:621
  51.3 3.6 %collective-permute-start.3 = (bf16[32,128]{1,0:T(8,128)(2,1)S(1)}, bf16[32,128]{1,0:T(8,128)(2,1)S(1)}, u32[]{:S(2)}, u32[]{:S(2)}) collective-permute-start(bf16[32,128]{1,0:T(8,128)(2,1)S(1)} %shard_map.126.score_ref), channel_id=1, source_target_pairs={{0,1},{1,0},{2,3},{3,2},{4,5},{5,4},{6,7},{7,6},{8,9},{9,8},{10,11... | collective-permute-start | bytes 24584 | tf_op jit(solution)/shard_map/ppermute | solution.py:621
  55.9 16.7 %all-to-all-start.2 = ((bf16[16,160,128]{2,1,0:T(8,128)(2,1)}), bf16[16,160,128]{2,1,0:T(8,128)(2,1)S(1)}, u32[]{:S(2)}, u32[]{:S(2)}) async-start(bf16[16,160,128]{2,1,0:T(8,128)(2,1)} %shard_map.127), calls=%async_computation.2 | async-start | bytes 1310720 | tf_op jit(solution)/shard_map/all_to_all | solution.py:700

commit v5 on v4

--- a/solution.py
+++ b/solution.py
@@ -126,38 +126,32 @@
 
 def value_kernel(
     pair_ref,
+    value_ref,
     features_hbm,
-    value_hbm,
     pair_out,
     slope_out,
     values_out,
     pool_out,
     features_buf,
-    value_buf,
     slope_buf,
     values_buf,
     preact_buf,
     spread_buf,
-    load_sems,
+    load_sem,
     sems,
 ):
     positions = pool_out.shape[0]
     reads = features_buf.shape[0] // positions
-    load = [
-        pltpu.make_async_copy(features_hbm, features_buf, load_sems.at[0]),
-        pltpu.make_async_copy(value_hbm, value_buf, load_sems.at[1]),
-    ]
-    for copy in load:
-        copy.start()
+    load = pltpu.make_async_copy(features_hbm, features_buf, load_sem)
+    load.start()
     spread_buf[0] = dot(pair_ref[...], spread_of(0))
-    for copy in load:
-        copy.wait()
+    load.wait()
     stores = [pltpu.make_async_copy(pair_ref, pair_out, sems.at[1])]
     stores[0].start()
 
     def multiply(part):
         cols = slice(part * OWN_UNITS, (part + 1) * OWN_UNITS)
-        preact_buf[part % 2] = dot(features_buf[...], value_buf[cols, :], 1, 1)
+        preact_buf[part % 2] = dot(features_buf[...], value_ref[cols, :], 1, 1)
         if part:
             spread_buf[part % 2] = dot(pair_ref[...], spread_of(part))
 
@@ -170,7 +164,7 @@
             near = slice(p * reads, (p + 1) * reads)
             preact = preact_buf[part % 2, near, :].astype(BF16)
             spread = spread_buf[part % 2, near, :].astype(BF16)
-            sigma = 0.5 * jnp.tanh(0.5 * preact) + 0.5
+            sigma = pl.reciprocal(1.0 + jnp.exp(-preact), approx=True)
             values = preact * sigma
             slope = sigma + values * (1.0 - sigma)
             slope_buf[part, near, :] = spread * slope
@@ -234,7 +228,7 @@
     rows, channels = features.shape
     return pl.pallas_call(
         value_kernel,
-        in_specs=[VMEM, HBM, HBM],
+        in_specs=[VMEM, VMEM, HBM],
         out_specs=[HBM] * 3 + [VMEM],
         out_shape=[
             pltpu.HBM((rows, LANES), BF16),
@@ -244,12 +238,11 @@
         ],
         scratch_shapes=[
             pltpu.VMEM((rows, channels), BF16),
-            pltpu.VMEM(value_weight.shape, BF16),
             pltpu.VMEM((N_DEPTH, rows, OWN_UNITS), BF16),
             pltpu.VMEM((N_DEPTH, rows, OWN_UNITS), BF16),
             pltpu.VMEM((2, rows, OWN_UNITS), F32),
             pltpu.VMEM((2, rows, OWN_UNITS), F32),
-            pltpu.SemaphoreType.DMA((2,)),
+            pltpu.SemaphoreType.DMA,
             pltpu.SemaphoreType.DMA((2 + 4 * N_DEPTH,)),
         ],
         compiler_params=pltpu.CompilerParams(vmem_limit_bytes=32 * 2**20),
@@ -258,7 +251,7 @@
             bytes_accessed=16 * 2**20,
             transcendentals=rows * UNITS,
         ),
-    )(pair, *in_hbm(features, value_weight))
+    )(pair, value_weight, *in_hbm(features))
 
 
 def rim_kernel(before_ref, local_ref, after_ref, weight_ref, stat_ref, payload_out, cols_out):
@@ -468,7 +461,7 @@
             pltpu.HBM((rows, LANES), F32),
         ],
         scratch_shapes=[
-            pltpu.VMEM((4, UNITS, 128), F32),
+            pltpu.VMEM((4, UNITS + 16, 128), F32),
             pltpu.VMEM((N_DEPTH, rows, OWN_UNITS), BF16),
             pltpu.VMEM((N_DEPTH, rows, OWN_UNITS), BF16),
             pltpu.VMEM((rows, channels), BF16),

time: 109 us -> 109 us (level)
  no operation moved by 1% of the time
where the time goes in v5:
time: 109 us
  blocking collectives  35.3 us (32%)
  Pallas kernels  29.7 us (27%)
  starting transfers between devices  25.9 us (24%)
  waiting for transfers between devices  16.9 us (16%)
    all_to_all x1, blocking collectives, body(): lax.all_to_all(line_send, 'z', split_axis=0, concat_axis=0, tiled=True)  35.3 us
    all_to_all x1, waiting for transfers between devices, body(): lax.all_to_all(plane_send, ('depth', 'xlo', 'xhi'), split_axis=0, concat_...  11.8 us
    pallas_call x1, Pallas kernels, gradients(): pl.pallas_call(gradient_kernel, in_specs=[SMEM] + [VMEM] * 2 + [HBM] * 4,...  9.5 us
    pallas_call x1, Pallas kernels, make_values(): pl.pallas_call(value_kernel, in_specs=[VMEM, VMEM, HBM], out_specs=[HBM]...  7.72 us
    all_to_all x1, starting transfers between devices, body(): lax.all_to_all(send, ('depth', 'xlo', 'xhi', 'core'), split_axis=0, conca...  7.26 us
    pallas_call x6, Pallas kernels, small_call(): pl.pallas_call(kernel, in_specs=specs or [VMEM] * len(operands), out_spec...  5.07 us
    pallas_call x1, Pallas kernels, encode(): pl.pallas_call(encode_kernel, in_specs=[SMEM, SMEM, HBM] + [VMEM] * 5, ou...  5.02 us
    ppermute x2, starting transfers between devices, exchange(): return lax.ppermute(block, axis, [(0, 1), (1, 0)])  4.75 us
  transfers between devices with their start and end apart: 7, of which 4 were waited for; matrix products, arithmetic and copies ran while one was open for 0% of the time, Pallas kernels for 23%

profile of v5, /device:TPU:32, one launch (start us, length us, event | category | flops | bytes accessed | tf_op | source)
XLA Modules:
  0.0 108.6 jit_solution(7014410737369998407)
XLA Ops:
  0.6 0.0 copy-start.1
  0.6 0.0 copy-start
  0.7 0.0 copy-start.2
  0.7 3.1 %collective-permute-start.1 = (bf16[64,512]{1,0:T(8,128)(2,1)}, bf16[64,512]{1,0:T(8,128)(2,1)S(1)}, u32[]{:S(2)}, u32[]{:S(2)}) collective-permute-start(bf16[64,512]{1,0:T(8,128)(2,1)} %bitcast.17), channel_id=1, source_target_pairs={{4,0},{8,4},{12,8},{16,12},{20,16},{24,20},{28,24},{32,28},{36,32}... | collective-permute-start | bytes 196616 | tf_op jit(solution)/shard_map/ppermute | solution.py:640
  3.7 2.9 %collective-permute-start = (bf16[64,512]{1,0:T(8,128)(2,1)}, bf16[64,512]{1,0:T(8,128)(2,1)S(1)}, u32[]{:S(2)}, u32[]{:S(2)}) collective-permute-start(bf16[64,512]{1,0:T(8,128)(2,1)} %bitcast.18), channel_id=1, source_target_pairs={{0,4},{4,8},{8,12},{12,16},{16,20},{20,24},{24,28},{28,32},{32,36}... | collective-permute-start | bytes 196616 | tf_op jit(solution)/shard_map/ppermute | solution.py:639
  6.7 5.0 %shard_map.121 = (bf16[2048,512]{1,0:T(8,128)(2,1)}, bf16[2048,128]{1,0:T(8,128)(2,1)S(1)}, f32[64,128]{1,0:T(8,128)S(1)}, bf16[64,128]{1,0:T(8,128)(2,1)S(1)}) custom-call(s32[1]{0:T(128)} %bitcast.3.depth_ref, s32[64]{0:T(128)} %bitcast.24, bf16[64,32,512]{2,1,0:T(8,128)(2,1)} %bitcast.20, s32[32,64]{1,0:T(8,128)} %bitcast.21, s32[32,64]{1,0:T(8,128)} %bitcast.22, ...), custom_call_target="tpu_custom_call" | custom-call | flops 536870912 | bytes 4194304 | tf_op jit(solution)/shard_map/pallas_call | solution.py:200
  11.7 0.0 collective-permute-done.1.after_ref
  11.7 2.3 %collective-permute-done.before_ref = bf16[64,512]{1,0:T(8,128)(2,1)S(1)} collective-permute-done((bf16[64,512]{1,0:T(8,128)(2,1)}, bf16[64,512]{1,0:T(8,128)(2,1)S(1)}, u32[]{:S(2)}, u32[]{:S(2)}) %collective-permute-start) | collective-permute-done | bytes 65568 | tf_op jit(solution)/shard_map/ppermute | solution.py:639
  14.0 0.0 copy-done.1
  14.0 0.0 copy-done
  14.0 1.2 %shard_map.122 = (bf16[4,64,384]{2,1,0:T(8,128)(2,1)}, bf16[4,80,128]{2,1,0:T(8,128)(2,1)S(1)}) custom-call(bf16[64,512]{1,0:T(8,128)(2,1)S(1)} %collective-permute-done.before_ref, bf16[64,512]{1,0:T(8,128)(2,1)S(1)} %bitcast.19, bf16[64,512]{1,0:T(8,128)(2,1)S(1)} %collective-permute-done.1.after_ref, bf16[5,256,512]{2,1,0:T(8,128)(2,1)S(1)} %bitcast.16, ...), custom_call_target="tpu_custom_call" | custom-call | flops 1000000 | bytes 100000 | tf_op jit(solution)/shard_map/pallas_call | solution.py:602
  15.2 3.4 %all-to-all-start = ((bf16[4,64,384]{2,1,0:T(8,128)(2,1)}), bf16[4,64,384]{2,1,0:T(8,128)(2,1)S(1)}, u32[]{:S(2)}, u32[]{:S(2)}) async-start(bf16[4,64,384]{2,1,0:T(8,128)(2,1)} %get-tuple-element.22), calls=%async_computation | async-start | bytes 393216 | tf_op jit(solution)/shard_map/all_to_all | solution.py:662
  18.6 0.0 copy-done.2
  18.6 7.7 %shard_map.123 = (bf16[2048,128]{1,0:T(8,128)(2,1)}, bf16[4,2048,256]{2,1,0:T(8,128)(2,1)}, bf16[4,2048,256]{2,1,0:T(8,128)(2,1)}, f32[64,1024]{1,0:T(8,128)S(1)}) custom-call(bf16[2048,128]{1,0:T(8,128)(2,1)S(1)} %get-tuple-element.24.pair_ref, bf16[1024,512]{1,0:T(8,128)(2,1)S(1)} %copy-done.2, bf16[2048,512]{1,0:T(8,128)(2,1)} %get-tuple-element.25.features_hbm), custom_call_target="tpu_custom_call" | custom-call | flops 3221225472 | bytes 16777216 | tf_op jit(solution)/shard_map/pallas_call | solution.py:229
  26.4 0.0 all-to-all-done.payload_ref
  26.4 1.7 %shard_map.124 = (bf16[32,96,128]{2,1,0:T(8,128)(2,1)}, f32[64,128]{1,0:T(8,128)S(1)}) custom-call(s32[1]{0:T(128)} %bitcast.3.depth_ref, bf16[4,64,384]{2,1,0:T(8,128)(2,1)S(1)} %all-to-all-done.payload_ref, f32[64,128]{1,0:T(8,128)S(1)} %get-tuple-element.23.top_ref, f32[64,1024]{1,0:T(8,128)S(1)} %get-tuple-element.26.pool_ref, ...), custom_call_target="tpu_custom_call" | custom-call | flops 1000000 | bytes 100000 | tf_op jit(solution)/shard_map/pallas_call | solution.py:602
  28.0 7.3 %all-to-all-start.1 = ((bf16[32,96,128]{2,1,0:T(8,128)(2,1)}), bf16[32,96,128]{2,1,0:T(8,128)(2,1)S(1)}, u32[]{:S(2)}, u32[]{:S(2)}) async-start(bf16[32,96,128]{2,1,0:T(8,128)(2,1)} %get-tuple-element.34), calls=%async_computation.1 | async-start | bytes 1572864 | tf_op jit(solution)/shard_map/all_to_all | solution.py:679
  35.3 9.5 %shard_map.125 = (bf16[16,128,128]{2,1,0:T(8,128)(2,1)S(1)}, bf16[16,128,128]{2,1,0:T(8,128)(2,1)S(1)}, f32[2048,128]{1,0:T(8,128)}) custom-call(s32[1]{0:T(128)} %bitcast.core_ref, bf16[4,64,384]{2,1,0:T(8,128)(2,1)S(1)} %all-to-all-done.payload_ref, f32[64,128]{1,0:T(8,128)S(1)} %get-tuple-element.28.scale_ref, ...), custom_call_target="tpu_custom_call" | custom-call | flops 3221225472 | bytes 16777216 | tf_op jit(solution)/shard_map/pallas_call | solution.py:454
  44.8 2.0 %collective-permute-start.2 = (bf16[16,128,128]{2,1,0:T(8,128)(2,1)S(1)}, bf16[16,128,128]{2,1,0:T(8,128)(2,1)S(1)}, u32[]{:S(2)}, u32[]{:S(2)}) collective-permute-start(bf16[16,128,128]{2,1,0:T(8,128)(2,1)S(1)} %get-tuple-element.33), channel_id=1, source_target_pairs={{0,1},{1,0},{2,3},{3,2},{4,5},{5,4},{6,7},{7,6},{8,9},{9,8},{10,11... | collective-permute-start | bytes 1572872 | tf_op jit(solution)/shard_map/ppermute | solution.py:614
  46.8 2.0 %all-to-all-done.1.recv_ref = bf16[32,96,128]{2,1,0:T(8,128)(2,1)S(1)} async-done(((bf16[32,96,128]{2,1,0:T(8,128)(2,1)}), bf16[32,96,128]{2,1,0:T(8,128)(2,1)S(1)}, u32[]{:S(2)}, u32[]{:S(2)}) %all-to-all-start.1) | async-done | bytes 786464 | tf_op jit(solution)/shard_map/all_to_all | solution.py:679
  48.8 2.4 %shard_map.126.score_ref = bf16[32,128]{1,0:T(8,128)(2,1)S(1)} custom-call(s32[1]{0:T(128)} %bitcast.11.place_ref, bf16[32,96,128]{2,1,0:T(8,128)(2,1)S(1)} %all-to-all-done.1.recv_ref, f32[2048,128]{1,0:T(8,128)} %get-tuple-element.35.probs_hbm, bf16[2048,512]{1,0:T(8,128)(2,1)} %get-tuple-element.25.features_hbm), custom_call_target="tpu_custom_call" | custom-call | flops 100000000 | bytes 1000000 | tf_op jit(solution)/shard_map/pallas_call | solution.py:528
  51.2 2.7 %collective-permute-start.3 = (bf16[32,128]{1,0:T(8,128)(2,1)S(1)}, bf16[32,128]{1,0:T(8,128)(2,1)S(1)}, u32[]{:S(2)}, u32[]{:S(2)}) collective-permute-start(bf16[32,128]{1,0:T(8,128)(2,1)S(1)} %shard_map.126.score_ref), channel_id=1, source_target_pairs={{0,1},{1,0},{2,3},{3,2},{4,5},{5,4},{6,7},{7,6},{8,9},{9,8},{10,11... | collective-permute-start | bytes 24584 | tf_op jit(solution)/shard_map/ppermute | solution.py:614
  54.0 0.0 collective-permute-done.2.theirs_ref
  54.0 0.8 collective-permute-done.3.other_ref
  54.8 1.0 shard_map.127
  55.8 4.5 %all-to-all-start.2 = ((bf16[16,160,128]{2,1,0:T(8,128)(2,1)}), bf16[16,160,128]{2,1,0:T(8,128)(2,1)S(1)}, u32[]{:S(2)}, u32[]{:S(2)}) async-start(bf16[16,160,128]{2,1,0:T(8,128)(2,1)} %shard_map.127), calls=%async_computation.2 | async-start | bytes 1310720 | tf_op jit(solution)/shard_map/all_to_all | solution.py:693
  60.3 0.4 shard_map.128.conv_ref
  60.7 11.8 %all-to-all-done.2.recv_ref = bf16[16,160,128]{2,1,0:T(8,128)(2,1)S(1)} async-done(((bf16[16,160,128]{2,1,0:T(8,128)(2,1)}), bf16[16,160,128]{2,1,0:T(8,128)(2,1)S(1)}, u32[]{:S(2)}, u32[]{:S(2)}) %all-to-all-start.2) | async-done | bytes 655392 | tf_op jit(solution)/shard_map/all_to_all | solution.py:693
  72.5 0.1 shard_map.129
  72.6 35.3 %all_to_all.20.recv_ref = bf16[16,80,128]{2,1,0:T(8,128)(2,1)S(1)} all-to-all(bf16[16,80,128]{2,1,0:T(8,128)(2,1)S(1)} %shard_map.129), channel_id=1, replica_groups=mesh['depth'=4,'z'=16,'xlo'=2,'xhi'=2,'core'=2] {'z'}, dimensions={0} | all-to-all | bytes 655360 | tf_op jit(solution)/shard_map/all_to_all | solution.py:705
  107.9 0.7 shard_map.130
Async XLA Ops:
  0.6 13.4 %copy-start.1 = (bf16[1,64,512]{2,1,0:T(8,128)(2,1)S(1)}, bf16[1,64,512]{2,1,0:T(8,128)(2,1)}, u32[]{:S(2)}) copy-start(bf16[1,64,512]{2,1,0:T(8,128)(2,1)} %param.19) | copy-start | bytes 196612
  0.6 13.4 %copy-start = (bf16[256,5,512]{2,0,1:T(8,128)(2,1)S(1)}, bf16[256,5,512]{2,0,1:T(8,128)(2,1)}, u32[]{:S(2)}) copy-start(bf16[256,5,512]{2,0,1:T(8,128)(2,1)} %param.18) | copy-start | bytes 3932164
  0.7 18.0 %copy-start.2 = (bf16[1024,512]{1,0:T(8,128)(2,1)S(1)}, bf16[1024,512]{1,0:T(8,128)(2,1)}, u32[]{:S(2)}) copy-start(bf16[1024,512]{1,0:T(8,128)(2,1)} %value_ref.1) | copy-start | bytes 3145732
  0.7 11.0 %collective-permute-start.1 = (bf16[64,512]{1,0:T(8,128)(2,1)}, bf16[64,512]{1,0:T(8,128)(2,1)S(1)}, u32[]{:S(2)}, u32[]{:S(2)}) collective-permute-start(bf16[64,512]{1,0:T(8,128)(2,1)} %bitcast.17), channel_id=1, source_target_pairs={{4,0},{8,4},{12,8},{16,12},{20,16},{24,20},{28,24},{32,28},{36,32}... | collective-permute-start | bytes 196616 | tf_op jit(solution)/shard_map/ppermute | solution.py:640
  3.7 10.3 %collective-permute-start = (bf16[64,512]{1,0:T(8,128)(2,1)}, bf16[64,512]{1,0:T(8,128)(2,1)S(1)}, u32[]{:S(2)}, u32[]{:S(2)}) collective-permute-start(bf16[64,512]{1,0:T(8,128)(2,1)} %bitcast.18), channel_id=1, source_target_pairs={{0,4},{4,8},{8,12},{12,16},{16,20},{20,24},{24,28},{28,32},{32,36}... | collective-permute-start | bytes 196616 | tf_op jit(solution)/shard_map/ppermute | solution.py:639
  15.2 11.1 %all-to-all-start = ((bf16[4,64,384]{2,1,0:T(8,128)(2,1)}), bf16[4,64,384]{2,1,0:T(8,128)(2,1)S(1)}, u32[]{:S(2)}, u32[]{:S(2)}) async-start(bf16[4,64,384]{2,1,0:T(8,128)(2,1)} %get-tuple-element.22), calls=%async_computation | async-start | bytes 393216 | tf_op jit(solution)/shard_map/all_to_all | solution.py:662
  28.0 20.8 %all-to-all-start.1 = ((bf16[32,96,128]{2,1,0:T(8,128)(2,1)}), bf16[32,96,128]{2,1,0:T(8,128)(2,1)S(1)}, u32[]{:S(2)}, u32[]{:S(2)}) async-start(bf16[32,96,128]{2,1,0:T(8,128)(2,1)} %get-tuple-element.34), calls=%async_computation.1 | async-start | bytes 1572864 | tf_op jit(solution)/shard_map/all_to_all | solution.py:679
  44.8 9.2 %collective-permute-start.2 = (bf16[16,128,128]{2,1,0:T(8,128)(2,1)S(1)}, bf16[16,128,128]{2,1,0:T(8,128)(2,1)S(1)}, u32[]{:S(2)}, u32[]{:S(2)}) collective-permute-start(bf16[16,128,128]{2,1,0:T(8,128)(2,1)S(1)} %get-tuple-element.33), channel_id=1, source_target_pairs={{0,1},{1,0},{2,3},{3,2},{4,5},{5,4},{6,7},{7,6},{8,9},{9,8},{10,11... | collective-permute-start | bytes 1572872 | tf_op jit(solution)/shard_map/ppermute | solution.py:614
  51.2 3.6 %collective-permute-start.3 = (bf16[32,128]{1,0:T(8,128)(2,1)S(1)}, bf16[32,128]{1,0:T(8,128)(2,1)S(1)}, u32[]{:S(2)}, u32[]{:S(2)}) collective-permute-start(bf16[32,128]{1,0:T(8,128)(2,1)S(1)} %shard_map.126.score_ref), channel_id=1, source_target_pairs={{0,1},{1,0},{2,3},{3,2},{4,5},{5,4},{6,7},{7,6},{8,9},{9,8},{10,11... | collective-permute-start | bytes 24584 | tf_op jit(solution)/shard_map/ppermute | solution.py:614
  55.8 16.7 %all-to-all-start.2 = ((bf16[16,160,128]{2,1,0:T(8,128)(2,1)}), bf16[16,160,128]{2,1,0:T(8,128)(2,1)S(1)}, u32[]{:S(2)}, u32[]{:S(2)}) async-start(bf16[16,160,128]{2,1,0:T(8,128)(2,1)} %shard_map.127), calls=%async_computation.2 | async-start | bytes 1310720 | tf_op jit(solution)/shard_map/all_to_all | solution.py:693

commit v6 on v5

--- a/solution.py
+++ b/solution.py
@@ -41,6 +41,7 @@
     depth_ref,
     count_ref,
     feat_hbm,
+    conv_hbm,
     base_codes_ref,
     qual_codes_ref,
     base_ref,
@@ -50,6 +51,7 @@
     pair_out,
     top_out,
     stat_out,
+    conv_out,
     feat_buf,
     features_buf,
     hot_buf,
@@ -68,6 +70,7 @@
         copies.append(pltpu.make_async_copy(feat_hbm.at[span], feat_buf.at[span], sems.at[i]))
         copies[i].start()
     stores = []
+    fetch = pltpu.make_async_copy(conv_hbm, conv_out, out_sems.at[tiles])
     n_qual, n_base = qual_ref.shape[0], base_ref.shape[0]
     place = (iota((LANES, n_qual), 0) == iota((LANES, n_qual), 1)).astype(BF16)
     table = dot(place, qual_ref[...])
@@ -88,6 +91,8 @@
             hot_buf[p * reads : (p + 1) * reads, :] = hot.astype(BF16)
         embed_buf[...] = dot(hot_buf[...], table)
         copies[i].wait()
+        if i == tiles - 1:
+            fetch.start()
         for p in range(TILE):
             near = slice(p * reads, (p + 1) * reads)
             feature = feat_buf[i * TILE + p].astype(F32) + embed_buf[near, :]
@@ -120,8 +125,8 @@
         high, low = split_pair(weights)
         pair_out[near, :] = jnp.where(lane < HEADS, high, low).astype(BF16)
     stat_out[...] = stat_buf[...].astype(BF16)
-    for store in stores:
-        store.wait()
+    for copy in stores + [fetch]:
+        copy.wait()
 
 
 def value_kernel(
@@ -193,19 +198,20 @@
     return [pltpu.with_memory_space_constraint(array, pltpu.HBM) for array in arrays]
 
 
-def encode(depth_index, counts, feats, *rest):
+def encode(depth_index, counts, feats, conv, *rest):
     positions, reads, channels = feats.shape
     rows = positions * reads
     step = TILE * reads
     return pl.pallas_call(
         encode_kernel,
-        in_specs=[SMEM, SMEM, HBM] + [VMEM] * 5,
-        out_specs=[HBM] + [VMEM] * 3,
+        in_specs=[SMEM, SMEM, HBM, HBM] + [VMEM] * 5,
+        out_specs=[HBM] + [VMEM] * 4,
         out_shape=[
             pltpu.HBM((rows, channels), BF16),
             jax.ShapeDtypeStruct((rows, LANES), BF16),
             jax.ShapeDtypeStruct((positions, LANES), F32),
             jax.ShapeDtypeStruct((positions, LANES), BF16),
+            jax.ShapeDtypeStruct(conv.shape, BF16),
         ],
         scratch_shapes=[
             pltpu.VMEM(feats.shape, BF16),
@@ -215,13 +221,13 @@
             pltpu.VMEM((rows, LANES), F32),
             pltpu.VMEM((positions, LANES), F32),
             pltpu.SemaphoreType.DMA((positions // TILE,)),
-            pltpu.SemaphoreType.DMA((positions // TILE,)),
+            pltpu.SemaphoreType.DMA((positions // TILE + 1,)),
         ],
         compiler_params=pltpu.CompilerParams(vmem_limit_bytes=20 * 2**20),
         cost_estimate=pl.CostEstimate(
             flops=2 * rows * channels * 256, bytes_accessed=4 * 2**20, transcendentals=rows * LANES
         ),
-    )(depth_index, *in_hbm(counts, feats, *rest))
+    )(depth_index, *in_hbm(counts, feats, conv, *rest))
 
 
 def make_values(features, pair, value_weight, positions):
@@ -639,10 +645,11 @@
     before = lax.ppermute(grad_local, SEQ, forward)
     after = lax.ppermute(grad_local, SEQ, [(b, a) for a, b in forward])
 
-    features, pair, top, stat = encode(
+    features, pair, top, stat, conv_taps = encode(
         depth_index.reshape(1),
         depth_counts[0],
         read_feats[0],
+        conv_weight.transpose(1, 0, 2),
         base_codes[0].T,
         qual_codes[0].T,
         base_table,
@@ -656,7 +663,7 @@
         before,
         grad_local,
         after,
-        conv_weight.transpose(1, 0, 2),
+        conv_taps,
         stat,
     )
     payload = lax.all_to_all(payload, "depth", split_axis=0, concat_axis=0, tiled=True)

time: 109 us -> 110 us (level)
  transfers between devices with their start and end apart: 7 -> 7, of which waited for: 4 -> 4; matrix products, arithmetic and copies ran while one was open for 0% -> 0% of each run, Pallas kernels for 23% -> 24%
where the time goes in v6:
time: 110 us; the launch traced here: 109 us
  blocking collectives  35.3 us (32%)
  Pallas kernels  30.4 us (28%)
  starting transfers between devices  26.6 us (24%)
  waiting for transfers between devices  16.1 us (15%)
    all_to_all x1, blocking collectives, body(): lax.all_to_all(line_send, 'z', split_axis=0, concat_axis=0, tiled=True)  35.3 us
    all_to_all x1, waiting for transfers between devices, body(): lax.all_to_all(plane_send, ('depth', 'xlo', 'xhi'), split_axis=0, concat_...  11.8 us
    pallas_call x1, Pallas kernels, gradients(): pl.pallas_call(gradient_kernel, in_specs=[SMEM] + [VMEM] * 2 + [HBM] * 4,...  9.5 us
    all_to_all x1, starting transfers between devices, body(): lax.all_to_all(send, ('depth', 'xlo', 'xhi', 'core'), split_axis=0, conca...  7.97 us
    pallas_call x1, Pallas kernels, make_values(): pl.pallas_call(value_kernel, in_specs=[VMEM, VMEM, HBM], out_specs=[HBM]...  7.7 us
    pallas_call x1, Pallas kernels, encode(): pl.pallas_call(encode_kernel, in_specs=[SMEM, SMEM, HBM, HBM] + [VMEM] *...  5.73 us
    pallas_call x6, Pallas kernels, small_call(): pl.pallas_call(kernel, in_specs=specs or [VMEM] * len(operands), out_spec...  5.07 us
    ppermute x2, starting transfers between devices, exchange(): return lax.ppermute(block, axis, [(0, 1), (1, 0)])  4.75 us
  transfers between devices with their start and end apart: 7, of which 4 were waited for; matrix products, arithmetic and copies ran while one was open for 0% of the time, Pallas kernels for 24%

profile of v6, /device:TPU:32, one launch (start us, length us, event | category | flops | bytes accessed | tf_op | source)
XLA Modules:
  0.0 109.3 jit_solution(5582364363063887705)
XLA Ops:
  0.6 0.0 copy-start
  0.6 3.1 %collective-permute-start.1 = (bf16[64,512]{1,0:T(8,128)(2,1)}, bf16[64,512]{1,0:T(8,128)(2,1)S(1)}, u32[]{:S(2)}, u32[]{:S(2)}) collective-permute-start(bf16[64,512]{1,0:T(8,128)(2,1)} %bitcast.16), channel_id=1, source_target_pairs={{4,0},{8,4},{12,8},{16,12},{20,16},{24,20},{28,24},{32,28},{36,32}... | collective-permute-start | bytes 196616 | tf_op jit(solution)/shard_map/ppermute | solution.py:646
  3.7 2.9 %collective-permute-start = (bf16[64,512]{1,0:T(8,128)(2,1)}, bf16[64,512]{1,0:T(8,128)(2,1)S(1)}, u32[]{:S(2)}, u32[]{:S(2)}) collective-permute-start(bf16[64,512]{1,0:T(8,128)(2,1)} %bitcast.17), channel_id=1, source_target_pairs={{0,4},{4,8},{8,12},{12,16},{16,20},{20,24},{24,28},{28,32},{32,36}... | collective-permute-start | bytes 196616 | tf_op jit(solution)/shard_map/ppermute | solution.py:645
  6.6 0.0 copy-start.1
  6.6 5.7 %shard_map.121 = (bf16[2048,512]{1,0:T(8,128)(2,1)}, bf16[2048,128]{1,0:T(8,128)(2,1)S(1)}, f32[64,128]{1,0:T(8,128)S(1)}, bf16[64,128]{1,0:T(8,128)(2,1)S(1)}, bf16[5,256,512]{2,1,0:T(8,128)(2,1)S(1)}) custom-call(s32[1]{0:T(128)} %bitcast.2.depth_ref, s32[64]{0:T(128)} %bitcast.24, bf16[64,32,512]{2,1,0:T(8,128)(2,1)} %bitcast.19, ...), custom_call_target="tpu_custom_call" | custom-call | flops 536870912 | bytes 4194304 | tf_op jit(solution)/shard_map/pallas_call | solution.py:205
  12.4 0.0 collective-permute-done.1.after_ref
  12.4 1.6 %collective-permute-done.before_ref = bf16[64,512]{1,0:T(8,128)(2,1)S(1)} collective-permute-done((bf16[64,512]{1,0:T(8,128)(2,1)}, bf16[64,512]{1,0:T(8,128)(2,1)S(1)}, u32[]{:S(2)}, u32[]{:S(2)}) %collective-permute-start) | collective-permute-done | bytes 65568 | tf_op jit(solution)/shard_map/ppermute | solution.py:645
  14.0 0.0 copy-done
  14.0 1.2 %shard_map.122 = (bf16[4,64,384]{2,1,0:T(8,128)(2,1)}, bf16[4,80,128]{2,1,0:T(8,128)(2,1)S(1)}) custom-call(bf16[64,512]{1,0:T(8,128)(2,1)S(1)} %collective-permute-done.before_ref, bf16[64,512]{1,0:T(8,128)(2,1)S(1)} %bitcast.18, bf16[64,512]{1,0:T(8,128)(2,1)S(1)} %collective-permute-done.1.after_ref, ...), custom_call_target="tpu_custom_call" | custom-call | flops 1000000 | bytes 100000 | tf_op jit(solution)/shard_map/pallas_call | solution.py:608
  15.2 3.4 %all-to-all-start = ((bf16[4,64,384]{2,1,0:T(8,128)(2,1)}), bf16[4,64,384]{2,1,0:T(8,128)(2,1)S(1)}, u32[]{:S(2)}, u32[]{:S(2)}) async-start(bf16[4,64,384]{2,1,0:T(8,128)(2,1)} %get-tuple-element.24), calls=%async_computation | async-start | bytes 393216 | tf_op jit(solution)/shard_map/all_to_all | solution.py:669
  18.6 0.0 copy-done.1
  18.6 7.7 %shard_map.123 = (bf16[2048,128]{1,0:T(8,128)(2,1)}, bf16[4,2048,256]{2,1,0:T(8,128)(2,1)}, bf16[4,2048,256]{2,1,0:T(8,128)(2,1)}, f32[64,1024]{1,0:T(8,128)S(1)}) custom-call(bf16[2048,128]{1,0:T(8,128)(2,1)S(1)} %get-tuple-element.26.pair_ref, bf16[1024,512]{1,0:T(8,128)(2,1)S(1)} %copy-done.1, bf16[2048,512]{1,0:T(8,128)(2,1)} %get-tuple-element.27.features_hbm), custom_call_target="tpu_custom_call" | custom-call | flops 3221225472 | bytes 16777216 | tf_op jit(solution)/shard_map/pallas_call | solution.py:235
  26.3 0.0 all-to-all-done.payload_ref
  26.3 1.7 %shard_map.124 = (bf16[32,96,128]{2,1,0:T(8,128)(2,1)}, f32[64,128]{1,0:T(8,128)S(1)}) custom-call(s32[1]{0:T(128)} %bitcast.2.depth_ref, bf16[4,64,384]{2,1,0:T(8,128)(2,1)S(1)} %all-to-all-done.payload_ref, f32[64,128]{1,0:T(8,128)S(1)} %get-tuple-element.25.top_ref, f32[64,1024]{1,0:T(8,128)S(1)} %get-tuple-element.28.pool_ref, ...), custom_call_target="tpu_custom_call" | custom-call | flops 1000000 | bytes 100000 | tf_op jit(solution)/shard_map/pallas_call | solution.py:608
  28.0 8.0 %all-to-all-start.1 = ((bf16[32,96,128]{2,1,0:T(8,128)(2,1)}), bf16[32,96,128]{2,1,0:T(8,128)(2,1)S(1)}, u32[]{:S(2)}, u32[]{:S(2)}) async-start(bf16[32,96,128]{2,1,0:T(8,128)(2,1)} %get-tuple-element.36), calls=%async_computation.1 | async-start | bytes 1572864 | tf_op jit(solution)/shard_map/all_to_all | solution.py:686
  36.0 9.5 %shard_map.125 = (bf16[16,128,128]{2,1,0:T(8,128)(2,1)S(1)}, bf16[16,128,128]{2,1,0:T(8,128)(2,1)S(1)}, f32[2048,128]{1,0:T(8,128)}) custom-call(s32[1]{0:T(128)} %bitcast.core_ref, bf16[4,64,384]{2,1,0:T(8,128)(2,1)S(1)} %all-to-all-done.payload_ref, f32[64,128]{1,0:T(8,128)S(1)} %get-tuple-element.30.scale_ref, ...), custom_call_target="tpu_custom_call" | custom-call | flops 3221225472 | bytes 16777216 | tf_op jit(solution)/shard_map/pallas_call | solution.py:460
  45.5 2.0 %collective-permute-start.2 = (bf16[16,128,128]{2,1,0:T(8,128)(2,1)S(1)}, bf16[16,128,128]{2,1,0:T(8,128)(2,1)S(1)}, u32[]{:S(2)}, u32[]{:S(2)}) collective-permute-start(bf16[16,128,128]{2,1,0:T(8,128)(2,1)S(1)} %get-tuple-element.35), channel_id=1, source_target_pairs={{0,1},{1,0},{2,3},{3,2},{4,5},{5,4},{6,7},{7,6},{8,9},{9,8},{10,11... | collective-permute-start | bytes 1572872 | tf_op jit(solution)/shard_map/ppermute | solution.py:620
  47.5 2.0 %all-to-all-done.1.recv_ref = bf16[32,96,128]{2,1,0:T(8,128)(2,1)S(1)} async-done(((bf16[32,96,128]{2,1,0:T(8,128)(2,1)}), bf16[32,96,128]{2,1,0:T(8,128)(2,1)S(1)}, u32[]{:S(2)}, u32[]{:S(2)}) %all-to-all-start.1) | async-done | bytes 786464 | tf_op jit(solution)/shard_map/all_to_all | solution.py:686
  49.5 2.4 %shard_map.126.score_ref = bf16[32,128]{1,0:T(8,128)(2,1)S(1)} custom-call(s32[1]{0:T(128)} %bitcast.11.place_ref, bf16[32,96,128]{2,1,0:T(8,128)(2,1)S(1)} %all-to-all-done.1.recv_ref, f32[2048,128]{1,0:T(8,128)} %get-tuple-element.37.probs_hbm, bf16[2048,512]{1,0:T(8,128)(2,1)} %get-tuple-element.27.features_hbm), custom_call_target="tpu_custom_call" | custom-call | flops 100000000 | bytes 1000000 | tf_op jit(solution)/shard_map/pallas_call | solution.py:534
  51.9 2.7 %collective-permute-start.3 = (bf16[32,128]{1,0:T(8,128)(2,1)S(1)}, bf16[32,128]{1,0:T(8,128)(2,1)S(1)}, u32[]{:S(2)}, u32[]{:S(2)}) collective-permute-start(bf16[32,128]{1,0:T(8,128)(2,1)S(1)} %shard_map.126.score_ref), channel_id=1, source_target_pairs={{0,1},{1,0},{2,3},{3,2},{4,5},{5,4},{6,7},{7,6},{8,9},{9,8},{10,11... | collective-permute-start | bytes 24584 | tf_op jit(solution)/shard_map/ppermute | solution.py:620
  54.7 0.0 collective-permute-done.2.theirs_ref
  54.7 0.8 collective-permute-done.3.other_ref
  55.5 1.0 shard_map.127
  56.4 4.5 %all-to-all-start.2 = ((bf16[16,160,128]{2,1,0:T(8,128)(2,1)}), bf16[16,160,128]{2,1,0:T(8,128)(2,1)S(1)}, u32[]{:S(2)}, u32[]{:S(2)}) async-start(bf16[16,160,128]{2,1,0:T(8,128)(2,1)} %shard_map.127), calls=%async_computation.2 | async-start | bytes 1310720 | tf_op jit(solution)/shard_map/all_to_all | solution.py:700
  60.9 0.4 shard_map.128.conv_ref
  61.4 11.8 %all-to-all-done.2.recv_ref = bf16[16,160,128]{2,1,0:T(8,128)(2,1)S(1)} async-done(((bf16[16,160,128]{2,1,0:T(8,128)(2,1)}), bf16[16,160,128]{2,1,0:T(8,128)(2,1)S(1)}, u32[]{:S(2)}, u32[]{:S(2)}) %all-to-all-start.2) | async-done | bytes 655392 | tf_op jit(solution)/shard_map/all_to_all | solution.py:700
  73.1 0.1 shard_map.129
  73.3 35.3 %all_to_all.20.recv_ref = bf16[16,80,128]{2,1,0:T(8,128)(2,1)S(1)} all-to-all(bf16[16,80,128]{2,1,0:T(8,128)(2,1)S(1)} %shard_map.129), channel_id=1, replica_groups=mesh['depth'=4,'z'=16,'xlo'=2,'xhi'=2,'core'=2] {'z'}, dimensions={0} | all-to-all | bytes 655360 | tf_op jit(solution)/shard_map/all_to_all | solution.py:712
  108.6 0.7 shard_map.130
Async XLA Ops:
  0.6 13.4 %copy-start = (bf16[1,64,512]{2,1,0:T(8,128)(2,1)S(1)}, bf16[1,64,512]{2,1,0:T(8,128)(2,1)}, u32[]{:S(2)}) copy-start(bf16[1,64,512]{2,1,0:T(8,128)(2,1)} %param.19) | copy-start | bytes 196612
  0.6 11.7 %collective-permute-start.1 = (bf16[64,512]{1,0:T(8,128)(2,1)}, bf16[64,512]{1,0:T(8,128)(2,1)S(1)}, u32[]{:S(2)}, u32[]{:S(2)}) collective-permute-start(bf16[64,512]{1,0:T(8,128)(2,1)} %bitcast.16), channel_id=1, source_target_pairs={{4,0},{8,4},{12,8},{16,12},{20,16},{24,20},{28,24},{32,28},{36,32}... | collective-permute-start | bytes 196616 | tf_op jit(solution)/shard_map/ppermute | solution.py:646
  3.7 10.3 %collective-permute-start = (bf16[64,512]{1,0:T(8,128)(2,1)}, bf16[64,512]{1,0:T(8,128)(2,1)S(1)}, u32[]{:S(2)}, u32[]{:S(2)}) collective-permute-start(bf16[64,512]{1,0:T(8,128)(2,1)} %bitcast.17), channel_id=1, source_target_pairs={{0,4},{4,8},{8,12},{12,16},{16,20},{20,24},{24,28},{28,32},{32,36}... | collective-permute-start | bytes 196616 | tf_op jit(solution)/shard_map/ppermute | solution.py:645
  6.6 11.9 %copy-start.1 = (bf16[1024,512]{1,0:T(8,128)(2,1)S(1)}, bf16[1024,512]{1,0:T(8,128)(2,1)}, u32[]{:S(2)}) copy-start(bf16[1024,512]{1,0:T(8,128)(2,1)} %value_ref.1) | copy-start | bytes 3145732
  15.2 11.1 %all-to-all-start = ((bf16[4,64,384]{2,1,0:T(8,128)(2,1)}), bf16[4,64,384]{2,1,0:T(8,128)(2,1)S(1)}, u32[]{:S(2)}, u32[]{:S(2)}) async-start(bf16[4,64,384]{2,1,0:T(8,128)(2,1)} %get-tuple-element.24), calls=%async_computation | async-start | bytes 393216 | tf_op jit(solution)/shard_map/all_to_all | solution.py:669
  28.0 21.5 %all-to-all-start.1 = ((bf16[32,96,128]{2,1,0:T(8,128)(2,1)}), bf16[32,96,128]{2,1,0:T(8,128)(2,1)S(1)}, u32[]{:S(2)}, u32[]{:S(2)}) async-start(bf16[32,96,128]{2,1,0:T(8,128)(2,1)} %get-tuple-element.36), calls=%async_computation.1 | async-start | bytes 1572864 | tf_op jit(solution)/shard_map/all_to_all | solution.py:686
  45.5 9.2 %collective-permute-start.2 = (bf16[16,128,128]{2,1,0:T(8,128)(2,1)S(1)}, bf16[16,128,128]{2,1,0:T(8,128)(2,1)S(1)}, u32[]{:S(2)}, u32[]{:S(2)}) collective-permute-start(bf16[16,128,128]{2,1,0:T(8,128)(2,1)S(1)} %get-tuple-element.35), channel_id=1, source_target_pairs={{0,1},{1,0},{2,3},{3,2},{4,5},{5,4},{6,7},{7,6},{8,9},{9,8},{10,11... | collective-permute-start | bytes 1572872 | tf_op jit(solution)/shard_map/ppermute | solution.py:620
  51.9 3.6 %collective-permute-start.3 = (bf16[32,128]{1,0:T(8,128)(2,1)S(1)}, bf16[32,128]{1,0:T(8,128)(2,1)S(1)}, u32[]{:S(2)}, u32[]{:S(2)}) collective-permute-start(bf16[32,128]{1,0:T(8,128)(2,1)S(1)} %shard_map.126.score_ref), channel_id=1, source_target_pairs={{0,1},{1,0},{2,3},{3,2},{4,5},{5,4},{6,7},{7,6},{8,9},{9,8},{10,11... | collective-permute-start | bytes 24584 | tf_op jit(solution)/shard_map/ppermute | solution.py:620
  56.4 16.7 %all-to-all-start.2 = ((bf16[16,160,128]{2,1,0:T(8,128)(2,1)}), bf16[16,160,128]{2,1,0:T(8,128)(2,1)S(1)}, u32[]{:S(2)}, u32[]{:S(2)}) async-start(bf16[16,160,128]{2,1,0:T(8,128)(2,1)} %shard_map.127), calls=%async_computation.2 | async-start | bytes 1310720 | tf_op jit(solution)/shard_map/all_to_all | solution.py:700
